TPU v7x, 32 devices: a whole 2x2x4 slice. The times are simulated.
32 devices in a mesh: files: 2 (over y), ctx: 4 (over z), chan: 4 (over x, core).
Axes of the slice: x: 2, y: 2, z: 4, core: 2. Of those that a mesh axis runs over, the one named last changes fastest.
Arguments:
- activations: bfloat16 [4096, 4096], P(('files', 'ctx'), 'chan'), parts along dimension 0, may hold values from -6 to 6
- proj_weight: bfloat16 [3, 256, 4096], P(None, 'chan'), may hold values from -0.09375 to 0.09375
- long_filter: float32 [256, 2048], P('chan', 'ctx'), may hold values from -6 to 6
- skip_gain: float32 [256], P('chan'), may hold values from -1 to 1
- out_grad: bfloat16 [256, 4096], P('chan', ('files', 'ctx')), parts along dimension 1, may hold values from -6 to 6
Outputs:
- grad_input: bfloat16 [4096, 4096], P(('files', 'ctx'), 'chan'), parts along dimension 0
- grad_weight: float32 [6, 256, 4096], P('files', 'chan'), parts along dimension 0
- grad_filter: float32 [256, 4096], P('chan', ('files', 'ctx')), parts along dimension 1
There are 2 independent parts, one for each index of `files`. A program takes and returns all parts, laid end to end along the dimension named above; an argument that names none is the same for every part. Nothing has to cross between parts.
All inputs are finite; a program needn't handle non-finite values.
Results may differ from a plain program's by a relative error of at most 0.0095.
Values may be sent and summed in bfloat16 or wider, within the bound.
No kernel may reach another device: no remote copies, remote signals or barrier semaphores. Data moves between devices by JAX's collectives and lax.ppermute only.
A program may use at most 64 MiB of HBM per device.

v0:
```python
import functools
import math

import jax
import jax.numpy as jnp
import numpy as np
from jax import lax
from jax.experimental import pallas as pl
from jax.experimental.pallas import tpu as pltpu
from jax.sharding import PartitionSpec as P

LANES = 128
BF16 = jnp.bfloat16
F32 = jnp.float32


def split_table(table):
    high = np.asarray(table, np.float32).astype(BF16)
    low = (np.asarray(table, np.float64) - high.astype(np.float64)).astype(BF16)
    return np.stack([high, low])


def fourier_tables(tokens, group):
    period = 2 * tokens
    rows = period // LANES
    used = rows // 2
    freqs = rows // 2 + 1
    part = -(-freqs * group // 8) * 8
    k1 = np.arange(freqs)
    n1 = np.arange(used)
    angle = 2.0 * math.pi * (np.outer(k1, n1) % rows) / rows
    eye = np.eye(group)
    forward = np.zeros((2 * part, used * group))
    forward[: freqs * group] = np.kron(np.cos(angle), eye)
    forward[part : part + freqs * group] = np.kron(-np.sin(angle), eye)
    weight = np.where((k1 == 0) | (k1 == rows // 2), 1.0, 2.0)[None, :] / period
    inverse = np.zeros((used * group, 2 * part))
    inverse[:, : freqs * group] = np.kron(np.cos(angle.T) * weight, eye)
    inverse[:, part : part + freqs * group] = np.kron(-np.sin(angle.T) * weight, eye)
    n2 = np.arange(LANES)
    turn = 2.0 * math.pi * np.outer(k1, n2) / period
    twiddle = np.zeros((2, part, LANES), np.float32)
    twiddle[0, : freqs * group] = np.repeat(np.cos(turn), group, axis=0)
    twiddle[1, : freqs * group] = np.repeat(np.sin(turn), group, axis=0)
    inner = 2.0 * math.pi * (np.outer(n2, n2) % LANES) / LANES
    cos, sin = np.cos(inner), np.sin(inner)
    second = np.block([[cos, -sin], [sin, cos]])
    second_back = np.block([[cos, sin], [-sin, cos]])
    return (
        split_table(forward),
        split_table(second),
        split_table(second_back),
        split_table(inverse),
        twiddle,
    )


def halves(values):
    high = values.astype(BF16)
    return high, (values - high.astype(F32)).astype(BF16)


def mm(left, right):
    return jnp.dot(left, right, preferred_element_type=F32)


def table_left(table, values):
    high, low = halves(values)
    return mm(table[0], high) + (mm(table[0], low) + mm(table[1], high))


def table_right(values, table):
    high, low = halves(values)
    return mm(high, table[0]) + (mm(low, table[0]) + mm(high, table[1]))


def conv_kernel(blocks, chans, group, factor, *refs):
    signal_refs = refs[:blocks]
    upstream_refs = refs[blocks : 2 * blocks]
    filter_refs = refs[2 * blocks : 3 * blocks]
    gain_ref, fwd_ref, second_ref, back_ref, inv_ref, twiddle_ref = refs[3 * blocks : 3 * blocks + 6]
    refs = refs[3 * blocks + 6 :]
    grad_refs = refs[:blocks]
    grad_filter_refs = refs[blocks : 2 * blocks]
    series, results = refs[2 * blocks :]
    place = lax.axis_index("ctx")
    length = series.shape[-1]
    cuts = length // LANES
    for m in range(blocks):
        where = place ^ m
        values = signal_refs[m][...].astype(F32)
        upstream = upstream_refs[m][...].astype(F32)
        series[0, where] = filter_refs[m][...] * factor
        series[1, where] = values[:chans] * values[2 * chans :]
        series[2, where] = upstream * values[chans : 2 * chans]
    part = twiddle_ref.shape[1]
    cos, sin = twiddle_ref[0], twiddle_ref[1]
    for start in range(0, chans, group):
        picked = []
        for q in range(3):
            tiles = []
            for z in range(blocks):
                loaded = series[q, z]
                loaded = loaded[start : start + group]
                for n in range(cuts):
                    tiles.append(loaded[:, n * LANES : (n + 1) * LANES])
            picked.append(jnp.concatenate(tiles, axis=0))
        first = table_left(fwd_ref, jnp.concatenate(picked, axis=1))
        turned = []
        for q in range(3):
            re = first[:part, q * LANES : (q + 1) * LANES]
            im = first[part:, q * LANES : (q + 1) * LANES]
            turned.append(jnp.concatenate([re * cos + im * sin, im * cos - re * sin], axis=1))
        spectra = table_right(jnp.concatenate(turned, axis=0), second_ref)
        parts = [
            (spectra[q * part : (q + 1) * part, :LANES], spectra[q * part : (q + 1) * part, LANES:])
            for q in range(3)
        ]
        (fr, fi), (gr, gi), (ur, ui) = parts
        products = jnp.concatenate(
            [
                jnp.concatenate([fr * gr - fi * gi, fr * gi + fi * gr], axis=1),
                jnp.concatenate([fr * ur + fi * ui, fr * ui - fi * ur], axis=1),
                jnp.concatenate([gr * ur + gi * ui, gr * ui - gi * ur], axis=1),
            ],
            axis=0,
        )
        back = table_right(products, back_ref)
        turned = []
        for q in range(3):
            re = back[q * part : (q + 1) * part, :LANES]
            im = back[q * part : (q + 1) * part, LANES:]
            turned.append(jnp.concatenate([re * cos - im * sin, im * cos + re * sin], axis=0))
        final = table_left(inv_ref, jnp.concatenate(turned, axis=1))
        for q in range(3):
            for z in range(blocks):
                tiles = [
                    final[(z * cuts + n) * group : (z * cuts + n + 1) * group, q * LANES : (q + 1) * LANES]
                    for n in range(cuts)
                ]
                results[q, z, start : start + group, :] = jnp.concatenate(tiles, axis=1)
    gain = gain_ref[...]
    for m in range(blocks):
        where = place ^ m
        values = signal_refs[m][...].astype(F32)
        upstream = upstream_refs[m][...].astype(F32)
        conv_out = results[0, where] + gain * series[1, where]
        grad_gated = results[1, where] + gain * series[2, where]
        grad_refs[m][...] = jnp.concatenate(
            [grad_gated * values[2 * chans :], upstream * conv_out, grad_gated * values[:chans]], axis=0
        ).astype(BF16)
        grad_filter_refs[m][...] = factor * results[2, where]


def convolve(signals, upstream, filters, gain):
    blocks = len(signals)
    chans, length = upstream[0].shape
    tokens = blocks * length
    group = max(1, min(chans, 8, LANES * LANES // tokens))
    tables = fourier_tables(tokens, group)
    vmem = pl.BlockSpec(memory_space=pltpu.VMEM)
    count = 3 * blocks + 6
    part = tables[4].shape[1]
    flops = 2 * 3 * (chans // group) * 3 * (4 * part * group * (tokens // LANES) * LANES + 2 * part * 256 * 256)
    outs = pl.pallas_call(
        functools.partial(conv_kernel, blocks, chans, group, tokens ** (-0.5)),
        out_shape=[jax.ShapeDtypeStruct((3 * chans, length), BF16)] * blocks
        + [jax.ShapeDtypeStruct((chans, length), F32)] * blocks,
        in_specs=[vmem] * count,
        out_specs=[vmem] * (2 * blocks),
        scratch_shapes=[pltpu.VMEM((3, blocks, chans, length), F32)] * 2,
        compiler_params=pltpu.CompilerParams(vmem_limit_bytes=40 * 2**20),
        cost_estimate=pl.CostEstimate(flops=flops, bytes_accessed=4 * 2**20, transcendentals=0),
        name="conv",
    )(*signals, *upstream, *filters, gain, *[jnp.asarray(t) for t in tables])
    return outs[:blocks], outs[blocks:]


def swap(values, axis, mask):
    if mask == 0:
        return values
    size = lax.axis_size(axis)
    return lax.ppermute(values, axis, [(i, i ^ mask) for i in range(size)])


def after(values, *others):
    return lax.optimization_barrier((values, *others))[0]


def sum_over_ctx(local, place):
    if lax.axis_size("ctx") != 4:
        return [lax.psum(x.astype(BF16), "ctx").astype(F32) for x in local]
    middle = (place == 1) | (place == 2)
    totals = []
    for x in local:
        from_end = lax.ppermute(x.astype(BF16), "ctx", [(0, 1), (3, 2)])
        pair = x + from_end.astype(F32)
        from_pair = lax.ppermute(pair.astype(BF16), "ctx", [(1, 2), (2, 1)])
        total = pair + from_pair.astype(F32)
        given = lax.ppermute(total.astype(BF16), "ctx", [(1, 0), (2, 3)])
        totals.append(jnp.where(middle, total, given.astype(F32)))
    return totals


def per_device(activations, proj_weight, long_filter, skip_gain, out_grad):
    blocks = lax.axis_size("ctx")
    slabs = lax.axis_size("chan")
    place = lax.axis_index("ctx")
    mine = lax.axis_index("chan")
    length, width = activations.shape
    kinds, own, depth = proj_weight.shape
    share = own // blocks
    factor = (length * blocks) ** (-0.5)
    rows = kinds * own

    upstream = [swap(lax.dynamic_slice_in_dim(out_grad, (place ^ m) * share, share, 0), "ctx", m) for m in range(blocks)]
    filters = [swap(lax.dynamic_slice_in_dim(long_filter, (place ^ m) * share, share, 0), "ctx", m) for m in range(blocks)]
    gain = lax.dynamic_slice_in_dim(skip_gain, place * share, share, 0)[:, None]

    if slabs == 4:
        far = swap(activations, "chan", 2)
        features = [activations, swap(activations, "chan", 1), far, swap(far, "chan", 1)]
    else:
        features = [swap(activations, "chan", m) for m in range(slabs)]

    def columns(array, m):
        return lax.dynamic_slice_in_dim(array, (mine ^ m) * width, width, array.ndim - 1)

    weight_rows = proj_weight.reshape(rows, depth)
    projected = 0.0
    for m in range(slabs):
        projected = projected + lax.dot_general(
            columns(weight_rows, m), features[m], (((1,), (1,)), ((), ())), preferred_element_type=F32
        )
    projected = projected.astype(BF16).reshape(kinds, own, length)

    held = after(proj_weight, features[slabs // 2])
    weight_cols = [swap(columns(held, m), "chan", m).reshape(rows, width) for m in range(slabs)]

    signals = [
        swap(
            lax.dynamic_slice_in_dim(projected, (place ^ m) * share, share, 1).reshape(kinds * share, length),
            "ctx",
            m,
        )
        for m in range(blocks)
    ]
    grads, grad_filters = convolve(signals, upstream, filters, gain)

    def collect(pieces, dtype, kinds):
        found = jnp.zeros((kinds, own, length), dtype)
        for m in range(blocks):
            piece = swap(pieces[m], "ctx", m).reshape(kinds, share, length)
            found = lax.dynamic_update_slice_in_dim(found, piece, (place ^ m) * share, 1)
        return found.reshape(kinds * own, length)

    grad_proj = collect(grads, BF16, kinds)
    grad_filter = collect(grad_filters, F32, 1)

    local = [mm(grad_proj, features[m]) for m in range(slabs)]
    totals = sum_over_ctx(local, place)
    grad_weight = jnp.zeros((rows, depth), F32)
    for m in range(slabs):
        grad_weight = lax.dynamic_update_slice_in_dim(grad_weight, totals[m] * factor, (mine ^ m) * width, 1)

    if slabs == 4:
        far = swap(grad_proj, "chan", 2)
        gathered = [grad_proj, swap(grad_proj, "chan", 1), far, swap(far, "chan", 1)]
    else:
        gathered = [swap(grad_proj, "chan", m) for m in range(slabs)]
    grad_rows = 0.0
    for m in range(slabs):
        grad_rows = grad_rows + lax.dot_general(
            gathered[m], weight_cols[m], (((0,), (0,)), ((), ())), preferred_element_type=F32
        )
    return (
        grad_rows.astype(BF16),
        grad_weight.reshape(kinds, own, depth),
        grad_filter,
    )


def solution(mesh):
    placed = (
        P(("files", "ctx"), "chan"),
        P(None, "chan", None),
        P("chan", "ctx"),
        P("chan"),
        P("chan", ("files", "ctx")),
    )
    return jax.shard_map(
        per_device,
        mesh=mesh,
        in_specs=placed,
        out_specs=(
            P(("files", "ctx"), "chan"),
            P("files", "chan", None),
            P("chan", ("files", "ctx")),
        ),
        check_vma=False,
    )
```

profile of v0, /device:TPU:0, one launch (start us, length us, event | category | flops | bytes accessed | tf_op | source)
XLA Modules:
  0.0 168.2 jit_solution(7931618049782570296)
XLA Ops:
  0.7 3.0 %collective-permute-start.1 = (bf16[512,1024]{1,0:T(8,128)(2,1)}, bf16[512,1024]{1,0:T(8,128)(2,1)S(1)}, u32[]{:S(2)}, u32[]{:S(2)}) collective-permute-start(bf16[512,1024]{1,0:T(8,128)(2,1)} %param.10), channel_id=1, source_target_pairs={{0,2},{1,3},{2,0},{3,1},{4,6},{5,7},{6,4},{7,5},{8,10},{9,11},{10,... | collective-permute-start | bytes 3145736 | tf_op jit(solution)/shard_map/ppermute | solution.py:183
  3.7 23.4 %collective-permute-done.1 = bf16[512,1024]{1,0:T(8,128)(2,1)S(1)} collective-permute-done((bf16[512,1024]{1,0:T(8,128)(2,1)}, bf16[512,1024]{1,0:T(8,128)(2,1)S(1)}, u32[]{:S(2)}, u32[]{:S(2)}) %collective-permute-start.1) | collective-permute-done | bytes 1048608 | tf_op jit(solution)/shard_map/ppermute | solution.py:183
  27.8 1.8 %collective-permute-start.6 = (bf16[16,512]{1,0:T(8,128)(2,1)S(1)}, bf16[16,512]{1,0:T(8,128)(2,1)S(1)}, u32[]{:S(2)}, u32[]{:S(2)}) collective-permute-start(bf16[16,512]{1,0:T(8,128)(2,1)S(1)} %get-tuple-element.33), channel_id=1, source_target_pairs={{0,4},{4,0},{8,12},{12,8},{1,5},{5,1},{9,13},{13,9},{2,6},{6,2},{1... | collective-permute-start | bytes 49160 | tf_op jit(solution)/shard_map/ppermute | solution.py:183
  29.6 2.6 %collective-permute-start.7 = (bf16[16,512]{1,0:T(8,128)(2,1)S(1)}, bf16[16,512]{1,0:T(8,128)(2,1)S(1)}, u32[]{:S(2)}, u32[]{:S(2)}) collective-permute-start(bf16[16,512]{1,0:T(8,128)(2,1)S(1)} %get-tuple-element.35), channel_id=1, source_target_pairs={{0,8},{4,12},{8,0},{12,4},{1,9},{5,13},{9,1},{13,5},{2,10},{6,14},... | collective-permute-start | bytes 49160 | tf_op jit(solution)/shard_map/ppermute | solution.py:183
  33.2 1.9 %fusion.13 = f32[192,512]{1,0:T(8,128)S(1)} fusion(bf16[512,1024]{1,0:T(8,128)(2,1)} %param.10, bf16[192,4096]{1,0:T(8,128)(2,1)} %bitcast.52, s32[]{:T(128)S(6)} %select_n.36), kind=kOutput, calls=%fused_computation.29 | convolution fusion | flops 201326592 | bytes 1835012 | tf_op jit(solution)/shard_map/dot_general | solution.py:232
  36.1 1.7 %convolution_add_fusion.2 = f32[192,512]{1,0:T(8,128)S(1)} fusion(f32[192,512]{1,0:T(8,128)S(1)} %fusion.13, bf16[512,1024]{1,0:T(8,128)(2,1)} %collective-permute-done, bf16[192,4096]{1,0:T(8,128)(2,1)S(1)} %bitcast.53, s32[]{:T(128)S(6)} %select_n.70), kind=kOutput, calls=%fused_computation.6 | convolution fusion | flops 201424896 | bytes 2228228 | tf_op jit(solution)/shard_map/dot_general | solution.py:232
  38.4 3.6 %collective-permute-start.10 = (f32[16,512]{1,0:T(8,128)S(1)}, f32[16,512]{1,0:T(8,128)S(1)}, u32[]{:S(2)}, u32[]{:S(2)}) collective-permute-start(f32[16,512]{1,0:T(8,128)S(1)} %get-tuple-element.31), channel_id=1, source_target_pairs={{0,8},{4,12},{8,0},{12,4},{1,9},{5,13},{9,1},{13,5},{2,10},{6,14},... | collective-permute-start | bytes 98312 | tf_op jit(solution)/shard_map/ppermute | solution.py:183
  41.9 1.7 %fusion.3 = bf16[192,512]{1,0:T(8,128)(2,1)S(1)} fusion(f32[192,512]{1,0:T(8,128)S(1)} %convolution_add_fusion.1, bf16[512,1024]{1,0:T(8,128)(2,1)} %collective-permute-done.2, bf16[192,4096]{1,0:T(8,128)(2,1)S(1)} %bitcast.55, s32[]{:T(128)S(6)} %select_n.72), kind=kOutput, calls=%fused_computation.7 | convolution fusion | flops 201523200 | bytes 2031620 | tf_op jit(solution)/shard_map/dot_general | solution.py:232
  44.5 3.7 %collective-permute-start.4 = (bf16[48,512]{1,0:T(8,128)(2,1)S(1)}, bf16[48,512]{1,0:T(8,128)(2,1)S(1)}, u32[]{:S(2)}, u32[]{:S(2)}) collective-permute-start(bf16[48,512]{1,0:T(8,128)(2,1)S(1)} %bitcast.62), channel_id=1, source_target_pairs={{0,8},{4,12},{8,0},{12,4},{1,9},{5,13},{9,1},{13,5},{2,10},{6,14},... | collective-permute-start | bytes 147464 | tf_op jit(solution)/shard_map/ppermute | solution.py:183
  48.4 1.7 collective-permute-start.18
  51.2 2.9 %collective-permute-done.5.refs_3_ = bf16[48,512]{1,0:T(8,128)(2,1)S(1)} collective-permute-done((bf16[48,512]{1,0:T(8,128)(2,1)S(1)}, bf16[48,512]{1,0:T(8,128)(2,1)S(1)}, u32[]{:S(2)}, u32[]{:S(2)}) %collective-permute-start.5) | collective-permute-done | bytes 49184 | tf_op jit(solution)/shard_map/ppermute | solution.py:183
  54.1 3.0 %conv.1 = (bf16[48,512]{1,0:T(8,128)(2,1)S(1)}, bf16[48,512]{1,0:T(8,128)(2,1)S(1)}, bf16[48,512]{1,0:T(8,128)(2,1)S(1)}, bf16[48,512]{1,0:T(8,128)(2,1)S(1)}, f...) custom-call(bf16[48,512]{1,0:T(8,128)(2,1)S(1)} %bitcast.44, ...), custom_call_target="tpu_custom_call" | custom-call | flops 962592768 | bytes 4194304 | tf_op jit(solution)/shard_map/conv/pallas_call | solution.py:165
  57.2 2.0 %collective-permute-start.33 = (f32[16,512]{1,0:T(8,128)S(1)}, f32[16,512]{1,0:T(8,128)S(1)}, u32[]{:S(2)}, u32[]{:S(2)}) collective-permute-start(f32[16,512]{1,0:T(8,128)S(1)} %get-tuple-element.18), channel_id=1, source_target_pairs={{0,4},{4,0},{8,12},{12,8},{1,5},{5,1},{9,13},{13,9},{2,6},{6,2},{1... | collective-permute-start | bytes 98312 | tf_op jit(solution)/shard_map/ppermute | solution.py:183
  59.3 2.3 %collective-permute-done.33 = f32[16,512]{1,0:T(8,128)S(1)} collective-permute-done((f32[16,512]{1,0:T(8,128)S(1)}, f32[16,512]{1,0:T(8,128)S(1)}, u32[]{:S(2)}, u32[]{:S(2)}) %collective-permute-start.33) | collective-permute-done | bytes 32800 | tf_op jit(solution)/shard_map/ppermute | solution.py:183
  62.2 4.6 %collective-permute-done.34 = f32[16,512]{1,0:T(8,128)S(1)} collective-permute-done((f32[16,512]{1,0:T(8,128)S(1)}, f32[16,512]{1,0:T(8,128)S(1)}, u32[]{:S(2)}, u32[]{:S(2)}) %collective-permute-start.34) | collective-permute-done | bytes 32800 | tf_op jit(solution)/shard_map/ppermute | solution.py:183
  67.4 5.2 %collective-permute-done.35 = f32[16,512]{1,0:T(8,128)S(1)} collective-permute-done((f32[16,512]{1,0:T(8,128)S(1)}, f32[16,512]{1,0:T(8,128)S(1)}, u32[]{:S(2)}, u32[]{:S(2)}) %collective-permute-start.35) | collective-permute-done | bytes 32800 | tf_op jit(solution)/shard_map/ppermute | solution.py:183
  72.6 1.9 %collective-permute-start.14 = (bf16[48,512]{1,0:T(8,128)(2,1)S(1)}, bf16[48,512]{1,0:T(8,128)(2,1)S(1)}, u32[]{:S(2)}, u32[]{:S(2)}) collective-permute-start(bf16[48,512]{1,0:T(8,128)(2,1)S(1)} %get-tuple-element.15), channel_id=1, source_target_pairs={{0,12},{4,8},{8,4},{12,0},{1,13},{5,9},{9,5},{13,1},{2,14},{6,10},... | collective-permute-start | bytes 147464 | tf_op jit(solution)/shard_map/ppermute | solution.py:183
  74.5 3.0 %collective-permute-done.13 = bf16[48,512]{1,0:T(8,128)(2,1)S(1)} collective-permute-done((bf16[48,512]{1,0:T(8,128)(2,1)S(1)}, bf16[48,512]{1,0:T(8,128)(2,1)S(1)}, u32[]{:S(2)}, u32[]{:S(2)}) %collective-permute-start.13) | collective-permute-done | bytes 49184 | tf_op jit(solution)/shard_map/ppermute | solution.py:183
  78.6 1.5 collective-permute-start.17
  80.6 1.6 fusion.25
  82.6 1.6 fusion.27
  84.7 2.0 %collective-permute-start.21 = (bf16[192,1024]{1,0:T(8,128)(2,1)S(1)}, bf16[192,1024]{1,0:T(8,128)(2,1)S(1)}, u32[]{:S(2)}, u32[]{:S(2)}) collective-permute-start(bf16[192,1024]{1,0:T(8,128)(2,1)S(1)} %get-tuple-element.36), channel_id=1, source_target_pairs={{0,4},{12,8},{1,5},{13,9},{2,6},{14,10},{3,7},{15,11},{16,20},{28,... | collective-permute-start | bytes 1179656 | tf_op jit(solution)/shard_map/ppermute | solution.py:196
  91.6 4.4 %collective-permute-done.21 = bf16[192,1024]{1,0:T(8,128)(2,1)S(1)} collective-permute-done((bf16[192,1024]{1,0:T(8,128)(2,1)S(1)}, bf16[192,1024]{1,0:T(8,128)(2,1)S(1)}, u32[]{:S(2)}, u32[]{:S(2)}) %collective-permute-start.21) | collective-permute-done | bytes 393248 | tf_op jit(solution)/shard_map/ppermute | solution.py:196
  96.1 8.3 %collective-permute-done.24 = bf16[192,1024]{1,0:T(8,128)(2,1)S(1)} collective-permute-done((bf16[192,1024]{1,0:T(8,128)(2,1)S(1)}, bf16[192,1024]{1,0:T(8,128)(2,1)S(1)}, u32[]{:S(2)}, u32[]{:S(2)}) %collective-permute-start.24) | collective-permute-done | bytes 393248 | tf_op jit(solution)/shard_map/ppermute | solution.py:196
  105.3 7.6 %collective-permute-done.27 = bf16[192,1024]{1,0:T(8,128)(2,1)S(1)} collective-permute-done((bf16[192,1024]{1,0:T(8,128)(2,1)S(1)}, bf16[192,1024]{1,0:T(8,128)(2,1)S(1)}, u32[]{:S(2)}, u32[]{:S(2)}) %collective-permute-start.27) | collective-permute-done | bytes 393248 | tf_op jit(solution)/shard_map/ppermute | solution.py:196
  113.7 7.3 %collective-permute-done.30 = bf16[192,1024]{1,0:T(8,128)(2,1)S(1)} collective-permute-done((bf16[192,1024]{1,0:T(8,128)(2,1)S(1)}, bf16[192,1024]{1,0:T(8,128)(2,1)S(1)}, u32[]{:S(2)}, u32[]{:S(2)}) %collective-permute-start.30) | collective-permute-done | bytes 393248 | tf_op jit(solution)/shard_map/ppermute | solution.py:196
  122.4 1.5 fusion.2
  129.9 12.4 %collective-permute-done.23 = bf16[192,1024]{1,0:T(8,128)(2,1)S(1)} collective-permute-done((bf16[192,1024]{1,0:T(8,128)(2,1)S(1)}, bf16[192,1024]{1,0:T(8,128)(2,1)S(1)}, u32[]{:S(2)}, u32[]{:S(2)}) %collective-permute-start.23) | collective-permute-done | bytes 393248 | tf_op jit(solution)/shard_map/ppermute | solution.py:200
  142.9 7.8 %collective-permute-done.26 = bf16[192,1024]{1,0:T(8,128)(2,1)S(1)} collective-permute-done((bf16[192,1024]{1,0:T(8,128)(2,1)S(1)}, bf16[192,1024]{1,0:T(8,128)(2,1)S(1)}, u32[]{:S(2)}, u32[]{:S(2)}) %collective-permute-start.26) | collective-permute-done | bytes 393248 | tf_op jit(solution)/shard_map/ppermute | solution.py:200
  151.0 8.2 %collective-permute-done.29 = bf16[192,1024]{1,0:T(8,128)(2,1)S(1)} collective-permute-done((bf16[192,1024]{1,0:T(8,128)(2,1)S(1)}, bf16[192,1024]{1,0:T(8,128)(2,1)S(1)}, u32[]{:S(2)}, u32[]{:S(2)}) %collective-permute-start.29) | collective-permute-done | bytes 393248 | tf_op jit(solution)/shard_map/ppermute | solution.py:200
  159.4 6.8 %collective-permute-done.32 = bf16[192,1024]{1,0:T(8,128)(2,1)S(1)} collective-permute-done((bf16[192,1024]{1,0:T(8,128)(2,1)S(1)}, bf16[192,1024]{1,0:T(8,128)(2,1)S(1)}, u32[]{:S(2)}, u32[]{:S(2)}) %collective-permute-start.32) | collective-permute-done | bytes 393248 | tf_op jit(solution)/shard_map/ppermute | solution.py:200
  166.6 1.7 copy-done.8
  (102 shorter events, 24.3 us)
Async XLA Ops:
  0.7 26.4 %collective-permute-start.1 = (bf16[512,1024]{1,0:T(8,128)(2,1)}, bf16[512,1024]{1,0:T(8,128)(2,1)S(1)}, u32[]{:S(2)}, u32[]{:S(2)}) collective-permute-start(bf16[512,1024]{1,0:T(8,128)(2,1)} %param.10), channel_id=1, source_target_pairs={{0,2},{1,3},{2,0},{3,1},{4,6},{5,7},{6,4},{7,5},{8,10},{9,11},{10,... | collective-permute-start | bytes 3145736 | tf_op jit(solution)/shard_map/ppermute | solution.py:183
  3.7 31.4 %collective-permute-start = (bf16[512,1024]{1,0:T(8,128)(2,1)}, bf16[512,1024]{1,0:T(8,128)(2,1)}, u32[]{:S(2)}, u32[]{:S(2)}) collective-permute-start(bf16[512,1024]{1,0:T(8,128)(2,1)} %param.10), channel_id=1, source_target_pairs={{0,1},{1,0},{2,3},{3,2},{4,5},{5,4},{6,7},{7,6},{8,9},{9,8},{10,11... | collective-permute-start | bytes 3145736 | tf_op jit(solution)/shard_map/ppermute | solution.py:183
  27.0 11.3 %collective-permute-start.2 = (bf16[512,1024]{1,0:T(8,128)(2,1)S(1)}, bf16[512,1024]{1,0:T(8,128)(2,1)}, u32[]{:S(2)}, u32[]{:S(2)}) collective-permute-start(bf16[512,1024]{1,0:T(8,128)(2,1)S(1)} %collective-permute-done.1), channel_id=1, source_target_pairs={{0,1},{1,0},{2,3},{3,2},{4,5},{5,4},{6,7},{7,6},{8,9},{9,8},{10,11... | collective-permute-start | bytes 3145736 | tf_op jit(solution)/shard_map/ppermute | solution.py:183
  27.8 15.9 %collective-permute-start.6 = (bf16[16,512]{1,0:T(8,128)(2,1)S(1)}, bf16[16,512]{1,0:T(8,128)(2,1)S(1)}, u32[]{:S(2)}, u32[]{:S(2)}) collective-permute-start(bf16[16,512]{1,0:T(8,128)(2,1)S(1)} %get-tuple-element.33), channel_id=1, source_target_pairs={{0,4},{4,0},{8,12},{12,8},{1,5},{5,1},{9,13},{13,9},{2,6},{6,2},{1... | collective-permute-start | bytes 49160 | tf_op jit(solution)/shard_map/ppermute | solution.py:183
  29.6 14.2 %collective-permute-start.7 = (bf16[16,512]{1,0:T(8,128)(2,1)S(1)}, bf16[16,512]{1,0:T(8,128)(2,1)S(1)}, u32[]{:S(2)}, u32[]{:S(2)}) collective-permute-start(bf16[16,512]{1,0:T(8,128)(2,1)S(1)} %get-tuple-element.35), channel_id=1, source_target_pairs={{0,8},{4,12},{8,0},{12,4},{1,9},{5,13},{9,1},{13,5},{2,10},{6,14},... | collective-permute-start | bytes 49160 | tf_op jit(solution)/shard_map/ppermute | solution.py:183
  32.2 12.2 %collective-permute-start.8 = (bf16[16,512]{1,0:T(8,128)(2,1)S(1)}, bf16[16,512]{1,0:T(8,128)(2,1)S(1)}, u32[]{:S(2)}, u32[]{:S(2)}) collective-permute-start(bf16[16,512]{1,0:T(8,128)(2,1)S(1)} %get-tuple-element.32), channel_id=1, source_target_pairs={{0,12},{4,8},{8,4},{12,0},{1,13},{5,9},{9,5},{13,1},{2,14},{6,10},... | collective-permute-start | bytes 49160 | tf_op jit(solution)/shard_map/ppermute | solution.py:183
  35.1 13.1 %collective-permute-start.9 = (f32[16,512]{1,0:T(8,128)S(1)}, f32[16,512]{1,0:T(8,128)S(1)}, u32[]{:S(2)}, u32[]{:S(2)}) collective-permute-start(f32[16,512]{1,0:T(8,128)S(1)} %get-tuple-element.29), channel_id=1, source_target_pairs={{0,4},{4,0},{8,12},{12,8},{1,5},{5,1},{9,13},{13,9},{2,6},{6,2},{1... | collective-permute-start | bytes 98312 | tf_op jit(solution)/shard_map/ppermute | solution.py:183
  38.4 10.0 %collective-permute-start.10 = (f32[16,512]{1,0:T(8,128)S(1)}, f32[16,512]{1,0:T(8,128)S(1)}, u32[]{:S(2)}, u32[]{:S(2)}) collective-permute-start(f32[16,512]{1,0:T(8,128)S(1)} %get-tuple-element.31), channel_id=1, source_target_pairs={{0,8},{4,12},{8,0},{12,4},{1,9},{5,13},{9,1},{13,5},{2,10},{6,14},... | collective-permute-start | bytes 98312 | tf_op jit(solution)/shard_map/ppermute | solution.py:183
  43.7 6.4 %collective-permute-start.11 = (f32[16,512]{1,0:T(8,128)S(1)}, f32[16,512]{1,0:T(8,128)S(1)}, u32[]{:S(2)}, u32[]{:S(2)}) collective-permute-start(f32[16,512]{1,0:T(8,128)S(1)} %get-tuple-element.28), channel_id=1, source_target_pairs={{0,12},{4,8},{8,4},{12,0},{1,13},{5,9},{9,5},{13,1},{2,14},{6,10},... | collective-permute-start | bytes 98312 | tf_op jit(solution)/shard_map/ppermute | solution.py:183
  43.8 6.3 %collective-permute-start.3 = (bf16[48,512]{1,0:T(8,128)(2,1)S(1)}, bf16[48,512]{1,0:T(8,128)(2,1)S(1)}, u32[]{:S(2)}, u32[]{:S(2)}) collective-permute-start(bf16[48,512]{1,0:T(8,128)(2,1)S(1)} %bitcast.63), channel_id=1, source_target_pairs={{0,4},{4,0},{8,12},{12,8},{1,5},{5,1},{9,13},{13,9},{2,6},{6,2},{1... | collective-permute-start | bytes 147464 | tf_op jit(solution)/shard_map/ppermute | solution.py:183
  44.5 6.8 %collective-permute-start.4 = (bf16[48,512]{1,0:T(8,128)(2,1)S(1)}, bf16[48,512]{1,0:T(8,128)(2,1)S(1)}, u32[]{:S(2)}, u32[]{:S(2)}) collective-permute-start(bf16[48,512]{1,0:T(8,128)(2,1)S(1)} %bitcast.62), channel_id=1, source_target_pairs={{0,8},{4,12},{8,0},{12,4},{1,9},{5,13},{9,1},{13,5},{2,10},{6,14},... | collective-permute-start | bytes 147464 | tf_op jit(solution)/shard_map/ppermute | solution.py:183
  48.2 5.9 %collective-permute-start.5 = (bf16[48,512]{1,0:T(8,128)(2,1)S(1)}, bf16[48,512]{1,0:T(8,128)(2,1)S(1)}, u32[]{:S(2)}, u32[]{:S(2)}) collective-permute-start(bf16[48,512]{1,0:T(8,128)(2,1)S(1)} %bitcast.61), channel_id=1, source_target_pairs={{0,12},{4,8},{8,4},{12,0},{1,13},{5,9},{9,5},{13,1},{2,14},{6,10},... | collective-permute-start | bytes 147464 | tf_op jit(solution)/shard_map/ppermute | solution.py:183
  48.4 36.3 %collective-permute-start.18 = (bf16[3,64,1024]{2,1,0:T(8,128)(2,1)S(1)}, bf16[3,64,1024]{2,1,0:T(8,128)(2,1)S(1)}, u32[]{:S(2)}, u32[]{:S(2)}) collective-permute-start(bf16[3,64,1024]{2,1,0:T(8,128)(2,1)S(1)} %get-tuple-element.22), channel_id=1, source_target_pairs={{0,2},{1,3},{2,0},{3,1},{4,6},{5,7},{6,4},{7,5},{8,10},{9,11},{10,... | collective-permute-start | bytes 1179656 | tf_op jit(solution)/shard_map/ppermute | solution.py:183
  50.1 38.4 %collective-permute-start.16 = (bf16[3,64,1024]{2,1,0:T(8,128)(2,1)S(1)}, bf16[3,64,1024]{2,1,0:T(8,128)(2,1)S(1)}, u32[]{:S(2)}, u32[]{:S(2)}) collective-permute-start(bf16[3,64,1024]{2,1,0:T(8,128)(2,1)S(1)} %get-tuple-element.23), channel_id=1, source_target_pairs={{0,1},{1,0},{2,3},{3,2},{4,5},{5,4},{6,7},{7,6},{8,9},{9,8},{10,11... | collective-permute-start | bytes 1179656 | tf_op jit(solution)/shard_map/ppermute | solution.py:183
  50.1 71.6 %collective-permute-start.20 = (bf16[3,64,1024]{2,1,0:T(8,128)(2,1)S(1)}, bf16[3,64,1024]{2,1,0:T(8,128)(2,1)S(1)}, u32[]{:S(2)}, u32[]{:S(2)}) collective-permute-start(bf16[3,64,1024]{2,1,0:T(8,128)(2,1)S(1)} %get-tuple-element.21), channel_id=1, source_target_pairs={{0,3},{1,2},{2,1},{3,0},{4,7},{5,6},{6,5},{7,4},{8,11},{9,10},{10,... | collective-permute-start | bytes 1179656 | tf_op jit(solution)/shard_map/ppermute | solution.py:183
  57.1 15.5 %collective-permute-start.12 = (bf16[48,512]{1,0:T(8,128)(2,1)S(1)}, bf16[48,512]{1,0:T(8,128)(2,1)S(1)}, u32[]{:S(2)}, u32[]{:S(2)}) collective-permute-start(bf16[48,512]{1,0:T(8,128)(2,1)S(1)} %get-tuple-element.13), channel_id=1, source_target_pairs={{0,4},{4,0},{8,12},{12,8},{1,5},{5,1},{9,13},{13,9},{2,6},{6,2},{1... | collective-permute-start | bytes 147464 | tf_op jit(solution)/shard_map/ppermute | solution.py:183
  72.6 6.0 %collective-permute-start.14 = (bf16[48,512]{1,0:T(8,128)(2,1)S(1)}, bf16[48,512]{1,0:T(8,128)(2,1)S(1)}, u32[]{:S(2)}, u32[]{:S(2)}) collective-permute-start(bf16[48,512]{1,0:T(8,128)(2,1)S(1)} %get-tuple-element.15), channel_id=1, source_target_pairs={{0,12},{4,8},{8,4},{12,0},{1,13},{5,9},{9,5},{13,1},{2,14},{6,10},... | collective-permute-start | bytes 147464 | tf_op jit(solution)/shard_map/ppermute | solution.py:183
  78.6 8.0 %collective-permute-start.17 = (bf16[192,512]{1,0:T(8,128)(2,1)S(1)}, bf16[192,512]{1,0:T(8,128)(2,1)S(1)}, u32[]{:S(2)}, u32[]{:S(2)}) collective-permute-start(bf16[192,512]{1,0:T(8,128)(2,1)S(1)} %bitcast.46), channel_id=1, source_target_pairs={{0,2},{1,3},{2,0},{3,1},{4,6},{5,7},{6,4},{7,5},{8,10},{9,11},{10,... | collective-permute-start | bytes 589832 | tf_op jit(solution)/shard_map/ppermute | solution.py:183
  80.2 9.6 %collective-permute-start.15 = (bf16[192,512]{1,0:T(8,128)(2,1)S(1)}, bf16[192,512]{1,0:T(8,128)(2,1)S(1)}, u32[]{:S(2)}, u32[]{:S(2)}) collective-permute-start(bf16[192,512]{1,0:T(8,128)(2,1)S(1)} %bitcast.47), channel_id=1, source_target_pairs={{0,1},{1,0},{2,3},{3,2},{4,5},{5,4},{6,7},{7,6},{8,9},{9,8},{10,11... | collective-permute-start | bytes 589832 | tf_op jit(solution)/shard_map/ppermute | solution.py:183
  84.7 11.4 %collective-permute-start.21 = (bf16[192,1024]{1,0:T(8,128)(2,1)S(1)}, bf16[192,1024]{1,0:T(8,128)(2,1)S(1)}, u32[]{:S(2)}, u32[]{:S(2)}) collective-permute-start(bf16[192,1024]{1,0:T(8,128)(2,1)S(1)} %get-tuple-element.36), channel_id=1, source_target_pairs={{0,4},{12,8},{1,5},{13,9},{2,6},{14,10},{3,7},{15,11},{16,20},{28,... | collective-permute-start | bytes 1179656 | tf_op jit(solution)/shard_map/ppermute | solution.py:196
  86.7 17.8 %collective-permute-start.24 = (bf16[192,1024]{1,0:T(8,128)(2,1)S(1)}, bf16[192,1024]{1,0:T(8,128)(2,1)S(1)}, u32[]{:S(2)}, u32[]{:S(2)}) collective-permute-start(bf16[192,1024]{1,0:T(8,128)(2,1)S(1)} %get-tuple-element.38), channel_id=1, source_target_pairs={{0,4},{12,8},{1,5},{13,9},{2,6},{14,10},{3,7},{15,11},{16,20},{28,... | collective-permute-start | bytes 1179656 | tf_op jit(solution)/shard_map/ppermute | solution.py:196
  88.5 24.4 %collective-permute-start.27 = (bf16[192,1024]{1,0:T(8,128)(2,1)S(1)}, bf16[192,1024]{1,0:T(8,128)(2,1)S(1)}, u32[]{:S(2)}, u32[]{:S(2)}) collective-permute-start(bf16[192,1024]{1,0:T(8,128)(2,1)S(1)} %get-tuple-element.40), channel_id=1, source_target_pairs={{0,4},{12,8},{1,5},{13,9},{2,6},{14,10},{3,7},{15,11},{16,20},{28,... | collective-permute-start | bytes 1179656 | tf_op jit(solution)/shard_map/ppermute | solution.py:196
  89.8 31.2 %collective-permute-start.30 = (bf16[192,1024]{1,0:T(8,128)(2,1)S(1)}, bf16[192,1024]{1,0:T(8,128)(2,1)S(1)}, u32[]{:S(2)}, u32[]{:S(2)}) collective-permute-start(bf16[192,1024]{1,0:T(8,128)(2,1)S(1)} %get-tuple-element.42), channel_id=1, source_target_pairs={{0,4},{12,8},{1,5},{13,9},{2,6},{14,10},{3,7},{15,11},{16,20},{28,... | collective-permute-start | bytes 1179656 | tf_op jit(solution)/shard_map/ppermute | solution.py:196
  96.0 26.4 %collective-permute-start.19 = (bf16[192,512]{1,0:T(8,128)(2,1)S(1)}, bf16[192,512]{1,0:T(8,128)(2,1)S(1)}, u32[]{:S(2)}, u32[]{:S(2)}) collective-permute-start(bf16[192,512]{1,0:T(8,128)(2,1)S(1)} %collective-permute-done.17), channel_id=1, source_target_pairs={{0,1},{1,0},{2,3},{3,2},{4,5},{5,4},{6,7},{7,6},{8,9},{9,8},{10,11... | collective-permute-start | bytes 589832 | tf_op jit(solution)/shard_map/ppermute | solution.py:183
  104.5 19.4 %collective-permute-start.22 = (bf16[192,1024]{1,0:T(8,128)(2,1)S(1)}, bf16[192,1024]{1,0:T(8,128)(2,1)S(1)}, u32[]{:S(2)}, u32[]{:S(2)}) collective-permute-start(bf16[192,1024]{1,0:T(8,128)(2,1)S(1)} %fusion.4), channel_id=1, source_target_pairs={{4,8},{8,4},{5,9},{9,5},{6,10},{10,6},{7,11},{11,7},{20,24},{24,20... | collective-permute-start | bytes 1179656 | tf_op jit(solution)/shard_map/ppermute | solution.py:198
  112.9 12.5 %collective-permute-start.25 = (bf16[192,1024]{1,0:T(8,128)(2,1)S(1)}, bf16[192,1024]{1,0:T(8,128)(2,1)S(1)}, u32[]{:S(2)}, u32[]{:S(2)}) collective-permute-start(bf16[192,1024]{1,0:T(8,128)(2,1)S(1)} %fusion.5), channel_id=1, source_target_pairs={{4,8},{8,4},{5,9},{9,5},{6,10},{10,6},{7,11},{11,7},{20,24},{24,20... | collective-permute-start | bytes 1179656 | tf_op jit(solution)/shard_map/ppermute | solution.py:198
  121.0 5.9 %collective-permute-start.28 = (bf16[192,1024]{1,0:T(8,128)(2,1)S(1)}, bf16[192,1024]{1,0:T(8,128)(2,1)S(1)}, u32[]{:S(2)}, u32[]{:S(2)}) collective-permute-start(bf16[192,1024]{1,0:T(8,128)(2,1)S(1)} %fusion.6), channel_id=1, source_target_pairs={{4,8},{8,4},{5,9},{9,5},{6,10},{10,6},{7,11},{11,7},{20,24},{24,20... | collective-permute-start | bytes 1179656 | tf_op jit(solution)/shard_map/ppermute | solution.py:198
  121.7 6.7 %collective-permute-start.31 = (bf16[192,1024]{1,0:T(8,128)(2,1)S(1)}, bf16[192,1024]{1,0:T(8,128)(2,1)S(1)}, u32[]{:S(2)}, u32[]{:S(2)}) collective-permute-start(bf16[192,1024]{1,0:T(8,128)(2,1)S(1)} %fusion.7), channel_id=1, source_target_pairs={{4,8},{8,4},{5,9},{9,5},{6,10},{10,6},{7,11},{11,7},{20,24},{24,20... | collective-permute-start | bytes 1179656 | tf_op jit(solution)/shard_map/ppermute | solution.py:198
  124.1 18.2 %collective-permute-start.23 = (bf16[192,1024]{1,0:T(8,128)(2,1)S(1)}, bf16[192,1024]{1,0:T(8,128)(2,1)S(1)}, u32[]{:S(2)}, u32[]{:S(2)}) collective-permute-start(bf16[192,1024]{1,0:T(8,128)(2,1)S(1)} %fusion.15), channel_id=1, source_target_pairs={{4,0},{8,12},{5,1},{9,13},{6,2},{10,14},{7,3},{11,15},{20,16},{24,... | collective-permute-start | bytes 1179656 | tf_op jit(solution)/shard_map/ppermute | solution.py:200
  125.6 25.2 %collective-permute-start.26 = (bf16[192,1024]{1,0:T(8,128)(2,1)S(1)}, bf16[192,1024]{1,0:T(8,128)(2,1)S(1)}, u32[]{:S(2)}, u32[]{:S(2)}) collective-permute-start(bf16[192,1024]{1,0:T(8,128)(2,1)S(1)} %fusion.16), channel_id=1, source_target_pairs={{4,0},{8,12},{5,1},{9,13},{6,2},{10,14},{7,3},{11,15},{20,16},{24,... | collective-permute-start | bytes 1179656 | tf_op jit(solution)/shard_map/ppermute | solution.py:200
  127.1 32.1 %collective-permute-start.29 = (bf16[192,1024]{1,0:T(8,128)(2,1)S(1)}, bf16[192,1024]{1,0:T(8,128)(2,1)S(1)}, u32[]{:S(2)}, u32[]{:S(2)}) collective-permute-start(bf16[192,1024]{1,0:T(8,128)(2,1)S(1)} %fusion.17), channel_id=1, source_target_pairs={{4,0},{8,12},{5,1},{9,13},{6,2},{10,14},{7,3},{11,15},{20,16},{24,... | collective-permute-start | bytes 1179656 | tf_op jit(solution)/shard_map/ppermute | solution.py:200
  128.6 37.7 %collective-permute-start.32 = (bf16[192,1024]{1,0:T(8,128)(2,1)S(1)}, bf16[192,1024]{1,0:T(8,128)(2,1)S(1)}, u32[]{:S(2)}, u32[]{:S(2)}) collective-permute-start(bf16[192,1024]{1,0:T(8,128)(2,1)S(1)} %fusion.18), channel_id=1, source_target_pairs={{4,0},{8,12},{5,1},{9,13},{6,2},{10,14},{7,3},{11,15},{20,16},{24,... | collective-permute-start | bytes 1179656 | tf_op jit(solution)/shard_map/ppermute | solution.py:200
  (14 other events, 203.4 us)
where the time goes:
time: 169 us; the launch traced here: 168 us
  waiting for transfers between devices  105 us (62%)
  starting transfers between devices  39.8 us (24%)
  matrix products  12.7 us (8%)
  local copies, waits for them, and re-layouts  4.02 us (2%)
  Pallas kernels  3.01 us (2%)
  other arithmetic  2.21 us (1%)
    ppermute x24, waiting for transfers between devices, swap(): return lax.ppermute(values, axis, [(i, i ^ mask) for i in range(size)])  42.4 us
    ppermute x4, waiting for transfers between devices, sum_over_ctx(): given = lax.ppermute(total.astype(BF16), 'ctx', [(1, 0), (2, 3)])  35.2 us
    ppermute x4, waiting for transfers between devices, sum_over_ctx(): from_end = lax.ppermute(x.astype(BF16), 'ctx', [(0, 1), (3, 2)])  27.7 us
    ppermute x24, starting transfers between devices, swap(): return lax.ppermute(values, axis, [(i, i ^ mask) for i in range(size)])  26 us
    ppermute x4, starting transfers between devices, sum_over_ctx(): from_end = lax.ppermute(x.astype(BF16), 'ctx', [(0, 1), (3, 2)])  5.9 us
    dot_general x4, matrix products, per_device(): lax.dot_general(columns(weight_rows, m), features[m], (((1,), (1,)), ((),...  5.84 us
    ppermute x4, starting transfers between devices, sum_over_ctx(): given = lax.ppermute(total.astype(BF16), 'ctx', [(1, 0), (2, 3)])  5.17 us
    dot_general x4, matrix products, mm(): return jnp.dot(left, right, preferred_element_type=F32)  3.99 us
  transfers between devices with their start and end apart: 36, of which 15 were waited for; matrix products, arithmetic and copies ran while one was open for 10% of the time, Pallas kernels for 2%

commit v1 on v0

v1 whole, which is shorter than its diff:
```python
import functools
import math

import jax
import jax.numpy as jnp
import numpy as np
from jax import lax
from jax.experimental import pallas as pl
from jax.experimental.pallas import tpu as pltpu
from jax.sharding import PartitionSpec as P

LANES = 128
BF16 = jnp.bfloat16
F32 = jnp.float32
VMEM = pl.BlockSpec(memory_space=pltpu.VMEM)
ANY = pl.BlockSpec(memory_space=pl.ANY)
HBM = pl.BlockSpec(memory_space=pltpu.HBM)


def split_table(table):
    high = np.asarray(table, np.float32).astype(BF16)
    low = (np.asarray(table, np.float64) - high.astype(np.float64)).astype(BF16)
    return np.stack([high, low])


def fourier_tables(tokens, group):
    period = 2 * tokens
    rows = period // LANES
    used = rows // 2
    freqs = rows // 2 + 1
    part = -(-freqs * group // 8) * 8
    k1 = np.arange(freqs)
    n1 = np.arange(used)
    angle = 2.0 * math.pi * (np.outer(k1, n1) % rows) / rows
    eye = np.eye(group)
    forward = np.zeros((2 * part, used * group))
    forward[: freqs * group] = np.kron(np.cos(angle), eye)
    forward[part : part + freqs * group] = np.kron(-np.sin(angle), eye)
    weight = np.where((k1 == 0) | (k1 == rows // 2), 1.0, 2.0)[None, :] / period
    inverse = np.zeros((used * group, 2 * part))
    inverse[:, : freqs * group] = np.kron(np.cos(angle.T) * weight, eye)
    inverse[:, part : part + freqs * group] = np.kron(-np.sin(angle.T) * weight, eye)
    n2 = np.arange(LANES)
    turn = 2.0 * math.pi * np.outer(k1, n2) / period
    twiddle = np.zeros((2, part, LANES), np.float32)
    twiddle[0, : freqs * group] = np.repeat(np.cos(turn), group, axis=0)
    twiddle[1, : freqs * group] = np.repeat(np.sin(turn), group, axis=0)
    inner = 2.0 * math.pi * (np.outer(n2, n2) % LANES) / LANES
    cos, sin = np.cos(inner), np.sin(inner)
    second = np.block([[cos, -sin], [sin, cos]])
    second_back = np.block([[cos, sin], [-sin, cos]])
    return (
        split_table(forward),
        split_table(second),
        split_table(second_back),
        split_table(inverse),
        twiddle,
    )


def halves(values):
    high = values.astype(BF16)
    return high, (values - high.astype(F32)).astype(BF16)


def mm(left, right):
    return jnp.dot(left, right, preferred_element_type=F32)


def table_left(table, values):
    high, low = halves(values)
    return mm(table[0], high) + (mm(table[0], low) + mm(table[1], high))


def table_right(values, table):
    high, low = halves(values)
    return mm(high, table[0]) + (mm(low, table[0]) + mm(high, table[1]))


def conv_kernel(blocks, chans, group, factor, *refs):
    count = 2 * blocks + 5
    gain_ref, sources, refs = refs[0], refs[1 : 1 + count], refs[1 + count :]
    out_refs = refs[:blocks]
    series, results, inputs = refs[blocks : 3 + blocks]
    held = refs[3 + blocks : 3 + blocks + count]
    sems = refs[3 + blocks + count]
    copies = [pltpu.make_async_copy(sources[i], held[i], sems.at[i]) for i in range(count)]
    for copy in copies:
        copy.start()
    ready_refs, signal_refs = held[:blocks], held[blocks : 2 * blocks]
    fwd_ref, second_ref, back_ref, inv_ref, twiddle_ref = held[2 * blocks :]
    place = lax.axis_index("ctx")
    length = series.shape[-1]
    cuts = length // LANES
    for m in range(blocks):
        where = place ^ m
        copies[m].wait()
        copies[blocks + m].wait()
        values = signal_refs[m][...].astype(F32)
        upstream = ready_refs[m][:chans, :]
        inputs[0, where] = values[:chans]
        inputs[1, where] = values[2 * chans :]
        inputs[2, where] = upstream
        series[0, where] = ready_refs[m][chans:, :] * factor
        series[1, where] = values[:chans] * values[2 * chans :]
        series[2, where] = upstream * values[chans : 2 * chans]
    for copy in copies[2 * blocks :]:
        copy.wait()
    part = twiddle_ref.shape[1]
    cos, sin = twiddle_ref[0], twiddle_ref[1]
    for start in range(0, chans, group):
        picked = []
        for q in range(3):
            tiles = []
            for z in range(blocks):
                loaded = series[q, z]
                loaded = loaded[start : start + group]
                for n in range(cuts):
                    tiles.append(loaded[:, n * LANES : (n + 1) * LANES])
            picked.append(jnp.concatenate(tiles, axis=0))
        first = table_left(fwd_ref, jnp.concatenate(picked, axis=1))
        turned = []
        for q in range(3):
            re = first[:part, q * LANES : (q + 1) * LANES]
            im = first[part:, q * LANES : (q + 1) * LANES]
            turned.append(jnp.concatenate([re * cos + im * sin, im * cos - re * sin], axis=1))
        spectra = table_right(jnp.concatenate(turned, axis=0), second_ref)
        parts = [
            (spectra[q * part : (q + 1) * part, :LANES], spectra[q * part : (q + 1) * part, LANES:])
            for q in range(3)
        ]
        (fr, fi), (gr, gi), (ur, ui) = parts
        products = jnp.concatenate(
            [
                jnp.concatenate([fr * gr - fi * gi, fr * gi + fi * gr], axis=1),
                jnp.concatenate([fr * ur + fi * ui, fr * ui - fi * ur], axis=1),
                jnp.concatenate([gr * ur + gi * ui, gr * ui - gi * ur], axis=1),
            ],
            axis=0,
        )
        back = table_right(products, back_ref)
        turned = []
        for q in range(3):
            re = back[q * part : (q + 1) * part, :LANES]
            im = back[q * part : (q + 1) * part, LANES:]
            turned.append(jnp.concatenate([re * cos - im * sin, im * cos + re * sin], axis=0))
        final = table_left(inv_ref, jnp.concatenate(turned, axis=1))
        for q in range(3):
            for z in range(blocks):
                tiles = [
                    final[(z * cuts + n) * group : (z * cuts + n + 1) * group, q * LANES : (q + 1) * LANES]
                    for n in range(cuts)
                ]
                results[q, z, start : start + group, :] = jnp.concatenate(tiles, axis=1)
    gain = gain_ref[...]
    for z in range(blocks):
        conv_out = results[0, z] + gain * series[1, z]
        grad_gated = results[1, z] + gain * series[2, z]
        grads = jnp.concatenate(
            [grad_gated * inputs[1, z], inputs[2, z] * conv_out, grad_gated * inputs[0, z]], axis=0
        ).astype(BF16)
        for ref in out_refs:
            ref[:, z * length : (z + 1) * length] = grads
    for m in range(blocks):
        found = factor * results[2, place ^ m]
        half = length // 2
        rows = jnp.concatenate([found[:, :half], found[:, half:], jnp.zeros((chans, half), F32)], axis=0)
        out_refs[m][:, blocks * length :] = rows.astype(BF16)


def convolve(signals, ready, gain):
    blocks = len(ready)
    chans, length = ready[0].shape[0] // 2, ready[0].shape[1]
    tokens = blocks * length
    group = max(1, min(chans, 8, LANES * LANES // tokens))
    tables = fourier_tables(tokens, group)
    arrays = [*ready, *signals, *[jnp.asarray(table) for table in tables]]
    part = tables[4].shape[1]
    flops = 2 * 3 * (chans // group) * 3 * (4 * part * group * (tokens // LANES) * LANES + 2 * part * 256 * 256)
    return pl.pallas_call(
        functools.partial(conv_kernel, blocks, chans, group, tokens ** (-0.5)),
        out_shape=[jax.ShapeDtypeStruct((3 * chans, tokens + length // 2), BF16)] * blocks,
        in_specs=[VMEM] + [HBM] * len(arrays),
        out_specs=[VMEM] * blocks,
        scratch_shapes=[pltpu.VMEM((3, blocks, chans, length), F32)] * 3
        + [pltpu.VMEM(array.shape, array.dtype) for array in arrays]
        + [pltpu.SemaphoreType.DMA((len(arrays),))],
        compiler_params=pltpu.CompilerParams(vmem_limit_bytes=40 * 2**20),
        cost_estimate=pl.CostEstimate(flops=flops, bytes_accessed=4 * 2**20, transcendentals=0),
        name="conv",
    )(gain, *arrays)


def partial_rows(weight_ref, refs, masks):
    mine = lax.axis_index("chan")
    sums = 0.0
    for m, ref in zip(masks, refs):
        width = ref.shape[1]
        at = pl.multiple_of((mine ^ m) * width, width)
        sums = sums + lax.dot_general(
            ref[...], weight_ref[:, pl.ds(at, width)], (((1,), (1,)), ((), ())), preferred_element_type=F32
        )
    return sums


def start_kernel(masks, weight_ref, *refs):
    refs[-1][...] = partial_rows(weight_ref, refs[:-1], masks)


def more_kernel(masks, weight_ref, sum_ref, *refs):
    refs[-1][...] = sum_ref[...] + partial_rows(weight_ref, refs[:-1], masks)


def finish_kernel(masks, blocks, kinds, share, weight_ref, sum_ref, *refs):
    out_refs = refs[len(masks) : len(masks) + blocks]
    total = refs[-1]
    place = lax.axis_index("ctx")
    total[...] = (sum_ref[...] + partial_rows(weight_ref, refs[: len(masks)], masks)).T
    for m in range(blocks):
        first = (place ^ m) * share
        rows = [total[pl.ds(pl.multiple_of(k * share * blocks + first, share), share), :] for k in range(kinds)]
        out_refs[m][...] = jnp.concatenate(rows, axis=0).astype(BF16)


def project(weight_rows, features, groups, blocks, kinds):
    rows, depth = weight_rows.shape
    length = features[0].shape[0]
    share = rows // kinds // blocks
    sums = []
    for i, masks in enumerate(groups):
        last = i == len(groups) - 1
        if last:
            body = functools.partial(finish_kernel, masks, blocks, kinds, share)
            shape = [jax.ShapeDtypeStruct((kinds * share, length), BF16)] * blocks
        else:
            body = functools.partial(more_kernel if i else start_kernel, masks)
            shape = [jax.ShapeDtypeStruct((length, rows), F32)]
        picked = [features[m] for m in masks]
        flops = 2 * rows * length * depth * len(masks) // len(features)
        sums = pl.pallas_call(
            body,
            out_shape=shape,
            in_specs=[VMEM] * (1 + len(sums) + len(picked)),
            out_specs=[VMEM] * len(shape),
            scratch_shapes=[pltpu.VMEM((rows, length), F32)] if last else [],
            compiler_params=pltpu.CompilerParams(vmem_limit_bytes=40 * 2**20),
            cost_estimate=pl.CostEstimate(flops=flops, bytes_accessed=2**20, transcendentals=0),
            name="project",
        )(weight_rows, *sums, *picked)
    return sums


def product_kernel(kinds, share, blocks, slabs, *refs):
    grad_refs = refs[:blocks]
    sources = refs[blocks : blocks + slabs]
    first_ref, second_ref, own_ref, filter_ref = refs[blocks + slabs : blocks + slabs + 4]
    turned, sems = refs[blocks + slabs + 4 :]
    place = lax.axis_index("ctx")
    length = own_ref.shape[1]
    width = sources[0].shape[1]
    copies = [pltpu.make_async_copy(sources[i], turned.at[i], sems.at[i]) for i in range(slabs)]
    for copy in copies:
        copy.start()
    mine = pl.ds(pl.multiple_of(place * length, length), length)
    for m in range(blocks):
        for k in range(kinds):
            to = pl.multiple_of(k * share * blocks + (place ^ m) * share, share)
            own_ref[pl.ds(to, share), :] = grad_refs[m][k * share : (k + 1) * share, mine]
        to = pl.multiple_of((place ^ m) * share, share)
        end = grad_refs[m][:, blocks * length :].astype(F32)
        filter_ref[pl.ds(to, share), :] = jnp.concatenate([end[:share], end[share : 2 * share]], axis=1)
    left = []
    for b in range(blocks):
        columns = pl.ds(pl.multiple_of((place ^ b) * length, length), length)
        left.append(jnp.concatenate([ref[:, columns] for ref in grad_refs], axis=0))
    left = jnp.concatenate(left, axis=1)
    half = left.shape[0] // 2
    for i in range(slabs):
        copies[i].wait()
        value = mm(left, turned[i]).astype(BF16)
        first_ref[:, i * width : (i + 1) * width] = value[:half]
        second_ref[:, i * width : (i + 1) * width] = value[half:]


def weight_products(grads, turned, kinds, share):
    blocks, slabs = len(grads), len(turned)
    tokens, width = turned[0].shape
    rows = kinds * share
    half = jax.ShapeDtypeStruct((rows * blocks // 2, width * slabs), BF16)
    return pl.pallas_call(
        functools.partial(product_kernel, kinds, share, blocks, slabs),
        out_shape=[
            half,
            half,
            jax.ShapeDtypeStruct((rows * blocks, tokens // blocks), BF16),
            jax.ShapeDtypeStruct((share * blocks, tokens // blocks), F32),
        ],
        in_specs=[VMEM] * blocks + [ANY] * slabs,
        out_specs=[VMEM] * 4,
        scratch_shapes=[pltpu.VMEM((slabs, tokens, width), BF16), pltpu.SemaphoreType.DMA((slabs,))],
        compiler_params=pltpu.CompilerParams(vmem_limit_bytes=40 * 2**20),
        cost_estimate=pl.CostEstimate(
            flops=2 * rows * blocks * tokens * width * slabs, bytes_accessed=6 * 2**20, transcendentals=0
        ),
        name="products",
    )(*grads, *turned)


def input_kernel(count, *refs):
    sums = 0.0
    for grad_ref, weight_ref in zip(refs[:count], refs[count : 2 * count]):
        sums = sums + lax.dot_general(
            grad_ref[...], weight_ref[...], (((0,), (0,)), ((), ())), preferred_element_type=F32
        )
    refs[-1][...] = sums.astype(BF16)


def input_gradient(grads, weights):
    rows, length = grads[0].shape
    width = weights[0].shape[1]
    return pl.pallas_call(
        functools.partial(input_kernel, len(grads)),
        out_shape=jax.ShapeDtypeStruct((length, width), BF16),
        in_specs=[VMEM] * (2 * len(grads)),
        out_specs=VMEM,
        compiler_params=pltpu.CompilerParams(vmem_limit_bytes=40 * 2**20),
        cost_estimate=pl.CostEstimate(
            flops=2 * rows * len(grads) * length * width, bytes_accessed=4 * 2**20, transcendentals=0
        ),
        name="inputs",
    )(*grads, *weights)


def place_kernel(kinds, share, factor, *refs):
    out_ref = refs[-1]
    blocks = (len(refs) - 1) // 2
    place = lax.axis_index("ctx")
    slab = lax.axis_index("chan") ^ pl.program_id(0)
    width = out_ref.shape[1] // blocks
    source = pl.ds(pl.multiple_of(slab * width, width), width)
    for a in range(2):
        for r in range(blocks):
            sender = lax.rem(place + (r if a else blocks - r), blocks)
            columns = pl.ds(pl.multiple_of(sender * width, width), width)
            for b in range(2):
                for k in range(kinds):
                    row = (b * kinds + k) * share
                    value = refs[a * blocks + r][row : row + share, source].astype(F32) * factor
                    to = pl.multiple_of(k * share * blocks + (sender ^ (2 * a + b)) * share, share)
                    out_ref[pl.ds(to, share), columns] = value


def place_weights(pieces, kinds, share, slabs, factor):
    flat = [piece for group in pieces for piece in group]
    depth = flat[0].shape[1]
    rows = kinds * share * len(pieces[0])
    return pl.pallas_call(
        functools.partial(place_kernel, kinds, share, factor),
        out_shape=jax.ShapeDtypeStruct((rows, depth * slabs), F32),
        grid=(slabs,),
        in_specs=[pl.BlockSpec(flat[0].shape, lambda i: (0, 0))] * len(flat),
        out_specs=pl.BlockSpec((rows, depth), lambda i: (0, i)),
        compiler_params=pltpu.CompilerParams(vmem_limit_bytes=40 * 2**20),
        cost_estimate=pl.CostEstimate(flops=0, bytes_accessed=6 * 2**20, transcendentals=0),
        name="place",
    )(*flat)


def swap(values, axis, mask):
    if mask == 0:
        return values
    size = lax.axis_size(axis)
    return lax.ppermute(values, axis, [(i, i ^ mask) for i in range(size)])


def after(values, *others):
    return lax.optimization_barrier((values, *others))[0]


def gather_chan(values):
    slabs = lax.axis_size("chan")
    if slabs != 4:
        return [swap(values, "chan", m) for m in range(slabs)]
    far = swap(values, "chan", 2)
    return [values, swap(values, "chan", 1), far, swap(far, "chan", 1)]


def ring(values, step):
    size = lax.axis_size("ctx")
    found = [values]
    while len(found) < size:
        found.append(lax.ppermute(found[-1], "ctx", [(i, (i + step) % size) for i in range(size)]))
    return found


def general_tail(messages, features, place, mine, kinds, share, factor):
    blocks = lax.axis_size("ctx")
    length, width = features[0].shape
    rows = kinds * share * blocks
    grad_proj = jnp.zeros((kinds, share * blocks, length), BF16)
    grad_filter = jnp.zeros((share * blocks, length), F32)
    for m, message in enumerate(messages):
        piece = lax.dynamic_slice_in_dim(message, (place ^ m) * length, length, 1)
        piece = swap(piece, "ctx", m).reshape(kinds, share, length)
        grad_proj = lax.dynamic_update_slice_in_dim(grad_proj, piece, (place ^ m) * share, 1)
        end = swap(message[: 2 * share, blocks * length :], "ctx", m).astype(F32)
        end = jnp.concatenate([end[:share], end[share:]], axis=1)
        grad_filter = lax.dynamic_update_slice_in_dim(grad_filter, end, (place ^ m) * share, 0)
    grad_proj = grad_proj.reshape(rows, length)
    grad_weight = jnp.zeros((rows, width * len(features)), F32)
    for m, slab in enumerate(features):
        total = lax.psum(mm(grad_proj, slab).astype(BF16), "ctx").astype(F32) * factor
        grad_weight = lax.dynamic_update_slice_in_dim(grad_weight, total, (mine ^ m) * width, 1)
    return grad_proj, grad_weight, grad_filter


def per_device(activations, proj_weight, long_filter, skip_gain, out_grad):
    blocks = lax.axis_size("ctx")
    slabs = lax.axis_size("chan")
    place = lax.axis_index("ctx")
    mine = lax.axis_index("chan")
    length, width = activations.shape
    kinds, own, depth = proj_weight.shape
    share = own // blocks
    factor = (length * blocks) ** (-0.5)
    rows = kinds * own
    line = blocks == 4 and slabs == 4 and width % (blocks * LANES) == 0 and share % 16 == 0
    weight_rows = proj_weight.reshape(rows, depth)

    def share_of(array, m, axis=0, size=share):
        return lax.dynamic_slice_in_dim(array, (place ^ m) * size, size, axis)

    if line:
        features = [activations, swap(activations, "chan", 1), swap(activations, "chan", 2)]
        quarter = width // blocks
        turned = [swap(share_of(activations, m, 1, quarter), "ctx", m) for m in range(blocks)]
    else:
        features = [swap(activations, "chan", m) for m in range(slabs)]

    ready = jnp.stack([out_grad.astype(F32), long_filter], axis=1).reshape(blocks, share, 2, length)
    ready = jnp.swapaxes(ready, 1, 2).reshape(blocks * 2 * share, length)
    ready = [share_of(ready, m, 0, 2 * share) for m in range(blocks)]
    ready = after(ready, features[1])
    ready = [swap(piece, "ctx", m) for m, piece in enumerate(ready)]
    gain = share_of(skip_gain, 0)[:, None]

    groups = [[0, 1], [2], [3]] if line else [[0], list(range(1, slabs))]
    if line:
        features[2], turned, ready = lax.optimization_barrier((features[2], turned, ready))
        features.append(swap(features[2], "chan", 1))
        turned = jnp.concatenate(turned, axis=0)
        far = swap(turned, "chan", 2)
        turned = [turned, swap(turned, "chan", 1), far]

    pieces = project(weight_rows, features, groups, blocks, kinds)
    signals = [swap(piece, "ctx", m) for m, piece in enumerate(pieces)]
    messages = convolve(signals, ready, gain)
    if line:
        turned.append(swap(after(far, messages[0]), "chan", 1))

    weight_cols = [lax.dynamic_slice_in_dim(weight_rows, (mine ^ m) * width, width, 1) for m in range(slabs)]
    weight_cols = after(weight_cols, turned[2] if line else signals[-1])
    weight_cols = [swap(cols, "chan", m) for m, cols in enumerate(weight_cols)]

    if line:
        messages = [swap(message, "ctx", m) for m, message in enumerate(messages)]
        first, second, grad_proj, grad_filter = weight_products(messages, turned, kinds, share)
        pieces = [ring(first, 1), ring(second, -1)]
        grad_weight = place_weights(pieces, kinds, share, slabs, factor)
    else:
        grad_proj, grad_weight, grad_filter = general_tail(messages, features, place, mine, kinds, share, factor)

    return (
        input_gradient(gather_chan(grad_proj), weight_cols),
        grad_weight.reshape(kinds, own, depth),
        grad_filter,
    )


def solution(mesh):
    placed = (
        P(("files", "ctx"), "chan"),
        P(None, "chan", None),
        P("chan", "ctx"),
        P("chan"),
        P("chan", ("files", "ctx")),
    )
    return jax.shard_map(
        per_device,
        mesh=mesh,
        in_specs=placed,
        out_specs=(
            P(("files", "ctx"), "chan"),
            P("files", "chan", None),
            P("chan", ("files", "ctx")),
        ),
        check_vma=False,
    )
```

time: 169 us -> 132 us (0.78)
  waiting for transfers between devices: 105 us -> 51.5 us
  Pallas kernels: 3.01 us -> 17.9 us
  local copies, waits for them, and re-layouts: 4.02 us -> 18.5 us
  matrix products: 12.7 us -> 0 us
  starting transfers between devices: 39.8 us -> 42.8 us
  other arithmetic: 2.21 us -> 0.03 us
    ppermute x12 -> x6, waiting for transfers between devices: 62.9 us -> 10.6 us  [ring(): lax.ppermute(found[-1], 'ctx', [(i, (i + step) % size) for i in range(siz...]
    pallas_call x0 -> x6, Pallas kernels: none -> 13.5 us  [the longest x3 5.42 us: project(): pl.pallas_call(body, out_shape=shape, in_specs=[VMEM] * (1 + len(sums) +...]
    unnamed x20 -> x41, local copies, waits for them, and re-layouts: 1.72 us -> 14.5 us
    dot_general x12 -> x0, matrix products: 12.7 us -> none  [the longest x4 5.84 us: per_device(): lax.dot_general(columns(weight_rows, m), features[m], (((1,), (1,)), ((),...]
    ppermute x12 -> x6, starting transfers between devices: 13.8 us -> 17.4 us  [ring(): lax.ppermute(found[-1], 'ctx', [(i, (i + step) % size) for i in range(siz...]
  transfers between devices with their start and end apart: 36 -> 30, of which waited for: 15 -> 12; matrix products, arithmetic and copies ran while one was open for 10% -> 6% of each run, Pallas kernels for 2% -> 12%
where the time goes in v1:
time: 132 us
  waiting for transfers between devices  51.5 us (39%)
  starting transfers between devices  42.8 us (32%)
  local copies, waits for them, and re-layouts  18.5 us (14%)
  Pallas kernels  17.9 us (14%)
    ppermute x24, waiting for transfers between devices, swap(): return lax.ppermute(values, axis, [(i, i ^ mask) for i in range(size)])  40.9 us
    ppermute x24, starting transfers between devices, swap(): return lax.ppermute(values, axis, [(i, i ^ mask) for i in range(size)])  25.4 us
    ppermute x6, starting transfers between devices, ring(): lax.ppermute(found[-1], 'ctx', [(i, (i + step) % size) for i in range(siz...  17.4 us
    unnamed x41, local copies, waits for them, and re-layouts  14.5 us
    ppermute x6, waiting for transfers between devices, ring(): lax.ppermute(found[-1], 'ctx', [(i, (i + step) % size) for i in range(siz...  10.6 us
    pallas_call x3, Pallas kernels, project(): pl.pallas_call(body, out_shape=shape, in_specs=[VMEM] * (1 + len(sums) +...  5.42 us
    pallas_call x1, Pallas kernels, convolve(): pl.pallas_call(functools.partial(conv_kernel, blocks, chans, group, token...  4.37 us
    pallas_call x1, Pallas kernels, weight_products(): pl.pallas_call(functools.partial(product_kernel, kinds, share, blocks, sl...  3.59 us
  transfers between devices with their start and end apart: 30, of which 12 were waited for; matrix products, arithmetic and copies ran while one was open for 6% of the time, Pallas kernels for 12%

profile of v1, /device:TPU:0, one launch (start us, length us, event | category | flops | bytes accessed | tf_op | source)
XLA Modules:
  0.0 131.6 jit_solution(12591446077830566087)
XLA Ops:
  1.2 2.6 %collective-permute-start = (bf16[512,1024]{1,0:T(8,128)(2,1)}, bf16[512,1024]{1,0:T(8,128)(2,1)}, u32[]{:S(2)}, u32[]{:S(2)}) collective-permute-start(bf16[512,1024]{1,0:T(8,128)(2,1)} %refs_0_.1), channel_id=1, source_target_pairs={{0,2},{1,3},{2,0},{3,1},{4,6},{5,7},{6,4},{7,5},{8,10},{9,11},{10,... | collective-permute-start | bytes 3145736 | tf_op jit(solution)/shard_map/ppermute | solution.py:373
  3.8 2.1 %constant_dynamic-slice_fusion.8 = (bf16[512,256]{1,0:T(8,128)(2,1)S(1)}, bf16[512,256]{1,0:T(8,128)(2,1)}, bf16[512,256]{1,0:T(8,128)(2,1)}, bf16[512,256]{1,0:T(8,128)(2,1)S(1)}) fusion(bf16[512,1024]{1,0:T(8,128)(2,1)} %refs_0_.1, s32[]{:T(128)S(6)} %select_n.43, s32[]{:T(128)S(6)} %select_n.42, s32[]{:T(128)S(6)} %select_n.41, s32[]{:T(128)S(6)} %select_n.40), kind=kLoop, calls=%fused_computation.13 | loop fusion | bytes 2097168 | tf_op jit(solution)/shard_map/dynamic_slice | solution.py:431
  7.4 2.6 %collective-permute-start.2 = (bf16[512,256]{1,0:T(8,128)(2,1)}, bf16[512,256]{1,0:T(8,128)(2,1)}, u32[]{:S(2)}, u32[]{:S(2)}) collective-permute-start(bf16[512,256]{1,0:T(8,128)(2,1)} %get-tuple-element.68), channel_id=1, source_target_pairs={{0,8},{4,12},{8,0},{12,4},{1,9},{5,13},{9,1},{13,5},{2,10},{6,14},... | collective-permute-start | bytes 786440 | tf_op jit(solution)/shard_map/ppermute | solution.py:373
  11.1 9.1 %collective-permute-done.1 = bf16[512,256]{1,0:T(8,128)(2,1)} collective-permute-done((bf16[512,256]{1,0:T(8,128)(2,1)}, bf16[512,256]{1,0:T(8,128)(2,1)}, u32[]{:S(2)}, u32[]{:S(2)}) %collective-permute-start.1) | collective-permute-done | bytes 262176 | tf_op jit(solution)/shard_map/ppermute | solution.py:373
  21.3 8.3 %collective-permute-done.2 = bf16[512,256]{1,0:T(8,128)(2,1)} collective-permute-done((bf16[512,256]{1,0:T(8,128)(2,1)}, bf16[512,256]{1,0:T(8,128)(2,1)}, u32[]{:S(2)}, u32[]{:S(2)}) %collective-permute-start.2) | collective-permute-done | bytes 262176 | tf_op jit(solution)/shard_map/ppermute | solution.py:373
  29.6 3.3 %collective-permute-start.7 = (f32[32,512]{1,0:T(8,128)S(1)}, f32[32,512]{1,0:T(8,128)S(1)}, u32[]{:S(2)}, u32[]{:S(2)}) collective-permute-start(f32[32,512]{1,0:T(8,128)S(1)} %get-tuple-element.36), channel_id=1, source_target_pairs={{0,12},{4,8},{8,4},{12,0},{1,13},{5,9},{9,5},{13,1},{2,14},{6,10},... | collective-permute-start | bytes 196616 | tf_op jit(solution)/shard_map/ppermute | solution.py:373
  33.0 5.4 %collective-permute-done.6.refs_3_ = f32[32,512]{1,0:T(8,128)S(1)} collective-permute-done((f32[32,512]{1,0:T(8,128)S(1)}, f32[32,512]{1,0:T(8,128)S(1)}, u32[]{:S(2)}, u32[]{:S(2)}) %collective-permute-start.6) | collective-permute-done | bytes 65568 | tf_op jit(solution)/shard_map/ppermute | solution.py:373
  39.1 1.7 %constant_dynamic-update-slice_fusion.2 = bf16[2048,256]{1,0:T(8,128)(2,1)} fusion(bf16[2048,256]{1,0:T(8,128)(2,1)} %constant_dynamic-update-slice_fusion.3, bf16[512,256]{1,0:T(8,128)(2,1)} %collective-permute-done.1), kind=kLoop, calls=%fused_computation.3 | loop fusion | bytes 524288
  40.8 1.7 %constant_dynamic-update-slice_fusion.1 = bf16[2048,256]{1,0:T(8,128)(2,1)} fusion(bf16[2048,256]{1,0:T(8,128)(2,1)} %constant_dynamic-update-slice_fusion.2, bf16[512,256]{1,0:T(8,128)(2,1)} %collective-permute-done.2), kind=kLoop, calls=%fused_computation.2 | loop fusion | bytes 524288
  42.5 1.7 %constant_dynamic-update-slice_fusion.refs_4_ = bf16[2048,256]{1,0:T(8,128)(2,1)} fusion(bf16[2048,256]{1,0:T(8,128)(2,1)} %constant_dynamic-update-slice_fusion.1, bf16[512,256]{1,0:T(8,128)(2,1)} %collective-permute-done.3), kind=kLoop, calls=%fused_computation.1 | loop fusion | bytes 524288 | tf_op jit(solution)/shard_map/concatenate | solution.py:451
  44.7 2.0 %project.3.sum_ref = f32[512,192]{1,0:T(8,128)S(1)} custom-call(bf16[192,4096]{1,0:T(8,128)(2,1)S(1)} %bitcast.15, bf16[512,1024]{1,0:T(8,128)(2,1)S(1)} %copy-done.2, bf16[512,1024]{1,0:T(8,128)(2,1)} %collective-permute-done.4.refs_1_), custom_call_target="tpu_custom_call" | custom-call | flops 402653184 | bytes 1048576 | tf_op jit(solution)/shard_map/project/pallas_call | solution.py:240
  47.0 1.7 %project.4.sum_ref = f32[512,192]{1,0:T(8,128)S(1)} custom-call(bf16[192,4096]{1,0:T(8,128)(2,1)S(1)} %bitcast.16, f32[512,192]{1,0:T(8,128)S(1)} %project.3.sum_ref, bf16[512,1024]{1,0:T(8,128)(2,1)} %collective-permute-done.refs_0_), custom_call_target="tpu_custom_call" | custom-call | flops 201326592 | bytes 1048576 | tf_op jit(solution)/shard_map/project/pallas_call | solution.py:240
  48.7 1.8 %project.5 = (bf16[48,512]{1,0:T(8,128)(2,1)S(1)}, bf16[48,512]{1,0:T(8,128)(2,1)S(1)}, bf16[48,512]{1,0:T(8,128)(2,1)S(1)}, bf16[48,512]{1,0:T(8,128)(2,1)S(1)}) custom-call(bf16[192,4096]{1,0:T(8,128)(2,1)S(1)} %bitcast.17, f32[512,192]{1,0:T(8,128)S(1)} %project.4.sum_ref, bf16[512,1024]{1,0:T(8,128)(2,1)} %collective-permute-done.8.refs_0_), custom_call_target="tpu_custom_call" | custom-call | flops 201326592 | bytes 1048576 | tf_op jit(solution)/shard_map/project/pallas_call | solution.py:240
  51.8 1.8 %collective-permute-start.10 = (bf16[48,512]{1,0:T(8,128)(2,1)S(1)}, bf16[48,512]{1,0:T(8,128)(2,1)S(1)}, u32[]{:S(2)}, u32[]{:S(2)}) collective-permute-start(bf16[48,512]{1,0:T(8,128)(2,1)S(1)} %get-tuple-element.44), channel_id=1, source_target_pairs={{0,8},{4,12},{8,0},{12,4},{1,9},{5,13},{9,1},{13,5},{2,10},{6,14},... | collective-permute-start | bytes 147464 | tf_op jit(solution)/shard_map/ppermute | solution.py:373
  55.7 2.1 %collective-permute-done.10.refs_7_ = bf16[48,512]{1,0:T(8,128)(2,1)S(1)} collective-permute-done((bf16[48,512]{1,0:T(8,128)(2,1)S(1)}, bf16[48,512]{1,0:T(8,128)(2,1)S(1)}, u32[]{:S(2)}, u32[]{:S(2)}) %collective-permute-start.10) | collective-permute-done | bytes 49184 | tf_op jit(solution)/shard_map/ppermute | solution.py:373
  68.1 4.4 %conv.1 = (bf16[48,2304]{1,0:T(8,128)(2,1)S(1)}, bf16[48,2304]{1,0:T(8,128)(2,1)S(1)}, bf16[48,2304]{1,0:T(8,128)(2,1)S(1)}, bf16[48,2304]{1,0:T(8,128)(2,1)S(1)}) custom-call(f32[16,1]{1,0:T(8,128)S(1)} %copy.15.refs_0_, f32[32,512]{1,0:T(8,128)S(1)} %get-tuple-element.37.refs_1_, f32[32,512]{1,0:T(8,128)S(1)} %collective-permute-done.5.refs_2_, ...), custom_call_target="tpu_custom_call" | custom-call | flops 962592768 | bytes 4194304 | tf_op jit(solution)/shard_map/conv/pallas_call | solution.py:180
  73.2 2.9 %collective-permute-start.13 = (bf16[48,2304]{1,0:T(8,128)(2,1)S(1)}, bf16[48,2304]{1,0:T(8,128)(2,1)S(1)}, u32[]{:S(2)}, u32[]{:S(2)}) collective-permute-start(bf16[48,2304]{1,0:T(8,128)(2,1)S(1)} %get-tuple-element.48), channel_id=1, source_target_pairs={{0,8},{4,12},{8,0},{12,4},{1,9},{5,13},{9,1},{13,5},{2,10},{6,14},... | collective-permute-start | bytes 663560 | tf_op jit(solution)/shard_map/ppermute | solution.py:373
  77.7 8.1 %collective-permute-done.12.refs_1_ = bf16[48,2304]{1,0:T(8,128)(2,1)S(1)} collective-permute-done((bf16[48,2304]{1,0:T(8,128)(2,1)}, bf16[48,2304]{1,0:T(8,128)(2,1)S(1)}, u32[]{:S(2)}, u32[]{:S(2)}) %collective-permute-start.12) | collective-permute-done | bytes 221216 | tf_op jit(solution)/shard_map/ppermute | solution.py:373
  87.1 4.8 %collective-permute-done.13.refs_2_ = bf16[48,2304]{1,0:T(8,128)(2,1)S(1)} collective-permute-done((bf16[48,2304]{1,0:T(8,128)(2,1)S(1)}, bf16[48,2304]{1,0:T(8,128)(2,1)S(1)}, u32[]{:S(2)}, u32[]{:S(2)}) %collective-permute-start.13) | collective-permute-done | bytes 221216 | tf_op jit(solution)/shard_map/ppermute | solution.py:373
  91.9 3.6 %products.1 = (bf16[96,1024]{1,0:T(8,128)(2,1)S(1)}, bf16[96,1024]{1,0:T(8,128)(2,1)S(1)}, bf16[192,512]{1,0:T(8,128)(2,1)S(1)}, f32[64,512]{1,0:T(8,128)}) custom-call(bf16[48,2304]{1,0:T(8,128)(2,1)S(1)} %get-tuple-element.46.refs_0_, bf16[48,2304]{1,0:T(8,128)(2,1)S(1)} %collective-permute-done.12.refs_1_, ...), custom_call_target="tpu_custom_call" | custom-call | flops 805306368 | bytes 6291456 | tf_op jit(solution)/shard_map/products/pallas_call | solution.py:290
  95.5 5.0 %collective-permute-start.24 = (bf16[96,1024]{1,0:T(8,128)(2,1)S(1)}, bf16[96,1024]{1,0:T(8,128)(2,1)S(1)}, u32[]{:S(2)}, u32[]{:S(2)}) collective-permute-start(bf16[96,1024]{1,0:T(8,128)(2,1)S(1)} %get-tuple-element.60.refs_0_), channel_id=1, source_target_pairs={{0,4},{4,8},{8,12},{12,0},{1,5},{5,9},{9,13},{13,1},{2,6},{6,10},{... | collective-permute-start | bytes 589832 | tf_op jit(solution)/shard_map/ppermute | solution.py:392
  102.2 3.5 %collective-permute-done.24.refs_1_ = bf16[96,1024]{1,0:T(8,128)(2,1)S(1)} collective-permute-done((bf16[96,1024]{1,0:T(8,128)(2,1)S(1)}, bf16[96,1024]{1,0:T(8,128)(2,1)S(1)}, u32[]{:S(2)}, u32[]{:S(2)}) %collective-permute-start.24) | collective-permute-done | bytes 196640 | tf_op jit(solution)/shard_map/ppermute | solution.py:392
  105.7 2.5 %collective-permute-start.25 = (bf16[96,1024]{1,0:T(8,128)(2,1)S(1)}, bf16[96,1024]{1,0:T(8,128)(2,1)S(1)}, u32[]{:S(2)}, u32[]{:S(2)}) collective-permute-start(bf16[96,1024]{1,0:T(8,128)(2,1)S(1)} %collective-permute-done.24.refs_1_), channel_id=1, source_target_pairs={{0,4},{4,8},{8,12},{12,0},{1,5},{5,9},{9,13},{13,1},{2,6},{6,10},{... | collective-permute-start | bytes 589832 | tf_op jit(solution)/shard_map/ppermute | solution.py:392
  108.2 1.8 %collective-permute-done.27.refs_5_ = bf16[96,1024]{1,0:T(8,128)(2,1)S(1)} collective-permute-done((bf16[96,1024]{1,0:T(8,128)(2,1)S(1)}, bf16[96,1024]{1,0:T(8,128)(2,1)S(1)}, u32[]{:S(2)}, u32[]{:S(2)}) %collective-permute-start.27) | collective-permute-done | bytes 196640 | tf_op jit(solution)/shard_map/ppermute | solution.py:392
  110.0 4.3 %collective-permute-start.28 = (bf16[96,1024]{1,0:T(8,128)(2,1)S(1)}, bf16[96,1024]{1,0:T(8,128)(2,1)S(1)}, u32[]{:S(2)}, u32[]{:S(2)}) collective-permute-start(bf16[96,1024]{1,0:T(8,128)(2,1)S(1)} %collective-permute-done.27.refs_5_), channel_id=1, source_target_pairs={{0,12},{4,0},{8,4},{12,8},{1,13},{5,1},{9,5},{13,9},{2,14},{6,2},{... | collective-permute-start | bytes 589832 | tf_op jit(solution)/shard_map/ppermute | solution.py:392
  114.3 1.8 %collective-permute-done.19.refs_2_ = bf16[192,512]{1,0:T(8,128)(2,1)S(1)} collective-permute-done((bf16[192,512]{1,0:T(8,128)(2,1)S(1)}, bf16[192,512]{1,0:T(8,128)(2,1)S(1)}, u32[]{:S(2)}, u32[]{:S(2)}) %collective-permute-start.19) | collective-permute-done | bytes 196640 | tf_op jit(solution)/shard_map/ppermute | solution.py:373
  116.1 2.0 %collective-permute-start.26 = (bf16[96,1024]{1,0:T(8,128)(2,1)S(1)}, bf16[96,1024]{1,0:T(8,128)(2,1)S(1)}, u32[]{:S(2)}, u32[]{:S(2)}) collective-permute-start(bf16[96,1024]{1,0:T(8,128)(2,1)S(1)} %collective-permute-done.25.refs_2_), channel_id=1, source_target_pairs={{0,4},{4,8},{8,12},{12,0},{1,5},{5,9},{9,13},{13,1},{2,6},{6,10},{... | collective-permute-start | bytes 589832 | tf_op jit(solution)/shard_map/ppermute | solution.py:392
  118.1 3.7 %collective-permute-start.29 = (bf16[96,1024]{1,0:T(8,128)(2,1)S(1)}, bf16[96,1024]{1,0:T(8,128)(2,1)S(1)}, u32[]{:S(2)}, u32[]{:S(2)}) collective-permute-start(bf16[96,1024]{1,0:T(8,128)(2,1)S(1)} %collective-permute-done.28.refs_6_), channel_id=1, source_target_pairs={{0,12},{4,0},{8,4},{12,8},{1,13},{5,1},{9,5},{13,9},{2,14},{6,2},{... | collective-permute-start | bytes 589832 | tf_op jit(solution)/shard_map/ppermute | solution.py:392
  121.8 2.3 %inputs.1 = bf16[512,1024]{1,0:T(8,128)(2,1)} custom-call(bf16[192,512]{1,0:T(8,128)(2,1)S(1)} %get-tuple-element.55.refs_0_, bf16[192,512]{1,0:T(8,128)(2,1)S(1)} %collective-permute-done.18.refs_1_, bf16[192,512]{1,0:T(8,128)(2,1)S(1)} %collective-permute-done.19.refs_2_, bf16[192,512]{1,0:T(8,128)(2,1)S(1)} %collective-permute-done.20.refs_3_, ...), custom_call_target="tpu_custom_call" | custom-call | flops 805306368 | bytes 4194304 | tf_op jit(solution)/shard_map/inputs/pallas_call | solution.py:321
  124.0 1.6 %collective-permute-done.26.refs_3_ = bf16[96,1024]{1,0:T(8,128)(2,1)S(1)} collective-permute-done((bf16[96,1024]{1,0:T(8,128)(2,1)S(1)}, bf16[96,1024]{1,0:T(8,128)(2,1)S(1)}, u32[]{:S(2)}, u32[]{:S(2)}) %collective-permute-start.26) | collective-permute-done | bytes 196640 | tf_op jit(solution)/shard_map/ppermute | solution.py:392
  125.6 3.7 %collective-permute-done.29.refs_7_ = bf16[96,1024]{1,0:T(8,128)(2,1)S(1)} collective-permute-done((bf16[96,1024]{1,0:T(8,128)(2,1)S(1)}, bf16[96,1024]{1,0:T(8,128)(2,1)S(1)}, u32[]{:S(2)}, u32[]{:S(2)}) %collective-permute-start.29) | collective-permute-done | bytes 196640 | tf_op jit(solution)/shard_map/ppermute | solution.py:392
  129.3 2.3 %place.1 = f32[192,4096]{1,0:T(8,128)} custom-call(bf16[96,1024]{1,0:T(8,128)(2,1)S(1)} %get-tuple-element.60.refs_0_, bf16[96,1024]{1,0:T(8,128)(2,1)S(1)} %collective-permute-done.24.refs_1_, bf16[96,1024]{1,0:T(8,128)(2,1)S(1)} %collective-permute-done.25.refs_2_, bf16[96,1024]{1,0:T(8,128)(2,1)S(1)} %collective-permute-done.26.refs_3_, ...), custom_call_target="tpu_custom_call" | custom-call | bytes 6291456 | tf_op jit(solution)/shard_map/place/pallas_call | solution.py:357
  (84 shorter events, 24.8 us)
Async XLA Ops:
  0.6 54.3 %copy-start = (f32[64]{0:T(128)S(1)}, f32[64]{0:T(128)}, u32[]{:S(2)}) copy-start(f32[64]{0:T(128)} %param.13) | copy-start | bytes 772
  0.7 9.7 %collective-permute-start.4 = (bf16[512,1024]{1,0:T(8,128)(2,1)}, bf16[512,1024]{1,0:T(8,128)(2,1)}, u32[]{:S(2)}, u32[]{:S(2)}) collective-permute-start(bf16[512,1024]{1,0:T(8,128)(2,1)} %refs_0_.1), channel_id=1, source_target_pairs={{0,1},{1,0},{2,3},{3,2},{4,5},{5,4},{6,7},{7,6},{8,9},{9,8},{10,11... | collective-permute-start | bytes 3145736 | tf_op jit(solution)/shard_map/ppermute | solution.py:373
  1.2 31.8 %collective-permute-start = (bf16[512,1024]{1,0:T(8,128)(2,1)}, bf16[512,1024]{1,0:T(8,128)(2,1)}, u32[]{:S(2)}, u32[]{:S(2)}) collective-permute-start(bf16[512,1024]{1,0:T(8,128)(2,1)} %refs_0_.1), channel_id=1, source_target_pairs={{0,2},{1,3},{2,0},{3,1},{4,6},{5,7},{6,4},{7,5},{8,10},{9,11},{10,... | collective-permute-start | bytes 3145736 | tf_op jit(solution)/shard_map/ppermute | solution.py:373
  5.8 14.4 %collective-permute-start.1 = (bf16[512,256]{1,0:T(8,128)(2,1)}, bf16[512,256]{1,0:T(8,128)(2,1)}, u32[]{:S(2)}, u32[]{:S(2)}) collective-permute-start(bf16[512,256]{1,0:T(8,128)(2,1)} %get-tuple-element.69), channel_id=1, source_target_pairs={{0,4},{4,0},{8,12},{12,8},{1,5},{5,1},{9,13},{13,9},{2,6},{6,2},{1... | collective-permute-start | bytes 786440 | tf_op jit(solution)/shard_map/ppermute | solution.py:373
  7.4 22.2 %collective-permute-start.2 = (bf16[512,256]{1,0:T(8,128)(2,1)}, bf16[512,256]{1,0:T(8,128)(2,1)}, u32[]{:S(2)}, u32[]{:S(2)}) collective-permute-start(bf16[512,256]{1,0:T(8,128)(2,1)} %get-tuple-element.68), channel_id=1, source_target_pairs={{0,8},{4,12},{8,0},{12,4},{1,9},{5,13},{9,1},{13,5},{2,10},{6,14},... | collective-permute-start | bytes 786440 | tf_op jit(solution)/shard_map/ppermute | solution.py:373
  10.0 23.0 %collective-permute-start.3 = (bf16[512,256]{1,0:T(8,128)(2,1)S(1)}, bf16[512,256]{1,0:T(8,128)(2,1)}, u32[]{:S(2)}, u32[]{:S(2)}) collective-permute-start(bf16[512,256]{1,0:T(8,128)(2,1)S(1)} %get-tuple-element.67), channel_id=1, source_target_pairs={{0,12},{4,8},{8,4},{12,0},{1,13},{5,9},{9,5},{13,1},{2,14},{6,10},... | collective-permute-start | bytes 786440 | tf_op jit(solution)/shard_map/ppermute | solution.py:373
  10.2 34.4 %copy-start.1 = (bf16[3,64,4096]{2,1,0:T(8,128)(2,1)S(1)}, bf16[3,64,4096]{2,1,0:T(8,128)(2,1)}, u32[]{:S(2)}) copy-start(bf16[3,64,4096]{2,1,0:T(8,128)(2,1)} %param.11) | copy-start | bytes 4718596
  10.3 22.6 %collective-permute-start.5 = (f32[32,512]{1,0:T(8,128)S(1)}, f32[32,512]{1,0:T(8,128)S(1)}, u32[]{:S(2)}, u32[]{:S(2)}) collective-permute-start(f32[32,512]{1,0:T(8,128)S(1)} %get-tuple-element.34), channel_id=1, source_target_pairs={{0,4},{4,0},{8,12},{12,8},{1,5},{5,1},{9,13},{13,9},{2,6},{6,2},{1... | collective-permute-start | bytes 196616 | tf_op jit(solution)/shard_map/ppermute | solution.py:373
  20.2 18.2 %collective-permute-start.6 = (f32[32,512]{1,0:T(8,128)S(1)}, f32[32,512]{1,0:T(8,128)S(1)}, u32[]{:S(2)}, u32[]{:S(2)}) collective-permute-start(f32[32,512]{1,0:T(8,128)S(1)} %get-tuple-element.35), channel_id=1, source_target_pairs={{0,8},{4,12},{8,0},{12,4},{1,9},{5,13},{9,1},{13,5},{2,10},{6,14},... | collective-permute-start | bytes 196616 | tf_op jit(solution)/shard_map/ppermute | solution.py:373
  29.6 8.8 %collective-permute-start.7 = (f32[32,512]{1,0:T(8,128)S(1)}, f32[32,512]{1,0:T(8,128)S(1)}, u32[]{:S(2)}, u32[]{:S(2)}) collective-permute-start(f32[32,512]{1,0:T(8,128)S(1)} %get-tuple-element.36), channel_id=1, source_target_pairs={{0,12},{4,8},{8,4},{12,0},{1,13},{5,9},{9,5},{13,1},{2,14},{6,10},... | collective-permute-start | bytes 196616 | tf_op jit(solution)/shard_map/ppermute | solution.py:373
  38.4 10.2 %collective-permute-start.8 = (bf16[512,1024]{1,0:T(8,128)(2,1)}, bf16[512,1024]{1,0:T(8,128)(2,1)}, u32[]{:S(2)}, u32[]{:S(2)}) collective-permute-start(bf16[512,1024]{1,0:T(8,128)(2,1)} %collective-permute-done.refs_0_), channel_id=1, source_target_pairs={{0,1},{1,0},{2,3},{3,2},{4,5},{5,4},{6,7},{7,6},{8,9},{9,8},{10,11... | collective-permute-start | bytes 3145736 | tf_op jit(solution)/shard_map/ppermute | solution.py:373
  44.1 29.0 %collective-permute-start.16 = (bf16[2048,256]{1,0:T(8,128)(2,1)}, bf16[2048,256]{1,0:T(8,128)(2,1)}, u32[]{:S(2)}, u32[]{:S(2)}) collective-permute-start(bf16[2048,256]{1,0:T(8,128)(2,1)} %constant_dynamic-update-slice_fusion.refs_4_), channel_id=1, source_target_pairs={{0,2},{1,3},{2,0},{3,1},{4,6},{5,7},{6,4},{7,5},{8,10},{9,11},{10,... | collective-permute-start | bytes 3145736 | tf_op jit(solution)/shard_map/ppermute | solution.py:373
  46.7 31.0 %collective-permute-start.15 = (bf16[2048,256]{1,0:T(8,128)(2,1)}, bf16[2048,256]{1,0:T(8,128)(2,1)S(1)}, u32[]{:S(2)}, u32[]{:S(2)}) collective-permute-start(bf16[2048,256]{1,0:T(8,128)(2,1)} %constant_dynamic-update-slice_fusion.refs_4_), channel_id=1, source_target_pairs={{0,1},{1,0},{2,3},{3,2},{4,5},{5,4},{6,7},{7,6},{8,9},{9,8},{10,11... | collective-permute-start | bytes 3145736 | tf_op jit(solution)/shard_map/ppermute | solution.py:373
  50.4 4.6 %collective-permute-start.9 = (bf16[48,512]{1,0:T(8,128)(2,1)S(1)}, bf16[48,512]{1,0:T(8,128)(2,1)S(1)}, u32[]{:S(2)}, u32[]{:S(2)}) collective-permute-start(bf16[48,512]{1,0:T(8,128)(2,1)S(1)} %get-tuple-element.43), channel_id=1, source_target_pairs={{0,4},{4,0},{8,12},{12,8},{1,5},{5,1},{9,13},{13,9},{2,6},{6,2},{1... | collective-permute-start | bytes 147464 | tf_op jit(solution)/shard_map/ppermute | solution.py:373
  51.8 6.1 %collective-permute-start.10 = (bf16[48,512]{1,0:T(8,128)(2,1)S(1)}, bf16[48,512]{1,0:T(8,128)(2,1)S(1)}, u32[]{:S(2)}, u32[]{:S(2)}) collective-permute-start(bf16[48,512]{1,0:T(8,128)(2,1)S(1)} %get-tuple-element.44), channel_id=1, source_target_pairs={{0,8},{4,12},{8,0},{12,4},{1,9},{5,13},{9,1},{13,5},{2,10},{6,14},... | collective-permute-start | bytes 147464 | tf_op jit(solution)/shard_map/ppermute | solution.py:373
  53.6 6.0 %collective-permute-start.11 = (bf16[48,512]{1,0:T(8,128)(2,1)S(1)}, bf16[48,512]{1,0:T(8,128)(2,1)S(1)}, u32[]{:S(2)}, u32[]{:S(2)}) collective-permute-start(bf16[48,512]{1,0:T(8,128)(2,1)S(1)} %get-tuple-element.45), channel_id=1, source_target_pairs={{0,12},{4,8},{8,4},{12,0},{1,13},{5,9},{9,5},{13,1},{2,14},{6,10},... | collective-permute-start | bytes 147464 | tf_op jit(solution)/shard_map/ppermute | solution.py:373
  73.1 18.7 %collective-permute-start.17 = (bf16[2048,256]{1,0:T(8,128)(2,1)}, bf16[2048,256]{1,0:T(8,128)(2,1)}, u32[]{:S(2)}, u32[]{:S(2)}) collective-permute-start(bf16[2048,256]{1,0:T(8,128)(2,1)} %collective-permute-done.16.refs_6_), channel_id=1, source_target_pairs={{0,1},{1,0},{2,3},{3,2},{4,5},{5,4},{6,7},{7,6},{8,9},{9,8},{10,11... | collective-permute-start | bytes 3145736 | tf_op jit(solution)/shard_map/ppermute | solution.py:373
  73.1 12.7 %collective-permute-start.12 = (bf16[48,2304]{1,0:T(8,128)(2,1)}, bf16[48,2304]{1,0:T(8,128)(2,1)S(1)}, u32[]{:S(2)}, u32[]{:S(2)}) collective-permute-start(bf16[48,2304]{1,0:T(8,128)(2,1)} %copy-done.3), channel_id=1, source_target_pairs={{0,4},{4,0},{8,12},{12,8},{1,5},{5,1},{9,13},{13,9},{2,6},{6,2},{1... | collective-permute-start | bytes 663560 | tf_op jit(solution)/shard_map/ppermute | solution.py:373
  73.2 18.7 %collective-permute-start.13 = (bf16[48,2304]{1,0:T(8,128)(2,1)S(1)}, bf16[48,2304]{1,0:T(8,128)(2,1)S(1)}, u32[]{:S(2)}, u32[]{:S(2)}) collective-permute-start(bf16[48,2304]{1,0:T(8,128)(2,1)S(1)} %get-tuple-element.48), channel_id=1, source_target_pairs={{0,8},{4,12},{8,0},{12,4},{1,9},{5,13},{9,1},{13,5},{2,10},{6,14},... | collective-permute-start | bytes 663560 | tf_op jit(solution)/shard_map/ppermute | solution.py:373
  76.1 15.7 %collective-permute-start.14 = (bf16[48,2304]{1,0:T(8,128)(2,1)S(1)}, bf16[48,2304]{1,0:T(8,128)(2,1)S(1)}, u32[]{:S(2)}, u32[]{:S(2)}) collective-permute-start(bf16[48,2304]{1,0:T(8,128)(2,1)S(1)} %get-tuple-element.49), channel_id=1, source_target_pairs={{0,12},{4,8},{8,4},{12,0},{1,13},{5,9},{9,5},{13,1},{2,14},{6,10},... | collective-permute-start | bytes 663560 | tf_op jit(solution)/shard_map/ppermute | solution.py:373
  77.7 23.2 %collective-permute-start.21 = (bf16[192,1024]{1,0:T(8,128)(2,1)S(1)}, bf16[192,1024]{1,0:T(8,128)(2,1)S(1)}, u32[]{:S(2)}, u32[]{:S(2)}) collective-permute-start(bf16[192,1024]{1,0:T(8,128)(2,1)S(1)} %get-tuple-element.57), channel_id=1, source_target_pairs={{0,1},{1,0},{2,3},{3,2},{4,5},{5,4},{6,7},{7,6},{8,9},{9,8},{10,11... | collective-permute-start | bytes 1179656 | tf_op jit(solution)/shard_map/ppermute | solution.py:373
  85.9 28.4 %collective-permute-start.22 = (bf16[192,1024]{1,0:T(8,128)(2,1)S(1)}, bf16[192,1024]{1,0:T(8,128)(2,1)S(1)}, u32[]{:S(2)}, u32[]{:S(2)}) collective-permute-start(bf16[192,1024]{1,0:T(8,128)(2,1)S(1)} %get-tuple-element.58), channel_id=1, source_target_pairs={{0,2},{1,3},{2,0},{3,1},{4,6},{5,7},{6,4},{7,5},{8,10},{9,11},{10,... | collective-permute-start | bytes 1179656 | tf_op jit(solution)/shard_map/ppermute | solution.py:373
  95.5 10.3 %collective-permute-start.24 = (bf16[96,1024]{1,0:T(8,128)(2,1)S(1)}, bf16[96,1024]{1,0:T(8,128)(2,1)S(1)}, u32[]{:S(2)}, u32[]{:S(2)}) collective-permute-start(bf16[96,1024]{1,0:T(8,128)(2,1)S(1)} %get-tuple-element.60.refs_0_), channel_id=1, source_target_pairs={{0,4},{4,8},{8,12},{12,0},{1,5},{5,9},{9,13},{13,1},{2,6},{6,10},{... | collective-permute-start | bytes 589832 | tf_op jit(solution)/shard_map/ppermute | solution.py:392
  100.4 9.6 %collective-permute-start.27 = (bf16[96,1024]{1,0:T(8,128)(2,1)S(1)}, bf16[96,1024]{1,0:T(8,128)(2,1)S(1)}, u32[]{:S(2)}, u32[]{:S(2)}) collective-permute-start(bf16[96,1024]{1,0:T(8,128)(2,1)S(1)} %get-tuple-element.61.refs_4_), channel_id=1, source_target_pairs={{0,12},{4,0},{8,4},{12,8},{1,13},{5,1},{9,5},{13,9},{2,14},{6,2},{... | collective-permute-start | bytes 589832 | tf_op jit(solution)/shard_map/ppermute | solution.py:392
  100.4 21.3 %collective-permute-start.23 = (bf16[192,1024]{1,0:T(8,128)(2,1)S(1)}, bf16[192,1024]{1,0:T(8,128)(2,1)S(1)}, u32[]{:S(2)}, u32[]{:S(2)}) collective-permute-start(bf16[192,1024]{1,0:T(8,128)(2,1)S(1)} %get-tuple-element.59), channel_id=1, source_target_pairs={{0,3},{1,2},{2,1},{3,0},{4,7},{5,6},{6,5},{7,4},{8,11},{9,10},{10,... | collective-permute-start | bytes 1179656 | tf_op jit(solution)/shard_map/ppermute | solution.py:373
  100.9 15.2 %collective-permute-start.19 = (bf16[192,512]{1,0:T(8,128)(2,1)S(1)}, bf16[192,512]{1,0:T(8,128)(2,1)S(1)}, u32[]{:S(2)}, u32[]{:S(2)}) collective-permute-start(bf16[192,512]{1,0:T(8,128)(2,1)S(1)} %get-tuple-element.55.refs_0_), channel_id=1, source_target_pairs={{0,2},{1,3},{2,0},{3,1},{4,6},{5,7},{6,4},{7,5},{8,10},{9,11},{10,... | collective-permute-start | bytes 589832 | tf_op jit(solution)/shard_map/ppermute | solution.py:373
  105.7 10.3 %collective-permute-start.25 = (bf16[96,1024]{1,0:T(8,128)(2,1)S(1)}, bf16[96,1024]{1,0:T(8,128)(2,1)S(1)}, u32[]{:S(2)}, u32[]{:S(2)}) collective-permute-start(bf16[96,1024]{1,0:T(8,128)(2,1)S(1)} %collective-permute-done.24.refs_1_), channel_id=1, source_target_pairs={{0,4},{4,8},{8,12},{12,0},{1,5},{5,9},{9,13},{13,1},{2,6},{6,10},{... | collective-permute-start | bytes 589832 | tf_op jit(solution)/shard_map/ppermute | solution.py:392
  110.0 8.1 %collective-permute-start.28 = (bf16[96,1024]{1,0:T(8,128)(2,1)S(1)}, bf16[96,1024]{1,0:T(8,128)(2,1)S(1)}, u32[]{:S(2)}, u32[]{:S(2)}) collective-permute-start(bf16[96,1024]{1,0:T(8,128)(2,1)S(1)} %collective-permute-done.27.refs_5_), channel_id=1, source_target_pairs={{0,12},{4,0},{8,4},{12,8},{1,13},{5,1},{9,5},{13,9},{2,14},{6,2},{... | collective-permute-start | bytes 589832 | tf_op jit(solution)/shard_map/ppermute | solution.py:392
  114.3 7.5 %collective-permute-start.18 = (bf16[192,512]{1,0:T(8,128)(2,1)S(1)}, bf16[192,512]{1,0:T(8,128)(2,1)S(1)}, u32[]{:S(2)}, u32[]{:S(2)}) collective-permute-start(bf16[192,512]{1,0:T(8,128)(2,1)S(1)} %get-tuple-element.55.refs_0_), channel_id=1, source_target_pairs={{0,1},{1,0},{2,3},{3,2},{4,5},{5,4},{6,7},{7,6},{8,9},{9,8},{10,11... | collective-permute-start | bytes 589832 | tf_op jit(solution)/shard_map/ppermute | solution.py:373
  116.0 5.7 %collective-permute-start.20 = (bf16[192,512]{1,0:T(8,128)(2,1)S(1)}, bf16[192,512]{1,0:T(8,128)(2,1)S(1)}, u32[]{:S(2)}, u32[]{:S(2)}) collective-permute-start(bf16[192,512]{1,0:T(8,128)(2,1)S(1)} %collective-permute-done.19.refs_2_), channel_id=1, source_target_pairs={{0,1},{1,0},{2,3},{3,2},{4,5},{5,4},{6,7},{7,6},{8,9},{9,8},{10,11... | collective-permute-start | bytes 589832 | tf_op jit(solution)/shard_map/ppermute | solution.py:373
  116.1 9.6 %collective-permute-start.26 = (bf16[96,1024]{1,0:T(8,128)(2,1)S(1)}, bf16[96,1024]{1,0:T(8,128)(2,1)S(1)}, u32[]{:S(2)}, u32[]{:S(2)}) collective-permute-start(bf16[96,1024]{1,0:T(8,128)(2,1)S(1)} %collective-permute-done.25.refs_2_), channel_id=1, source_target_pairs={{0,4},{4,8},{8,12},{12,0},{1,5},{5,9},{9,13},{13,1},{2,6},{6,10},{... | collective-permute-start | bytes 589832 | tf_op jit(solution)/shard_map/ppermute | solution.py:392
  118.1 11.3 %collective-permute-start.29 = (bf16[96,1024]{1,0:T(8,128)(2,1)S(1)}, bf16[96,1024]{1,0:T(8,128)(2,1)S(1)}, u32[]{:S(2)}, u32[]{:S(2)}) collective-permute-start(bf16[96,1024]{1,0:T(8,128)(2,1)S(1)} %collective-permute-done.28.refs_6_), channel_id=1, source_target_pairs={{0,12},{4,0},{8,4},{12,8},{1,13},{5,1},{9,5},{13,9},{2,14},{6,2},{... | collective-permute-start | bytes 589832 | tf_op jit(solution)/shard_map/ppermute | solution.py:392
  (17 other events, 72.2 us)

commit v2 on v1

--- a/solution.py
+++ b/solution.py
@@ -14,7 +14,7 @@
 F32 = jnp.float32
 VMEM = pl.BlockSpec(memory_space=pltpu.VMEM)
 ANY = pl.BlockSpec(memory_space=pl.ANY)
-HBM = pl.BlockSpec(memory_space=pltpu.HBM)
+VMEM_BYTES = 16 * 2**20
 
 
 def split_table(table):
@@ -78,7 +78,7 @@
 
 
 def conv_kernel(blocks, chans, group, factor, *refs):
-    count = 2 * blocks + 5
+    count = blocks + 5
     gain_ref, sources, refs = refs[0], refs[1 : 1 + count], refs[1 + count :]
     out_refs = refs[:blocks]
     series, results, inputs = refs[blocks : 3 + blocks]
@@ -87,24 +87,23 @@
     copies = [pltpu.make_async_copy(sources[i], held[i], sems.at[i]) for i in range(count)]
     for copy in copies:
         copy.start()
-    ready_refs, signal_refs = held[:blocks], held[blocks : 2 * blocks]
-    fwd_ref, second_ref, back_ref, inv_ref, twiddle_ref = held[2 * blocks :]
+    signal_refs = held[:blocks]
+    fwd_ref, second_ref, back_ref, inv_ref, twiddle_ref = held[blocks:]
     place = lax.axis_index("ctx")
     length = series.shape[-1]
     cuts = length // LANES
     for m in range(blocks):
         where = place ^ m
         copies[m].wait()
-        copies[blocks + m].wait()
         values = signal_refs[m][...].astype(F32)
-        upstream = ready_refs[m][:chans, :]
+        upstream = values[3 * chans : 4 * chans]
         inputs[0, where] = values[:chans]
-        inputs[1, where] = values[2 * chans :]
+        inputs[1, where] = values[2 * chans : 3 * chans]
         inputs[2, where] = upstream
-        series[0, where] = ready_refs[m][chans:, :] * factor
-        series[1, where] = values[:chans] * values[2 * chans :]
+        series[0, where] = values[4 * chans :] * factor
+        series[1, where] = values[:chans] * values[2 * chans : 3 * chans]
         series[2, where] = upstream * values[chans : 2 * chans]
-    for copy in copies[2 * blocks :]:
+    for copy in copies[blocks:]:
         copy.wait()
     part = twiddle_ref.shape[1]
     cos, sin = twiddle_ref[0], twiddle_ref[1]
@@ -161,31 +160,34 @@
         ).astype(BF16)
         for ref in out_refs:
             ref[:, z * length : (z + 1) * length] = grads
+    found = [(factor * results[2, place ^ m]).astype(BF16).astype(F32) for m in range(blocks)]
+    cut = 3 * length // 4
+    rest = jnp.zeros((chans, length - cut), F32)
     for m in range(blocks):
-        found = factor * results[2, place ^ m]
-        half = length // 2
-        rows = jnp.concatenate([found[:, :half], found[:, half:], jnp.zeros((chans, half), F32)], axis=0)
+        pair = found[m], found[min(m ^ 1, blocks - 1)]
+        last = jnp.concatenate([pair[0][:, cut:], pair[1][:, cut:], rest], axis=1)
+        rows = jnp.concatenate([pair[0][:, :cut], pair[1][:, :cut], last], axis=0)
         out_refs[m][:, blocks * length :] = rows.astype(BF16)
 
 
-def convolve(signals, ready, gain):
-    blocks = len(ready)
-    chans, length = ready[0].shape[0] // 2, ready[0].shape[1]
+def convolve(signals, gain):
+    blocks = len(signals)
+    chans, length = signals[0].shape[0] // 5, signals[0].shape[1]
     tokens = blocks * length
     group = max(1, min(chans, 8, LANES * LANES // tokens))
     tables = fourier_tables(tokens, group)
-    arrays = [*ready, *signals, *[jnp.asarray(table) for table in tables]]
+    arrays = [*signals, *[jnp.asarray(table) for table in tables]]
     part = tables[4].shape[1]
     flops = 2 * 3 * (chans // group) * 3 * (4 * part * group * (tokens // LANES) * LANES + 2 * part * 256 * 256)
     return pl.pallas_call(
         functools.partial(conv_kernel, blocks, chans, group, tokens ** (-0.5)),
-        out_shape=[jax.ShapeDtypeStruct((3 * chans, tokens + length // 2), BF16)] * blocks,
-        in_specs=[VMEM] + [HBM] * len(arrays),
+        out_shape=[jax.ShapeDtypeStruct((3 * chans, tokens + 3 * length // 4), BF16)] * blocks,
+        in_specs=[VMEM] + [ANY] * len(arrays),
         out_specs=[VMEM] * blocks,
         scratch_shapes=[pltpu.VMEM((3, blocks, chans, length), F32)] * 3
         + [pltpu.VMEM(array.shape, array.dtype) for array in arrays]
         + [pltpu.SemaphoreType.DMA((len(arrays),))],
-        compiler_params=pltpu.CompilerParams(vmem_limit_bytes=40 * 2**20),
+        compiler_params=pltpu.CompilerParams(vmem_limit_bytes=60 * 2**20),
         cost_estimate=pl.CostEstimate(flops=flops, bytes_accessed=4 * 2**20, transcendentals=0),
         name="conv",
     )(gain, *arrays)
@@ -211,7 +213,7 @@
     refs[-1][...] = sum_ref[...] + partial_rows(weight_ref, refs[:-1], masks)
 
 
-def finish_kernel(masks, blocks, kinds, share, weight_ref, sum_ref, *refs):
+def finish_kernel(masks, blocks, kinds, share, given_ref, filter_ref, weight_ref, sum_ref, *refs):
     out_refs = refs[len(masks) : len(masks) + blocks]
     total = refs[-1]
     place = lax.axis_index("ctx")
@@ -219,91 +221,130 @@
     for m in range(blocks):
         first = (place ^ m) * share
         rows = [total[pl.ds(pl.multiple_of(k * share * blocks + first, share), share), :] for k in range(kinds)]
+        for ref in (given_ref, filter_ref):
+            rows.append(ref[pl.ds(pl.multiple_of(first, share), share), :])
         out_refs[m][...] = jnp.concatenate(rows, axis=0).astype(BF16)
 
 
-def project(weight_rows, features, groups, blocks, kinds):
+def project(weight_rows, sums, features, masks, out=None):
     rows, depth = weight_rows.shape
-    length = features[0].shape[0]
-    share = rows // kinds // blocks
-    sums = []
-    for i, masks in enumerate(groups):
-        last = i == len(groups) - 1
-        if last:
-            body = functools.partial(finish_kernel, masks, blocks, kinds, share)
-            shape = [jax.ShapeDtypeStruct((kinds * share, length), BF16)] * blocks
-        else:
-            body = functools.partial(more_kernel if i else start_kernel, masks)
-            shape = [jax.ShapeDtypeStruct((length, rows), F32)]
-        picked = [features[m] for m in masks]
-        flops = 2 * rows * length * depth * len(masks) // len(features)
-        sums = pl.pallas_call(
-            body,
-            out_shape=shape,
-            in_specs=[VMEM] * (1 + len(sums) + len(picked)),
-            out_specs=[VMEM] * len(shape),
-            scratch_shapes=[pltpu.VMEM((rows, length), F32)] if last else [],
-            compiler_params=pltpu.CompilerParams(vmem_limit_bytes=40 * 2**20),
-            cost_estimate=pl.CostEstimate(flops=flops, bytes_accessed=2**20, transcendentals=0),
-            name="project",
-        )(weight_rows, *sums, *picked)
-    return sums
+    length, width = features[0].shape
+    along = []
+    if out is None:
+        body = functools.partial(more_kernel if sums else start_kernel, masks)
+        shape = [jax.ShapeDtypeStruct((length, rows), F32)]
+    else:
+        blocks, kinds, along = out
+        share = rows // kinds // blocks
+        body = functools.partial(finish_kernel, masks, blocks, kinds, share)
+        shape = [jax.ShapeDtypeStruct(((kinds + 2) * share, length), BF16)] * blocks
+    flops = 2 * rows * length * width * len(masks)
+    return pl.pallas_call(
+        body,
+        out_shape=shape,
+        in_specs=[VMEM] * (len(along) + 1 + len(sums) + len(features)),
+        out_specs=[VMEM] * len(shape),
+        scratch_shapes=[pltpu.VMEM((rows, length), F32)] if out else [],
+        compiler_params=pltpu.CompilerParams(vmem_limit_bytes=VMEM_BYTES),
+        cost_estimate=pl.CostEstimate(flops=flops, bytes_accessed=2**20, transcendentals=0),
+        name="project",
+    )(*along, weight_rows, *sums, *features)
 
 
 def product_kernel(kinds, share, blocks, slabs, *refs):
-    grad_refs = refs[:blocks]
-    sources = refs[blocks : blocks + slabs]
-    first_ref, second_ref, own_ref, filter_ref = refs[blocks + slabs : blocks + slabs + 4]
-    turned, sems = refs[blocks + slabs + 4 :]
+    grad_refs, turned = refs[: blocks + 1], refs[blocks + 1 : blocks + 1 + slabs]
+    left_ref, some_ref, own_ref, filter_ref = refs[blocks + 1 + slabs :]
     place = lax.axis_index("ctx")
     length = own_ref.shape[1]
-    width = sources[0].shape[1]
-    copies = [pltpu.make_async_copy(sources[i], turned.at[i], sems.at[i]) for i in range(slabs)]
-    for copy in copies:
-        copy.start()
+    width = turned[0].shape[1]
+    rows = kinds * share
+    tokens = blocks * length
     mine = pl.ds(pl.multiple_of(place * length, length), length)
+    middle = (place == 1) | (place == 2)
     for m in range(blocks):
+        value = grad_refs[m][:, :tokens]
+        if m == blocks - 1:
+            value = value + grad_refs[blocks][:, :tokens]
+        left_ref[m * rows : (m + 1) * rows, :] = value
         for k in range(kinds):
             to = pl.multiple_of(k * share * blocks + (place ^ m) * share, share)
-            own_ref[pl.ds(to, share), :] = grad_refs[m][k * share : (k + 1) * share, mine]
+            own_ref[pl.ds(to, share), :] = left_ref[m * rows + k * share : m * rows + (k + 1) * share, mine]
+        end = grad_refs[m][:, tokens:].astype(F32)
+        cut = end.shape[1]
+        size = length - cut
+        given = jnp.concatenate([end[:share], end[2 * share :, :size]], axis=1)
+        if m == blocks - 1:
+            end = grad_refs[blocks][:, tokens:].astype(F32)
+            handed = jnp.concatenate([end[share : 2 * share], end[2 * share :, size : 2 * size]], axis=1)
+            given = jnp.where(middle, given, handed)
         to = pl.multiple_of((place ^ m) * share, share)
-        end = grad_refs[m][:, blocks * length :].astype(F32)
-        filter_ref[pl.ds(to, share), :] = jnp.concatenate([end[:share], end[share : 2 * share]], axis=1)
-    left = []
-    for b in range(blocks):
-        columns = pl.ds(pl.multiple_of((place ^ b) * length, length), length)
-        left.append(jnp.concatenate([ref[:, columns] for ref in grad_refs], axis=0))
-    left = jnp.concatenate(left, axis=1)
-    half = left.shape[0] // 2
+        filter_ref[pl.ds(to, share), :] = given
     for i in range(slabs):
-        copies[i].wait()
-        value = mm(left, turned[i]).astype(BF16)
-        first_ref[:, i * width : (i + 1) * width] = value[:half]
-        second_ref[:, i * width : (i + 1) * width] = value[half:]
+        some_ref[:, i * width : (i + 1) * width] = mm(left_ref[...], turned[i][...]).astype(BF16)
+
+
+def last_kernel(left_ref, some_ref, turned_ref, first_ref, second_ref):
+    half, known = first_ref.shape[0], some_ref.shape[1]
+    value = mm(left_ref[...], turned_ref[...]).astype(BF16)
+    for i, ref in enumerate((first_ref, second_ref)):
+        ref[:, :known] = some_ref[i * half : (i + 1) * half, :]
+        ref[:, known:] = value[i * half : (i + 1) * half]
 
 
 def weight_products(grads, turned, kinds, share):
-    blocks, slabs = len(grads), len(turned)
+    blocks, slabs = len(grads) - 1, len(turned)
     tokens, width = turned[0].shape
-    rows = kinds * share
-    half = jax.ShapeDtypeStruct((rows * blocks // 2, width * slabs), BF16)
-    return pl.pallas_call(
+    rows = kinds * share * blocks
+    cost = dict(flops=2 * rows * tokens * width * slabs, bytes_accessed=4 * 2**20, transcendentals=0)
+    left, some, own, filters = pl.pallas_call(
         functools.partial(product_kernel, kinds, share, blocks, slabs),
         out_shape=[
-            half,
-            half,
-            jax.ShapeDtypeStruct((rows * blocks, tokens // blocks), BF16),
+            jax.ShapeDtypeStruct((rows, tokens), BF16),
+            jax.ShapeDtypeStruct((rows, width * slabs), BF16),
+            jax.ShapeDtypeStruct((rows, tokens // blocks), BF16),
             jax.ShapeDtypeStruct((share * blocks, tokens // blocks), F32),
         ],
-        in_specs=[VMEM] * blocks + [ANY] * slabs,
+        in_specs=[VMEM] * (blocks + 1 + slabs),
         out_specs=[VMEM] * 4,
-        scratch_shapes=[pltpu.VMEM((slabs, tokens, width), BF16), pltpu.SemaphoreType.DMA((slabs,))],
-        compiler_params=pltpu.CompilerParams(vmem_limit_bytes=40 * 2**20),
-        cost_estimate=pl.CostEstimate(
-            flops=2 * rows * blocks * tokens * width * slabs, bytes_accessed=6 * 2**20, transcendentals=0
-        ),
+        compiler_params=pltpu.CompilerParams(vmem_limit_bytes=VMEM_BYTES),
+        cost_estimate=pl.CostEstimate(**cost),
         name="products",
     )(*grads, *turned)
+    return left, some, own, filters
+
+
+def last_products(left, some, turned):
+    rows, known = some.shape
+    tokens, width = turned.shape
+    half = jax.ShapeDtypeStruct((rows // 2, known + width), BF16)
+    return pl.pallas_call(
+        last_kernel,
+        out_shape=[half, half],
+        in_specs=[VMEM] * 3,
+        out_specs=[VMEM] * 2,
+        compiler_params=pltpu.CompilerParams(vmem_limit_bytes=VMEM_BYTES),
+        cost_estimate=pl.CostEstimate(flops=2 * rows * tokens * width, bytes_accessed=2**20, transcendentals=0),
+        name="products",
+    )(left, some, turned)
+
+
+def piece_kernel(values_ref, out_ref):
+    width = out_ref.shape[2]
+    for i in range(out_ref.shape[0]):
+        out_ref[i] = values_ref[:, i * width : (i + 1) * width]
+
+
+def column_pieces(values, blocks):
+    rows, width = values.shape
+    return pl.pallas_call(
+        piece_kernel,
+        out_shape=jax.ShapeDtypeStruct((blocks, rows, width // blocks), values.dtype),
+        in_specs=[VMEM],
+        out_specs=VMEM,
+        compiler_params=pltpu.CompilerParams(vmem_limit_bytes=VMEM_BYTES),
+        cost_estimate=pl.CostEstimate(flops=0, bytes_accessed=2**21, transcendentals=0),
+        name="pieces",
+    )(values)
 
 
 def input_kernel(count, *refs):
@@ -323,7 +364,7 @@
         out_shape=jax.ShapeDtypeStruct((length, width), BF16),
         in_specs=[VMEM] * (2 * len(grads)),
         out_specs=VMEM,
-        compiler_params=pltpu.CompilerParams(vmem_limit_bytes=40 * 2**20),
+        compiler_params=pltpu.CompilerParams(vmem_limit_bytes=VMEM_BYTES),
         cost_estimate=pl.CostEstimate(
             flops=2 * rows * len(grads) * length * width, bytes_accessed=4 * 2**20, transcendentals=0
         ),
@@ -360,7 +401,7 @@
         grid=(slabs,),
         in_specs=[pl.BlockSpec(flat[0].shape, lambda i: (0, 0))] * len(flat),
         out_specs=pl.BlockSpec((rows, depth), lambda i: (0, i)),
-        compiler_params=pltpu.CompilerParams(vmem_limit_bytes=40 * 2**20),
+        compiler_params=pltpu.CompilerParams(vmem_limit_bytes=VMEM_BYTES),
         cost_estimate=pl.CostEstimate(flops=0, bytes_accessed=6 * 2**20, transcendentals=0),
         name="place",
     )(*flat)
@@ -403,8 +444,8 @@
         piece = lax.dynamic_slice_in_dim(message, (place ^ m) * length, length, 1)
         piece = swap(piece, "ctx", m).reshape(kinds, share, length)
         grad_proj = lax.dynamic_update_slice_in_dim(grad_proj, piece, (place ^ m) * share, 1)
-        end = swap(message[: 2 * share, blocks * length :], "ctx", m).astype(F32)
-        end = jnp.concatenate([end[:share], end[share:]], axis=1)
+        end = swap(message[:, blocks * length :], "ctx", m).astype(F32)
+        end = jnp.concatenate([end[:share], end[2 * share :, : length // 4]], axis=1)
         grad_filter = lax.dynamic_update_slice_in_dim(grad_filter, end, (place ^ m) * share, 0)
     grad_proj = grad_proj.reshape(rows, length)
     grad_weight = jnp.zeros((rows, width * len(features)), F32)
@@ -432,46 +473,51 @@
 
     if line:
         features = [activations, swap(activations, "chan", 1), swap(activations, "chan", 2)]
-        quarter = width // blocks
-        turned = [swap(share_of(activations, m, 1, quarter), "ctx", m) for m in range(blocks)]
     else:
         features = [swap(activations, "chan", m) for m in range(slabs)]
 
-    ready = jnp.stack([out_grad.astype(F32), long_filter], axis=1).reshape(blocks, share, 2, length)
-    ready = jnp.swapaxes(ready, 1, 2).reshape(blocks * 2 * share, length)
-    ready = [share_of(ready, m, 0, 2 * share) for m in range(blocks)]
-    ready = after(ready, features[1])
-    ready = [swap(piece, "ctx", m) for m, piece in enumerate(ready)]
+    along = [out_grad.astype(F32), long_filter]
     gain = share_of(skip_gain, 0)[:, None]
 
-    groups = [[0, 1], [2], [3]] if line else [[0], list(range(1, slabs))]
     if line:
-        features[2], turned, ready = lax.optimization_barrier((features[2], turned, ready))
+        turned = after(column_pieces(activations, blocks), features[1])
+        turned = lax.all_to_all(turned, "ctx", split_axis=0, concat_axis=0).reshape(length * blocks, width // blocks)
+        sums = project(weight_rows, [], features[:2], [0, 1])
+        features[2], sums, along = lax.optimization_barrier((features[2], sums, along))
         features.append(swap(features[2], "chan", 1))
-        turned = jnp.concatenate(turned, axis=0)
-        far = swap(turned, "chan", 2)
-        turned = [turned, swap(turned, "chan", 1), far]
-
-    pieces = project(weight_rows, features, groups, blocks, kinds)
+        sums = project(weight_rows, sums, features[2:3], [2])
+        pieces = project(weight_rows, sums, features[3:], [3], (blocks, kinds, along))
+    else:
+        sums = project(weight_rows, [], features[:1], [0])
+        pieces = project(weight_rows, sums, features[1:], list(range(1, slabs)), (blocks, kinds, along))
     signals = [swap(piece, "ctx", m) for m, piece in enumerate(pieces)]
-    messages = convolve(signals, ready, gain)
     if line:
-        turned.append(swap(after(far, messages[0]), "chan", 1))
-
+        signals, turned = lax.optimization_barrier((signals, turned))
+        turned = [turned, swap(turned, "chan", 1), swap(turned, "chan", 2)]
+    messages = convolve(signals, gain)
     weight_cols = [lax.dynamic_slice_in_dim(weight_rows, (mine ^ m) * width, width, 1) for m in range(slabs)]
     weight_cols = after(weight_cols, turned[2] if line else signals[-1])
     weight_cols = [swap(cols, "chan", m) for m, cols in enumerate(weight_cols)]
 
     if line:
-        messages = [swap(message, "ctx", m) for m, message in enumerate(messages)]
-        first, second, grad_proj, grad_filter = weight_products(messages, turned, kinds, share)
+        messages = [messages[0], swap(messages[1], "ctx", 1), swap(messages[2], "ctx", 2), messages[3]]
+        messages[3] = lax.ppermute(messages[3], "ctx", [(1, 2), (2, 1)])
+        messages.append(lax.ppermute(messages[2], "ctx", [(1, 0), (2, 3)]))
+        far, messages = lax.optimization_barrier((turned[2], messages))
+        far = swap(far, "chan", 1)
+        left, some, grad_proj, grad_filter = weight_products(messages, turned, kinds, share)
+        first, second = last_products(left, some, far)
+        first, second, grad_proj = lax.optimization_barrier((first, second, grad_proj))
         pieces = [ring(first, 1), ring(second, -1)]
+        gathered = gather_chan(grad_proj)
+        grad_rows = input_gradient(gathered, weight_cols)
+        grad_rows, pieces = lax.optimization_barrier((grad_rows, pieces))
         grad_weight = place_weights(pieces, kinds, share, slabs, factor)
     else:
         grad_proj, grad_weight, grad_filter = general_tail(messages, features, place, mine, kinds, share, factor)
-
+        grad_rows = input_gradient(gather_chan(grad_proj), weight_cols)
     return (
-        input_gradient(gather_chan(grad_proj), weight_cols),
+        grad_rows,
         grad_weight.reshape(kinds, own, depth),
         grad_filter,
     )

time: 132 us -> 114 us (0.86)
  starting transfers between devices: 42.8 us -> 30.4 us
  local copies, waits for them, and re-layouts: 18.5 us -> 7.88 us
  waiting for transfers between devices: 51.5 us -> 56.3 us
    ppermute x24 -> x17, starting transfers between devices: 25.4 us -> 14.5 us  [swap(): return lax.ppermute(values, axis, [(i, i ^ mask) for i in range(size)])]
    ppermute x6, starting transfers between devices: 17.4 us -> 9.11 us  [ring(): lax.ppermute(found[-1], 'ctx', [(i, (i + step) % size) for i in range(siz...]
    unnamed x41 -> x32, local copies, waits for them, and re-layouts: 14.5 us -> 7 us
    ppermute x0 -> x2, waiting for transfers between devices: none -> 6.56 us  [the longest x1 6.56 us: per_device(): messages.append(lax.ppermute(messages[2], 'ctx', [(1, 0), (2, 3)]))]
    all_to_all x0 -> x1, starting transfers between devices: none -> 4.87 us  [per_device(): lax.all_to_all(turned, 'ctx', split_axis=0, concat_axis=0)]
    ppermute x24 -> x17, waiting for transfers between devices: 40.9 us -> 36.6 us  [swap(): return lax.ppermute(values, axis, [(i, i ^ mask) for i in range(size)])]
    ppermute x6, waiting for transfers between devices: 10.6 us -> 13.2 us  [ring(): lax.ppermute(found[-1], 'ctx', [(i, (i + step) % size) for i in range(siz...]
    dynamic_slice x2 -> x0, local copies, waits for them, and re-layouts: 2.09 us -> none  [share_of(): return lax.dynamic_slice_in_dim(array, (place ^ m) * size, size, axis)]
  transfers between devices with their start and end apart: 30 -> 26, of which waited for: 12 -> 12; matrix products, arithmetic and copies ran while one was open for 6% -> 1% of each run, Pallas kernels for 12% -> 14%
where the time goes in v2:
time: 114 us; the launch traced here: 113 us
  waiting for transfers between devices  56.3 us (49%)
  starting transfers between devices  30.4 us (27%)
  Pallas kernels  17.6 us (15%)
  local copies, waits for them, and re-layouts  7.88 us (7%)
    ppermute x17, waiting for transfers between devices, swap(): return lax.ppermute(values, axis, [(i, i ^ mask) for i in range(size)])  36.6 us
    ppermute x17, starting transfers between devices, swap(): return lax.ppermute(values, axis, [(i, i ^ mask) for i in range(size)])  14.5 us
    ppermute x6, waiting for transfers between devices, ring(): lax.ppermute(found[-1], 'ctx', [(i, (i + step) % size) for i in range(siz...  13.2 us
    ppermute x6, starting transfers between devices, ring(): lax.ppermute(found[-1], 'ctx', [(i, (i + step) % size) for i in range(siz...  9.11 us
    unnamed x32, local copies, waits for them, and re-layouts  7 us
    ppermute x1, waiting for transfers between devices, per_device(): messages.append(lax.ppermute(messages[2], 'ctx', [(1, 0), (2, 3)]))  6.56 us
    pallas_call x1, Pallas kernels, convolve(): pl.pallas_call(functools.partial(conv_kernel, blocks, chans, group, token...  5.96 us
    all_to_all x1, starting transfers between devices, per_device(): lax.all_to_all(turned, 'ctx', split_axis=0, concat_axis=0)  4.87 us
  transfers between devices with their start and end apart: 26, of which 12 were waited for; matrix products, arithmetic and copies ran while one was open for 1% of the time, Pallas kernels for 14%

profile of v2, /device:TPU:0, one launch (start us, length us, event | category | flops | bytes accessed | tf_op | source)
XLA Modules:
  0.0 113.1 jit_solution(9048875726678634483)
XLA Ops:
  1.2 2.6 %collective-permute-start = (bf16[512,1024]{1,0:T(8,128)(2,1)}, bf16[512,1024]{1,0:T(8,128)(2,1)}, u32[]{:S(2)}, u32[]{:S(2)}) collective-permute-start(bf16[512,1024]{1,0:T(8,128)(2,1)} %values_ref.1), channel_id=1, source_target_pairs={{0,2},{1,3},{2,0},{3,1},{4,6},{5,7},{6,4},{7,5},{8,10},{9,11},{10,... | collective-permute-start | bytes 3145736 | tf_op jit(solution)/shard_map/ppermute | solution.py:414
  3.7 1.3 %copy-done.3 = bf16[512,1024]{1,0:T(8,128)(2,1)S(1)} copy-done((bf16[512,1024]{1,0:T(8,128)(2,1)S(1)}, bf16[512,1024]{1,0:T(8,128)(2,1)}, u32[]{:S(2)}) %copy-start.3) | copy-done | bytes 1048600
  7.0 4.9 %all-to-all-start = ((bf16[4,512,256]{2,1,0:T(8,128)(2,1)}), bf16[4,512,256]{2,1,0:T(8,128)(2,1)S(1)}, u32[]{:S(2)}, u32[]{:S(2)}) async-start(bf16[4,512,256]{2,1,0:T(8,128)(2,1)} %copy-done.2), calls=%async_computation | async-start | bytes 2097152 | tf_op jit(solution)/shard_map/all_to_all | solution.py:484
  11.9 1.2 %copy-done.4 = bf16[512,1024]{1,0:T(8,128)(2,1)S(1)} copy-done((bf16[512,1024]{1,0:T(8,128)(2,1)S(1)}, bf16[512,1024]{1,0:T(8,128)(2,1)}, u32[]{:S(2)}) %copy-start.4) | copy-done | bytes 1048600
  13.1 1.2 %copy-done.6 = bf16[512,1024]{1,0:T(8,128)(2,1)S(1)} copy-done((bf16[512,1024]{1,0:T(8,128)(2,1)S(1)}, bf16[512,1024]{1,0:T(8,128)(2,1)}, u32[]{:S(2)}) %copy-start.6) | copy-done | bytes 1048600
  15.1 12.7 %collective-permute-done.refs_0_ = bf16[512,1024]{1,0:T(8,128)(2,1)} collective-permute-done((bf16[512,1024]{1,0:T(8,128)(2,1)}, bf16[512,1024]{1,0:T(8,128)(2,1)}, u32[]{:S(2)}, u32[]{:S(2)}) %collective-permute-start) | collective-permute-done | bytes 1048608 | tf_op jit(solution)/shard_map/ppermute | solution.py:414
  27.8 1.7 %project.4.sum_ref = f32[512,192]{1,0:T(8,128)S(1)} custom-call(bf16[192,4096]{1,0:T(8,128)(2,1)S(1)} %bitcast.6, f32[512,192]{1,0:T(8,128)S(1)} %project.3.sum_ref, bf16[512,1024]{1,0:T(8,128)(2,1)} %collective-permute-done.refs_0_), custom_call_target="tpu_custom_call" | custom-call | flops 201326592 | bytes 1048576 | tf_op jit(solution)/shard_map/project/pallas_call | solution.py:242
  29.5 1.2 %collective-permute-done.2.refs_0_ = bf16[512,1024]{1,0:T(8,128)(2,1)S(1)} collective-permute-done((bf16[512,1024]{1,0:T(8,128)(2,1)}, bf16[512,1024]{1,0:T(8,128)(2,1)S(1)}, u32[]{:S(2)}, u32[]{:S(2)}) %collective-permute-start.2) | collective-permute-done | bytes 1048608 | tf_op jit(solution)/shard_map/ppermute | solution.py:414
  31.9 1.8 %collective-permute-start.3 = (bf16[80,512]{1,0:T(8,128)(2,1)S(1)}, bf16[80,512]{1,0:T(8,128)(2,1)S(1)}, u32[]{:S(2)}, u32[]{:S(2)}) collective-permute-start(bf16[80,512]{1,0:T(8,128)(2,1)S(1)} %get-tuple-element.54), channel_id=1, source_target_pairs={{0,4},{4,0},{8,12},{12,8},{1,5},{5,1},{9,13},{13,9},{2,6},{6,2},{1... | collective-permute-start | bytes 245768 | tf_op jit(solution)/shard_map/ppermute | solution.py:414
  33.7 2.6 %collective-permute-start.4 = (bf16[80,512]{1,0:T(8,128)(2,1)S(1)}, bf16[80,512]{1,0:T(8,128)(2,1)S(1)}, u32[]{:S(2)}, u32[]{:S(2)}) collective-permute-start(bf16[80,512]{1,0:T(8,128)(2,1)S(1)} %get-tuple-element.55), channel_id=1, source_target_pairs={{0,8},{4,12},{8,0},{12,4},{1,9},{5,13},{9,1},{13,5},{2,10},{6,14},... | collective-permute-start | bytes 245768 | tf_op jit(solution)/shard_map/ppermute | solution.py:414
  36.3 4.2 %collective-permute-done.3.refs_2_ = bf16[80,512]{1,0:T(8,128)(2,1)S(1)} collective-permute-done((bf16[80,512]{1,0:T(8,128)(2,1)S(1)}, bf16[80,512]{1,0:T(8,128)(2,1)S(1)}, u32[]{:S(2)}, u32[]{:S(2)}) %collective-permute-start.3) | collective-permute-done | bytes 81952 | tf_op jit(solution)/shard_map/ppermute | solution.py:414
  40.5 3.6 %collective-permute-done.4.refs_3_ = bf16[80,512]{1,0:T(8,128)(2,1)S(1)} collective-permute-done((bf16[80,512]{1,0:T(8,128)(2,1)S(1)}, bf16[80,512]{1,0:T(8,128)(2,1)S(1)}, u32[]{:S(2)}, u32[]{:S(2)}) %collective-permute-start.4) | collective-permute-done | bytes 81952 | tf_op jit(solution)/shard_map/ppermute | solution.py:414
  45.5 6.0 %conv.1 = (bf16[48,2432]{1,0:T(8,128)(2,1)}, bf16[48,2432]{1,0:T(8,128)(2,1)}, bf16[48,2432]{1,0:T(8,128)(2,1)}, bf16[48,2432]{1,0:T(8,128)(2,1)}) custom-call(f32[16,1]{1,0:T(8,128)} %copy.13.refs_0_, bf16[80,512]{1,0:T(8,128)(2,1)} %copy-done.11, bf16[80,512]{1,0:T(8,128)(2,1)} %copy-done.13, bf16[80,512]{1,0:T(8,128)(2,1)} %copy-done.14, ...), custom_call_target="tpu_custom_call" | custom-call | flops 962592768 | bytes 4194304 | tf_op jit(solution)/shard_map/conv/pallas_call | solution.py:182
  51.5 2.5 %collective-permute-start.8 = (bf16[48,2432]{1,0:T(8,128)(2,1)}, bf16[48,2432]{1,0:T(8,128)(2,1)S(1)}, u32[]{:S(2)}, u32[]{:S(2)}) collective-permute-start(bf16[48,2432]{1,0:T(8,128)(2,1)} %get-tuple-element.65), channel_id=1, source_target_pairs={{0,8},{4,12},{8,0},{12,4},{1,9},{5,13},{9,1},{13,5},{2,10},{6,14},... | collective-permute-start | bytes 700424 | tf_op jit(solution)/shard_map/ppermute | solution.py:414
  55.3 10.1 %collective-permute-done.8.refs_2_ = bf16[48,2432]{1,0:T(8,128)(2,1)S(1)} collective-permute-done((bf16[48,2432]{1,0:T(8,128)(2,1)}, bf16[48,2432]{1,0:T(8,128)(2,1)S(1)}, u32[]{:S(2)}, u32[]{:S(2)}) %collective-permute-start.8) | collective-permute-done | bytes 233504 | tf_op jit(solution)/shard_map/ppermute | solution.py:414
  65.4 1.3 %collective-permute-start.10 = (bf16[48,2432]{1,0:T(8,128)(2,1)S(1)}, bf16[48,2432]{1,0:T(8,128)(2,1)S(1)}, u32[]{:S(2)}, u32[]{:S(2)}) collective-permute-start(bf16[48,2432]{1,0:T(8,128)(2,1)S(1)} %collective-permute-done.8.refs_2_), channel_id=1, source_target_pairs={{4,0},{8,12},{5,1},{9,13},{6,2},{10,14},{7,3},{11,15},{20,16},{24,... | collective-permute-start | bytes 700424 | tf_op jit(solution)/shard_map/ppermute | solution.py:505
  66.7 6.6 %collective-permute-done.10.refs_4_ = bf16[48,2432]{1,0:T(8,128)(2,1)S(1)} collective-permute-done((bf16[48,2432]{1,0:T(8,128)(2,1)S(1)}, bf16[48,2432]{1,0:T(8,128)(2,1)S(1)}, u32[]{:S(2)}, u32[]{:S(2)}) %collective-permute-start.10) | collective-permute-done | bytes 233504 | tf_op jit(solution)/shard_map/ppermute | solution.py:505
  74.7 1.1 collective-permute-start.17
  75.8 2.5 %products.2 = (bf16[192,2048]{1,0:T(8,128)(2,1)S(1)}, bf16[192,768]{1,0:T(8,128)(2,1)S(1)}, bf16[192,512]{1,0:T(8,128)(2,1)S(1)}, f32[64,512]{1,0:T(8,128)}) custom-call(bf16[48,2432]{1,0:T(8,128)(2,1)S(1)} %copy-done.7, bf16[48,2432]{1,0:T(8,128)(2,1)S(1)} %collective-permute-done.7.refs_1_, bf16[48,2432]{1,0:T(8,128)(2,1)S(1)} %collective-permute-done.8.refs_2_, ...), custom_call_target="tpu_custom_call" | custom-call | flops 603979776 | bytes 4194304 | tf_op jit(solution)/shard_map/products/pallas_call | solution.py:299
  78.2 1.6 %products.3 = (bf16[96,1024]{1,0:T(8,128)(2,1)S(1)}, bf16[96,1024]{1,0:T(8,128)(2,1)S(1)}) custom-call(bf16[192,2048]{1,0:T(8,128)(2,1)S(1)} %get-tuple-element.72.left_ref, bf16[192,768]{1,0:T(8,128)(2,1)S(1)} %get-tuple-element.73.some_ref, bf16[2048,256]{1,0:T(8,128)(2,1)} %collective-permute-done.12.turned_ref), custom_call_target="tpu_custom_call" | custom-call | flops 201326592 | bytes 1048576 | tf_op jit(solution)/shard_map/products/pallas_call | solution.py:320
  79.9 3.8 %collective-permute-start.22 = (bf16[96,1024]{1,0:T(8,128)(2,1)S(1)}, bf16[96,1024]{1,0:T(8,128)(2,1)S(1)}, u32[]{:S(2)}, u32[]{:S(2)}) collective-permute-start(bf16[96,1024]{1,0:T(8,128)(2,1)S(1)} %get-tuple-element.90.refs_4_), channel_id=1, source_target_pairs={{0,12},{4,0},{8,4},{12,8},{1,13},{5,1},{9,5},{13,9},{2,14},{6,2},{... | collective-permute-start | bytes 589832 | tf_op jit(solution)/shard_map/ppermute | solution.py:433
  83.8 1.0 collective-permute-start.14
  84.7 4.8 %collective-permute-done.19.refs_1_ = bf16[96,1024]{1,0:T(8,128)(2,1)S(1)} collective-permute-done((bf16[96,1024]{1,0:T(8,128)(2,1)S(1)}, bf16[96,1024]{1,0:T(8,128)(2,1)S(1)}, u32[]{:S(2)}, u32[]{:S(2)}) %collective-permute-start.19) | collective-permute-done | bytes 196640 | tf_op jit(solution)/shard_map/ppermute | solution.py:433
  89.5 1.3 %collective-permute-done.22.refs_5_ = bf16[96,1024]{1,0:T(8,128)(2,1)S(1)} collective-permute-done((bf16[96,1024]{1,0:T(8,128)(2,1)S(1)}, bf16[96,1024]{1,0:T(8,128)(2,1)S(1)}, u32[]{:S(2)}, u32[]{:S(2)}) %collective-permute-start.22) | collective-permute-done | bytes 196640 | tf_op jit(solution)/shard_map/ppermute | solution.py:433
  90.8 2.9 %collective-permute-start.23 = (bf16[96,1024]{1,0:T(8,128)(2,1)S(1)}, bf16[96,1024]{1,0:T(8,128)(2,1)S(1)}, u32[]{:S(2)}, u32[]{:S(2)}) collective-permute-start(bf16[96,1024]{1,0:T(8,128)(2,1)S(1)} %collective-permute-done.22.refs_5_), channel_id=1, source_target_pairs={{0,12},{4,0},{8,4},{12,8},{1,13},{5,1},{9,5},{13,9},{2,14},{6,2},{... | collective-permute-start | bytes 589832 | tf_op jit(solution)/shard_map/ppermute | solution.py:433
  93.7 4.8 %collective-permute-done.14.refs_2_ = bf16[192,512]{1,0:T(8,128)(2,1)S(1)} collective-permute-done((bf16[192,512]{1,0:T(8,128)(2,1)S(1)}, bf16[192,512]{1,0:T(8,128)(2,1)S(1)}, u32[]{:S(2)}, u32[]{:S(2)}) %collective-permute-start.14) | collective-permute-done | bytes 196640 | tf_op jit(solution)/shard_map/ppermute | solution.py:414
  99.0 1.5 %collective-permute-done.23.refs_6_ = bf16[96,1024]{1,0:T(8,128)(2,1)S(1)} collective-permute-done((bf16[96,1024]{1,0:T(8,128)(2,1)S(1)}, bf16[96,1024]{1,0:T(8,128)(2,1)S(1)}, u32[]{:S(2)}, u32[]{:S(2)}) %collective-permute-start.23) | collective-permute-done | bytes 196640 | tf_op jit(solution)/shard_map/ppermute | solution.py:433
  100.5 2.4 %collective-permute-start.24 = (bf16[96,1024]{1,0:T(8,128)(2,1)S(1)}, bf16[96,1024]{1,0:T(8,128)(2,1)S(1)}, u32[]{:S(2)}, u32[]{:S(2)}) collective-permute-start(bf16[96,1024]{1,0:T(8,128)(2,1)S(1)} %collective-permute-done.23.refs_6_), channel_id=1, source_target_pairs={{0,12},{4,0},{8,4},{12,8},{1,13},{5,1},{9,5},{13,9},{2,14},{6,2},{... | collective-permute-start | bytes 589832 | tf_op jit(solution)/shard_map/ppermute | solution.py:433
  102.8 2.3 %inputs.1 = bf16[512,1024]{1,0:T(8,128)(2,1)} custom-call(bf16[192,512]{1,0:T(8,128)(2,1)S(1)} %get-tuple-element.78.refs_0_, bf16[192,512]{1,0:T(8,128)(2,1)S(1)} %collective-permute-done.13.refs_1_, bf16[192,512]{1,0:T(8,128)(2,1)S(1)} %collective-permute-done.14.refs_2_, bf16[192,512]{1,0:T(8,128)(2,1)S(1)} %collective-permute-done.15.refs_3_, ...), custom_call_target="tpu_custom_call" | custom-call | flops 805306368 | bytes 4194304 | tf_op jit(solution)/shard_map/inputs/pallas_call | solution.py:362
  105.1 3.5 %collective-permute-done.21.refs_3_ = bf16[96,1024]{1,0:T(8,128)(2,1)S(1)} collective-permute-done((bf16[96,1024]{1,0:T(8,128)(2,1)S(1)}, bf16[96,1024]{1,0:T(8,128)(2,1)S(1)}, u32[]{:S(2)}, u32[]{:S(2)}) %collective-permute-start.21) | collective-permute-done | bytes 196640 | tf_op jit(solution)/shard_map/ppermute | solution.py:433
  108.6 2.2 %collective-permute-done.24.refs_7_ = bf16[96,1024]{1,0:T(8,128)(2,1)S(1)} collective-permute-done((bf16[96,1024]{1,0:T(8,128)(2,1)S(1)}, bf16[96,1024]{1,0:T(8,128)(2,1)S(1)}, u32[]{:S(2)}, u32[]{:S(2)}) %collective-permute-start.24) | collective-permute-done | bytes 196640 | tf_op jit(solution)/shard_map/ppermute | solution.py:433
  110.8 2.3 %place.1 = f32[192,4096]{1,0:T(8,128)} custom-call(bf16[96,1024]{1,0:T(8,128)(2,1)S(1)} %get-tuple-element.86.refs_0_, bf16[96,1024]{1,0:T(8,128)(2,1)S(1)} %collective-permute-done.19.refs_1_, bf16[96,1024]{1,0:T(8,128)(2,1)S(1)} %collective-permute-done.20.refs_2_, bf16[96,1024]{1,0:T(8,128)(2,1)S(1)} %collective-permute-done.21.refs_3_, ...), custom_call_target="tpu_custom_call" | custom-call | bytes 6291456 | tf_op jit(solution)/shard_map/place/pallas_call | solution.py:398
  (65 shorter events, 9.3 us)
Async XLA Ops:
  0.6 44.1 %copy-start = (f32[64]{0:T(128)S(1)}, f32[64]{0:T(128)}, u32[]{:S(2)}) copy-start(f32[64]{0:T(128)} %param.13) | copy-start | bytes 772
  0.6 5.4 %collective-permute-start.1 = (bf16[512,1024]{1,0:T(8,128)(2,1)}, bf16[512,1024]{1,0:T(8,128)(2,1)S(1)}, u32[]{:S(2)}, u32[]{:S(2)}) collective-permute-start(bf16[512,1024]{1,0:T(8,128)(2,1)} %values_ref.1), channel_id=1, source_target_pairs={{0,1},{1,0},{2,3},{3,2},{4,5},{5,4},{6,7},{7,6},{8,9},{9,8},{10,11... | collective-permute-start | bytes 3145736 | tf_op jit(solution)/shard_map/ppermute | solution.py:414
  1.2 26.6 %collective-permute-start = (bf16[512,1024]{1,0:T(8,128)(2,1)}, bf16[512,1024]{1,0:T(8,128)(2,1)}, u32[]{:S(2)}, u32[]{:S(2)}) collective-permute-start(bf16[512,1024]{1,0:T(8,128)(2,1)} %values_ref.1), channel_id=1, source_target_pairs={{0,2},{1,3},{2,0},{3,1},{4,6},{5,7},{6,4},{7,5},{8,10},{9,11},{10,... | collective-permute-start | bytes 3145736 | tf_op jit(solution)/shard_map/ppermute | solution.py:414
  5.0 6.9 %copy-start.12 = (bf16[64,512]{1,0:T(8,128)(2,1)S(1)}, bf16[64,512]{1,0:T(8,128)(2,1)}, u32[]{:S(2)}) copy-start(bf16[64,512]{1,0:T(8,128)(2,1)} %param.14) | copy-start | bytes 196612
  6.0 5.9 %copy-start.1 = (bf16[3,64,4096]{2,1,0:T(8,128)(2,1)S(1)}, bf16[3,64,4096]{2,1,0:T(8,128)(2,1)}, u32[]{:S(2)}) copy-start(bf16[3,64,4096]{2,1,0:T(8,128)(2,1)} %param.11) | copy-start | bytes 4718596
  7.0 37.1 %all-to-all-start = ((bf16[4,512,256]{2,1,0:T(8,128)(2,1)}), bf16[4,512,256]{2,1,0:T(8,128)(2,1)S(1)}, u32[]{:S(2)}, u32[]{:S(2)}) async-start(bf16[4,512,256]{2,1,0:T(8,128)(2,1)} %copy-done.2), calls=%async_computation | async-start | bytes 2097152 | tf_op jit(solution)/shard_map/all_to_all | solution.py:484
  15.1 15.6 %copy-start.10 = (f32[64,512]{1,0:T(8,128)S(1)}, f32[64,512]{1,0:T(8,128)}, u32[]{:S(2)}) copy-start(f32[64,512]{1,0:T(8,128)} %filter_ref) | copy-start | bytes 393220
  27.8 2.9 %collective-permute-start.2 = (bf16[512,1024]{1,0:T(8,128)(2,1)}, bf16[512,1024]{1,0:T(8,128)(2,1)S(1)}, u32[]{:S(2)}, u32[]{:S(2)}) collective-permute-start(bf16[512,1024]{1,0:T(8,128)(2,1)} %collective-permute-done.refs_0_), channel_id=1, source_target_pairs={{0,1},{1,0},{2,3},{3,2},{4,5},{5,4},{6,7},{7,6},{8,9},{9,8},{10,11... | collective-permute-start | bytes 3145736 | tf_op jit(solution)/shard_map/ppermute | solution.py:414
  31.9 8.6 %collective-permute-start.3 = (bf16[80,512]{1,0:T(8,128)(2,1)S(1)}, bf16[80,512]{1,0:T(8,128)(2,1)S(1)}, u32[]{:S(2)}, u32[]{:S(2)}) collective-permute-start(bf16[80,512]{1,0:T(8,128)(2,1)S(1)} %get-tuple-element.54), channel_id=1, source_target_pairs={{0,4},{4,0},{8,12},{12,8},{1,5},{5,1},{9,13},{13,9},{2,6},{6,2},{1... | collective-permute-start | bytes 245768 | tf_op jit(solution)/shard_map/ppermute | solution.py:414
  33.7 10.4 %collective-permute-start.4 = (bf16[80,512]{1,0:T(8,128)(2,1)S(1)}, bf16[80,512]{1,0:T(8,128)(2,1)S(1)}, u32[]{:S(2)}, u32[]{:S(2)}) collective-permute-start(bf16[80,512]{1,0:T(8,128)(2,1)S(1)} %get-tuple-element.55), channel_id=1, source_target_pairs={{0,8},{4,12},{8,0},{12,4},{1,9},{5,13},{9,1},{13,5},{2,10},{6,14},... | collective-permute-start | bytes 245768 | tf_op jit(solution)/shard_map/ppermute | solution.py:414
  36.3 7.8 %collective-permute-start.5 = (bf16[80,512]{1,0:T(8,128)(2,1)S(1)}, bf16[80,512]{1,0:T(8,128)(2,1)S(1)}, u32[]{:S(2)}, u32[]{:S(2)}) collective-permute-start(bf16[80,512]{1,0:T(8,128)(2,1)S(1)} %get-tuple-element.56), channel_id=1, source_target_pairs={{0,12},{4,8},{8,4},{12,0},{1,13},{5,9},{9,5},{13,1},{2,14},{6,10},... | collective-permute-start | bytes 245768 | tf_op jit(solution)/shard_map/ppermute | solution.py:414
  40.5 5.0 %copy-start.13 = (bf16[80,512]{1,0:T(8,128)(2,1)}, bf16[80,512]{1,0:T(8,128)(2,1)S(1)}, u32[]{:S(2)}) copy-start(bf16[80,512]{1,0:T(8,128)(2,1)S(1)} %collective-permute-done.3.refs_2_) | copy-start | bytes 245764
  44.1 29.9 %collective-permute-start.6 = (bf16[2048,256]{1,0:T(8,128)(2,1)S(1)}, bf16[2048,256]{1,0:T(8,128)(2,1)}, u32[]{:S(2)}, u32[]{:S(2)}) collective-permute-start(bf16[2048,256]{1,0:T(8,128)(2,1)S(1)} %bitcast.9), channel_id=1, source_target_pairs={{0,2},{1,3},{2,0},{3,1},{4,6},{5,7},{6,4},{7,5},{8,10},{9,11},{10,... | collective-permute-start | bytes 3145736 | tf_op jit(solution)/shard_map/ppermute | solution.py:414
  51.5 13.9 %collective-permute-start.8 = (bf16[48,2432]{1,0:T(8,128)(2,1)}, bf16[48,2432]{1,0:T(8,128)(2,1)S(1)}, u32[]{:S(2)}, u32[]{:S(2)}) collective-permute-start(bf16[48,2432]{1,0:T(8,128)(2,1)} %get-tuple-element.65), channel_id=1, source_target_pairs={{0,8},{4,12},{8,0},{12,4},{1,9},{5,13},{9,1},{13,5},{2,10},{6,14},... | collective-permute-start | bytes 700424 | tf_op jit(solution)/shard_map/ppermute | solution.py:414
  53.9 12.8 %collective-permute-start.7 = (bf16[48,2432]{1,0:T(8,128)(2,1)}, bf16[48,2432]{1,0:T(8,128)(2,1)S(1)}, u32[]{:S(2)}, u32[]{:S(2)}) collective-permute-start(bf16[48,2432]{1,0:T(8,128)(2,1)} %get-tuple-element.64), channel_id=1, source_target_pairs={{0,4},{4,0},{8,12},{12,8},{1,5},{5,1},{9,13},{13,9},{2,6},{6,2},{1... | collective-permute-start | bytes 700424 | tf_op jit(solution)/shard_map/ppermute | solution.py:414
  54.6 12.1 %collective-permute-start.9 = (bf16[48,2432]{1,0:T(8,128)(2,1)}, bf16[48,2432]{1,0:T(8,128)(2,1)S(1)}, u32[]{:S(2)}, u32[]{:S(2)}) collective-permute-start(bf16[48,2432]{1,0:T(8,128)(2,1)} %get-tuple-element.66), channel_id=1, source_target_pairs={{4,8},{8,4},{5,9},{9,5},{6,10},{10,6},{7,11},{11,7},{20,24},{24,20... | collective-permute-start | bytes 700424 | tf_op jit(solution)/shard_map/ppermute | solution.py:504
  65.4 7.9 %collective-permute-start.10 = (bf16[48,2432]{1,0:T(8,128)(2,1)S(1)}, bf16[48,2432]{1,0:T(8,128)(2,1)S(1)}, u32[]{:S(2)}, u32[]{:S(2)}) collective-permute-start(bf16[48,2432]{1,0:T(8,128)(2,1)S(1)} %collective-permute-done.8.refs_2_), channel_id=1, source_target_pairs={{4,0},{8,12},{5,1},{9,13},{6,2},{10,14},{7,3},{11,15},{20,16},{24,... | collective-permute-start | bytes 700424 | tf_op jit(solution)/shard_map/ppermute | solution.py:505
  66.6 9.1 %collective-permute-start.11 = (bf16[2048,256]{1,0:T(8,128)(2,1)S(1)}, bf16[2048,256]{1,0:T(8,128)(2,1)}, u32[]{:S(2)}, u32[]{:S(2)}) collective-permute-start(bf16[2048,256]{1,0:T(8,128)(2,1)S(1)} %bitcast.10), channel_id=1, source_target_pairs={{0,1},{1,0},{2,3},{3,2},{4,5},{5,4},{6,7},{7,6},{8,9},{9,8},{10,11... | collective-permute-start | bytes 3145736 | tf_op jit(solution)/shard_map/ppermute | solution.py:414
  74.0 4.3 %collective-permute-start.12 = (bf16[2048,256]{1,0:T(8,128)(2,1)}, bf16[2048,256]{1,0:T(8,128)(2,1)}, u32[]{:S(2)}, u32[]{:S(2)}) collective-permute-start(bf16[2048,256]{1,0:T(8,128)(2,1)} %collective-permute-done.6.refs_7_), channel_id=1, source_target_pairs={{0,1},{1,0},{2,3},{3,2},{4,5},{5,4},{6,7},{7,6},{8,9},{9,8},{10,11... | collective-permute-start | bytes 3145736 | tf_op jit(solution)/shard_map/ppermute | solution.py:414
  74.0 1.8 %copy-start.7 = (bf16[48,2432]{1,0:T(8,128)(2,1)S(1)}, bf16[48,2432]{1,0:T(8,128)(2,1)}, u32[]{:S(2)}) copy-start(bf16[48,2432]{1,0:T(8,128)(2,1)} %get-tuple-element.67.refs_0_) | copy-start | bytes 700420
  74.2 9.6 %collective-permute-start.16 = (bf16[192,1024]{1,0:T(8,128)(2,1)S(1)}, bf16[192,1024]{1,0:T(8,128)(2,1)S(1)}, u32[]{:S(2)}, u32[]{:S(2)}) collective-permute-start(bf16[192,1024]{1,0:T(8,128)(2,1)S(1)} %get-tuple-element.80), channel_id=1, source_target_pairs={{0,1},{1,0},{2,3},{3,2},{4,5},{5,4},{6,7},{7,6},{8,9},{9,8},{10,11... | collective-permute-start | bytes 1179656 | tf_op jit(solution)/shard_map/ppermute | solution.py:414
  74.7 19.0 %collective-permute-start.17 = (bf16[192,1024]{1,0:T(8,128)(2,1)S(1)}, bf16[192,1024]{1,0:T(8,128)(2,1)S(1)}, u32[]{:S(2)}, u32[]{:S(2)}) collective-permute-start(bf16[192,1024]{1,0:T(8,128)(2,1)S(1)} %get-tuple-element.81), channel_id=1, source_target_pairs={{0,2},{1,3},{2,0},{3,1},{4,6},{5,7},{6,4},{7,5},{8,10},{9,11},{10,... | collective-permute-start | bytes 1179656 | tf_op jit(solution)/shard_map/ppermute | solution.py:414
  79.9 9.7 %collective-permute-start.19 = (bf16[96,1024]{1,0:T(8,128)(2,1)S(1)}, bf16[96,1024]{1,0:T(8,128)(2,1)S(1)}, u32[]{:S(2)}, u32[]{:S(2)}) collective-permute-start(bf16[96,1024]{1,0:T(8,128)(2,1)S(1)} %get-tuple-element.86.refs_0_), channel_id=1, source_target_pairs={{0,4},{4,8},{8,12},{12,0},{1,5},{5,9},{9,13},{13,1},{2,6},{6,10},{... | collective-permute-start | bytes 589832 | tf_op jit(solution)/shard_map/ppermute | solution.py:433
  79.9 10.9 %collective-permute-start.22 = (bf16[96,1024]{1,0:T(8,128)(2,1)S(1)}, bf16[96,1024]{1,0:T(8,128)(2,1)S(1)}, u32[]{:S(2)}, u32[]{:S(2)}) collective-permute-start(bf16[96,1024]{1,0:T(8,128)(2,1)S(1)} %get-tuple-element.90.refs_4_), channel_id=1, source_target_pairs={{0,12},{4,0},{8,4},{12,8},{1,13},{5,1},{9,5},{13,9},{2,14},{6,2},{... | collective-permute-start | bytes 589832 | tf_op jit(solution)/shard_map/ppermute | solution.py:433
  83.8 19.1 %collective-permute-start.18 = (bf16[192,1024]{1,0:T(8,128)(2,1)S(1)}, bf16[192,1024]{1,0:T(8,128)(2,1)S(1)}, u32[]{:S(2)}, u32[]{:S(2)}) collective-permute-start(bf16[192,1024]{1,0:T(8,128)(2,1)S(1)} %get-tuple-element.82), channel_id=1, source_target_pairs={{0,3},{1,2},{2,1},{3,0},{4,7},{5,6},{6,5},{7,4},{8,11},{9,10},{10,... | collective-permute-start | bytes 1179656 | tf_op jit(solution)/shard_map/ppermute | solution.py:414
  83.8 14.7 %collective-permute-start.14 = (bf16[192,512]{1,0:T(8,128)(2,1)S(1)}, bf16[192,512]{1,0:T(8,128)(2,1)S(1)}, u32[]{:S(2)}, u32[]{:S(2)}) collective-permute-start(bf16[192,512]{1,0:T(8,128)(2,1)S(1)} %get-tuple-element.78.refs_0_), channel_id=1, source_target_pairs={{0,2},{1,3},{2,0},{3,1},{4,6},{5,7},{6,4},{7,5},{8,10},{9,11},{10,... | collective-permute-start | bytes 589832 | tf_op jit(solution)/shard_map/ppermute | solution.py:414
  89.5 9.5 %collective-permute-start.20 = (bf16[96,1024]{1,0:T(8,128)(2,1)S(1)}, bf16[96,1024]{1,0:T(8,128)(2,1)S(1)}, u32[]{:S(2)}, u32[]{:S(2)}) collective-permute-start(bf16[96,1024]{1,0:T(8,128)(2,1)S(1)} %collective-permute-done.19.refs_1_), channel_id=1, source_target_pairs={{0,4},{4,8},{8,12},{12,0},{1,5},{5,9},{9,13},{13,1},{2,6},{6,10},{... | collective-permute-start | bytes 589832 | tf_op jit(solution)/shard_map/ppermute | solution.py:433
  90.8 9.7 %collective-permute-start.23 = (bf16[96,1024]{1,0:T(8,128)(2,1)S(1)}, bf16[96,1024]{1,0:T(8,128)(2,1)S(1)}, u32[]{:S(2)}, u32[]{:S(2)}) collective-permute-start(bf16[96,1024]{1,0:T(8,128)(2,1)S(1)} %collective-permute-done.22.refs_5_), channel_id=1, source_target_pairs={{0,12},{4,0},{8,4},{12,8},{1,13},{5,1},{9,5},{13,9},{2,14},{6,2},{... | collective-permute-start | bytes 589832 | tf_op jit(solution)/shard_map/ppermute | solution.py:433
  93.7 9.2 %collective-permute-start.13 = (bf16[192,512]{1,0:T(8,128)(2,1)S(1)}, bf16[192,512]{1,0:T(8,128)(2,1)S(1)}, u32[]{:S(2)}, u32[]{:S(2)}) collective-permute-start(bf16[192,512]{1,0:T(8,128)(2,1)S(1)} %get-tuple-element.78.refs_0_), channel_id=1, source_target_pairs={{0,1},{1,0},{2,3},{3,2},{4,5},{5,4},{6,7},{7,6},{8,9},{9,8},{10,11... | collective-permute-start | bytes 589832 | tf_op jit(solution)/shard_map/ppermute | solution.py:414
  98.5 4.4 %collective-permute-start.15 = (bf16[192,512]{1,0:T(8,128)(2,1)S(1)}, bf16[192,512]{1,0:T(8,128)(2,1)S(1)}, u32[]{:S(2)}, u32[]{:S(2)}) collective-permute-start(bf16[192,512]{1,0:T(8,128)(2,1)S(1)} %collective-permute-done.14.refs_2_), channel_id=1, source_target_pairs={{0,1},{1,0},{2,3},{3,2},{4,5},{5,4},{6,7},{7,6},{8,9},{9,8},{10,11... | collective-permute-start | bytes 589832 | tf_op jit(solution)/shard_map/ppermute | solution.py:414
  99.0 9.6 %collective-permute-start.21 = (bf16[96,1024]{1,0:T(8,128)(2,1)S(1)}, bf16[96,1024]{1,0:T(8,128)(2,1)S(1)}, u32[]{:S(2)}, u32[]{:S(2)}) collective-permute-start(bf16[96,1024]{1,0:T(8,128)(2,1)S(1)} %collective-permute-done.20.refs_2_), channel_id=1, source_target_pairs={{0,4},{4,8},{8,12},{12,0},{1,5},{5,9},{9,13},{13,1},{2,6},{6,10},{... | collective-permute-start | bytes 589832 | tf_op jit(solution)/shard_map/ppermute | solution.py:433
  100.5 10.4 %collective-permute-start.24 = (bf16[96,1024]{1,0:T(8,128)(2,1)S(1)}, bf16[96,1024]{1,0:T(8,128)(2,1)S(1)}, u32[]{:S(2)}, u32[]{:S(2)}) collective-permute-start(bf16[96,1024]{1,0:T(8,128)(2,1)S(1)} %collective-permute-done.23.refs_6_), channel_id=1, source_target_pairs={{0,12},{4,0},{8,4},{12,8},{1,13},{5,1},{9,5},{13,9},{2,14},{6,2},{... | collective-permute-start | bytes 589832 | tf_op jit(solution)/shard_map/ppermute | solution.py:433
  (10 other events, 11.5 us)

commit v3 on v2

--- a/solution.py
+++ b/solution.py
@@ -479,11 +479,15 @@
     along = [out_grad.astype(F32), long_filter]
     gain = share_of(skip_gain, 0)[:, None]
 
+    weight_cols = [lax.dynamic_slice_in_dim(weight_rows, (mine ^ m) * width, width, 1) for m in range(slabs)]
     if line:
         turned = after(column_pieces(activations, blocks), features[1])
         turned = lax.all_to_all(turned, "ctx", split_axis=0, concat_axis=0).reshape(length * blocks, width // blocks)
         sums = project(weight_rows, [], features[:2], [0, 1])
-        features[2], sums, along = lax.optimization_barrier((features[2], sums, along))
+        weight_cols[1] = swap(weight_cols[1], "chan", 1)
+        features[2], sums, along, gain, weight_cols = lax.optimization_barrier(
+            (features[2], sums, along, gain, weight_cols)
+        )
         features.append(swap(features[2], "chan", 1))
         sums = project(weight_rows, sums, features[2:3], [2])
         pieces = project(weight_rows, sums, features[3:], [3], (blocks, kinds, along))
@@ -495,9 +499,6 @@
         signals, turned = lax.optimization_barrier((signals, turned))
         turned = [turned, swap(turned, "chan", 1), swap(turned, "chan", 2)]
     messages = convolve(signals, gain)
-    weight_cols = [lax.dynamic_slice_in_dim(weight_rows, (mine ^ m) * width, width, 1) for m in range(slabs)]
-    weight_cols = after(weight_cols, turned[2] if line else signals[-1])
-    weight_cols = [swap(cols, "chan", m) for m, cols in enumerate(weight_cols)]
 
     if line:
         messages = [messages[0], swap(messages[1], "ctx", 1), swap(messages[2], "ctx", 2), messages[3]]
@@ -510,11 +511,14 @@
         first, second, grad_proj = lax.optimization_barrier((first, second, grad_proj))
         pieces = [ring(first, 1), ring(second, -1)]
         gathered = gather_chan(grad_proj)
+        weight_cols = after(weight_cols, gathered[2])
+        weight_cols = [*weight_cols[:2], swap(weight_cols[2], "chan", 2), swap(weight_cols[3], "chan", 3)]
         grad_rows = input_gradient(gathered, weight_cols)
         grad_rows, pieces = lax.optimization_barrier((grad_rows, pieces))
         grad_weight = place_weights(pieces, kinds, share, slabs, factor)
     else:
         grad_proj, grad_weight, grad_filter = general_tail(messages, features, place, mine, kinds, share, factor)
+        weight_cols = [swap(cols, "chan", m) for m, cols in enumerate(weight_cols)]
         grad_rows = input_gradient(gather_chan(grad_proj), weight_cols)
     return (
         grad_rows,

time: 114 us -> 111 us (0.974)
  starting transfers between devices: 30.4 us -> 27.3 us
  Pallas kernels: 17.6 us -> 15.2 us
  local copies, waits for them, and re-layouts: 7.88 us -> 9.06 us
    ppermute x6, waiting for transfers between devices: 13.2 us -> 18.1 us  [ring(): lax.ppermute(found[-1], 'ctx', [(i, (i + step) % size) for i in range(siz...]
    ppermute x17, waiting for transfers between devices: 36.6 us -> 32.3 us  [swap(): return lax.ppermute(values, axis, [(i, i ^ mask) for i in range(size)])]
    ppermute x6, starting transfers between devices: 9.11 us -> 6.91 us  [ring(): lax.ppermute(found[-1], 'ctx', [(i, (i + step) % size) for i in range(siz...]
    pallas_call x1, Pallas kernels: 1.62 us -> 0.37 us  [last_products(): pl.pallas_call(last_kernel, out_shape=[half, half], in_specs=[VMEM] * 3,...]
    pallas_call x1, Pallas kernels: 2.46 us -> 1.31 us  [weight_products(): pl.pallas_call(functools.partial(product_kernel, kinds, share, blocks, sl...]
    unnamed x32 -> x30, local copies, waits for them, and re-layouts: 7 us -> 7.24 us
  transfers between devices with their start and end apart: 26 -> 26, of which waited for: 12 -> 15; matrix products, arithmetic and copies ran while one was open for 1% -> 2% of each run, Pallas kernels for 14% -> 11%
where the time goes in v3:
time: 111 us; the launch traced here: 110 us
  waiting for transfers between devices  57 us (51%)
  starting transfers between devices  27.3 us (25%)
  Pallas kernels  15.2 us (14%)
  local copies, waits for them, and re-layouts  9.06 us (8%)
    ppermute x17, waiting for transfers between devices, swap(): return lax.ppermute(values, axis, [(i, i ^ mask) for i in range(size)])  32.3 us
    ppermute x6, waiting for transfers between devices, ring(): lax.ppermute(found[-1], 'ctx', [(i, (i + step) % size) for i in range(siz...  18.1 us
    ppermute x17, starting transfers between devices, swap(): return lax.ppermute(values, axis, [(i, i ^ mask) for i in range(size)])  13.6 us
    unnamed x30, local copies, waits for them, and re-layouts  7.24 us
    ppermute x6, starting transfers between devices, ring(): lax.ppermute(found[-1], 'ctx', [(i, (i + step) % size) for i in range(siz...  6.91 us
    ppermute x1, waiting for transfers between devices, per_device(): messages.append(lax.ppermute(messages[2], 'ctx', [(1, 0), (2, 3)]))  6.56 us
    pallas_call x1, Pallas kernels, convolve(): pl.pallas_call(functools.partial(conv_kernel, blocks, chans, group, token...  5.95 us
    all_to_all x1, starting transfers between devices, per_device(): lax.all_to_all(turned, 'ctx', split_axis=0, concat_axis=0)  4.87 us
  transfers between devices with their start and end apart: 26, of which 15 were waited for; matrix products, arithmetic and copies ran while one was open for 2% of the time, Pallas kernels for 11%

profile of v3, /device:TPU:0, one launch (start us, length us, event | category | flops | bytes accessed | tf_op | source)
XLA Modules:
  0.0 110.2 jit_solution(11450517510875863485)
XLA Ops:
  1.2 2.6 %collective-permute-start = (bf16[512,1024]{1,0:T(8,128)(2,1)}, bf16[512,1024]{1,0:T(8,128)(2,1)}, u32[]{:S(2)}, u32[]{:S(2)}) collective-permute-start(bf16[512,1024]{1,0:T(8,128)(2,1)} %values_ref.1), channel_id=1, source_target_pairs={{0,2},{1,3},{2,0},{3,1},{4,6},{5,7},{6,4},{7,5},{8,10},{9,11},{10,... | collective-permute-start | bytes 3145736 | tf_op jit(solution)/shard_map/ppermute | solution.py:414
  3.7 1.3 %copy-done.3 = bf16[512,1024]{1,0:T(8,128)(2,1)S(1)} copy-done((bf16[512,1024]{1,0:T(8,128)(2,1)S(1)}, bf16[512,1024]{1,0:T(8,128)(2,1)}, u32[]{:S(2)}) %copy-start.3) | copy-done | bytes 1048600
  7.0 4.9 %all-to-all-start = ((bf16[4,512,256]{2,1,0:T(8,128)(2,1)}), bf16[4,512,256]{2,1,0:T(8,128)(2,1)S(1)}, u32[]{:S(2)}, u32[]{:S(2)}) async-start(bf16[4,512,256]{2,1,0:T(8,128)(2,1)} %copy-done.2), calls=%async_computation | async-start | bytes 2097152 | tf_op jit(solution)/shard_map/all_to_all | solution.py:485
  11.9 1.1 constant_dynamic-slice_fusion
  13.9 1.2 %copy-done.4 = bf16[512,1024]{1,0:T(8,128)(2,1)S(1)} copy-done((bf16[512,1024]{1,0:T(8,128)(2,1)S(1)}, bf16[512,1024]{1,0:T(8,128)(2,1)}, u32[]{:S(2)}) %copy-start.4) | copy-done | bytes 1048600
  15.1 1.2 %copy-done.6 = bf16[512,1024]{1,0:T(8,128)(2,1)S(1)} copy-done((bf16[512,1024]{1,0:T(8,128)(2,1)S(1)}, bf16[512,1024]{1,0:T(8,128)(2,1)}, u32[]{:S(2)}) %copy-start.6) | copy-done | bytes 1048600
  17.1 10.7 %collective-permute-done.refs_0_ = bf16[512,1024]{1,0:T(8,128)(2,1)} collective-permute-done((bf16[512,1024]{1,0:T(8,128)(2,1)}, bf16[512,1024]{1,0:T(8,128)(2,1)}, u32[]{:S(2)}, u32[]{:S(2)}) %collective-permute-start) | collective-permute-done | bytes 1048608 | tf_op jit(solution)/shard_map/ppermute | solution.py:414
  27.8 1.7 %project.4.sum_ref = f32[512,192]{1,0:T(8,128)S(1)} custom-call(bf16[192,4096]{1,0:T(8,128)(2,1)S(1)} %bitcast.7, f32[512,192]{1,0:T(8,128)S(1)} %project.3.sum_ref, bf16[512,1024]{1,0:T(8,128)(2,1)} %collective-permute-done.refs_0_), custom_call_target="tpu_custom_call" | custom-call | flops 201326592 | bytes 1048576 | tf_op jit(solution)/shard_map/project/pallas_call | solution.py:242
  29.5 1.1 %collective-permute-done.3.refs_0_ = bf16[512,1024]{1,0:T(8,128)(2,1)S(1)} collective-permute-done((bf16[512,1024]{1,0:T(8,128)(2,1)}, bf16[512,1024]{1,0:T(8,128)(2,1)S(1)}, u32[]{:S(2)}, u32[]{:S(2)}) %collective-permute-start.3) | collective-permute-done | bytes 1048608 | tf_op jit(solution)/shard_map/ppermute | solution.py:414
  31.9 1.8 %collective-permute-start.4 = (bf16[80,512]{1,0:T(8,128)(2,1)S(1)}, bf16[80,512]{1,0:T(8,128)(2,1)S(1)}, u32[]{:S(2)}, u32[]{:S(2)}) collective-permute-start(bf16[80,512]{1,0:T(8,128)(2,1)S(1)} %get-tuple-element.59), channel_id=1, source_target_pairs={{0,4},{4,0},{8,12},{12,8},{1,5},{5,1},{9,13},{13,9},{2,6},{6,2},{1... | collective-permute-start | bytes 245768 | tf_op jit(solution)/shard_map/ppermute | solution.py:414
  33.7 2.6 %collective-permute-start.5 = (bf16[80,512]{1,0:T(8,128)(2,1)S(1)}, bf16[80,512]{1,0:T(8,128)(2,1)S(1)}, u32[]{:S(2)}, u32[]{:S(2)}) collective-permute-start(bf16[80,512]{1,0:T(8,128)(2,1)S(1)} %get-tuple-element.60), channel_id=1, source_target_pairs={{0,8},{4,12},{8,0},{12,4},{1,9},{5,13},{9,1},{13,5},{2,10},{6,14},... | collective-permute-start | bytes 245768 | tf_op jit(solution)/shard_map/ppermute | solution.py:414
  36.3 4.2 %collective-permute-done.4.refs_2_ = bf16[80,512]{1,0:T(8,128)(2,1)S(1)} collective-permute-done((bf16[80,512]{1,0:T(8,128)(2,1)S(1)}, bf16[80,512]{1,0:T(8,128)(2,1)S(1)}, u32[]{:S(2)}, u32[]{:S(2)}) %collective-permute-start.4) | collective-permute-done | bytes 81952 | tf_op jit(solution)/shard_map/ppermute | solution.py:414
  40.5 3.6 %collective-permute-done.5.refs_3_ = bf16[80,512]{1,0:T(8,128)(2,1)S(1)} collective-permute-done((bf16[80,512]{1,0:T(8,128)(2,1)S(1)}, bf16[80,512]{1,0:T(8,128)(2,1)S(1)}, u32[]{:S(2)}, u32[]{:S(2)}) %collective-permute-start.5) | collective-permute-done | bytes 81952 | tf_op jit(solution)/shard_map/ppermute | solution.py:414
  45.4 6.0 %conv.1 = (bf16[48,2432]{1,0:T(8,128)(2,1)}, bf16[48,2432]{1,0:T(8,128)(2,1)}, bf16[48,2432]{1,0:T(8,128)(2,1)}, bf16[48,2432]{1,0:T(8,128)(2,1)}) custom-call(f32[16,1]{1,0:T(8,128)} %copy.13.refs_0_, bf16[80,512]{1,0:T(8,128)(2,1)} %copy-done.9, bf16[80,512]{1,0:T(8,128)(2,1)} %copy-done.12, bf16[80,512]{1,0:T(8,128)(2,1)} %copy-done.13, ...), custom_call_target="tpu_custom_call" | custom-call | flops 962592768 | bytes 4194304 | tf_op jit(solution)/shard_map/conv/pallas_call | solution.py:182
  51.4 2.5 %collective-permute-start.9 = (bf16[48,2432]{1,0:T(8,128)(2,1)}, bf16[48,2432]{1,0:T(8,128)(2,1)S(1)}, u32[]{:S(2)}, u32[]{:S(2)}) collective-permute-start(bf16[48,2432]{1,0:T(8,128)(2,1)} %get-tuple-element.71), channel_id=1, source_target_pairs={{0,8},{4,12},{8,0},{12,4},{1,9},{5,13},{9,1},{13,5},{2,10},{6,14},... | collective-permute-start | bytes 700424 | tf_op jit(solution)/shard_map/ppermute | solution.py:414
  55.2 10.1 %collective-permute-done.9.refs_2_ = bf16[48,2432]{1,0:T(8,128)(2,1)S(1)} collective-permute-done((bf16[48,2432]{1,0:T(8,128)(2,1)}, bf16[48,2432]{1,0:T(8,128)(2,1)S(1)}, u32[]{:S(2)}, u32[]{:S(2)}) %collective-permute-start.9) | collective-permute-done | bytes 233504 | tf_op jit(solution)/shard_map/ppermute | solution.py:414
  65.3 1.3 %collective-permute-start.11 = (bf16[48,2432]{1,0:T(8,128)(2,1)S(1)}, bf16[48,2432]{1,0:T(8,128)(2,1)S(1)}, u32[]{:S(2)}, u32[]{:S(2)}) collective-permute-start(bf16[48,2432]{1,0:T(8,128)(2,1)S(1)} %collective-permute-done.9.refs_2_), channel_id=1, source_target_pairs={{4,0},{8,12},{5,1},{9,13},{6,2},{10,14},{7,3},{11,15},{20,16},{24,... | collective-permute-start | bytes 700424 | tf_op jit(solution)/shard_map/ppermute | solution.py:506
  66.7 6.6 %collective-permute-done.11.refs_4_ = bf16[48,2432]{1,0:T(8,128)(2,1)S(1)} collective-permute-done((bf16[48,2432]{1,0:T(8,128)(2,1)S(1)}, bf16[48,2432]{1,0:T(8,128)(2,1)S(1)}, u32[]{:S(2)}, u32[]{:S(2)}) %collective-permute-start.11) | collective-permute-done | bytes 233504 | tf_op jit(solution)/shard_map/ppermute | solution.py:506
  74.2 1.3 %products.2 = (bf16[192,2048]{1,0:T(8,128)(2,1)S(1)}, bf16[192,768]{1,0:T(8,128)(2,1)S(1)}, bf16[192,512]{1,0:T(8,128)(2,1)S(1)}, f32[64,512]{1,0:T(8,128)}) custom-call(bf16[48,2432]{1,0:T(8,128)(2,1)S(1)} %copy-done.7, bf16[48,2432]{1,0:T(8,128)(2,1)S(1)} %collective-permute-done.8.refs_1_, bf16[48,2432]{1,0:T(8,128)(2,1)S(1)} %collective-permute-done.9.refs_2_, ...), custom_call_target="tpu_custom_call" | custom-call | flops 603979776 | bytes 4194304 | tf_op jit(solution)/shard_map/products/pallas_call | solution.py:299
  76.3 1.1 %collective-permute-start.15 = (bf16[192,512]{1,0:T(8,128)(2,1)S(1)}, bf16[192,512]{1,0:T(8,128)(2,1)S(1)}, u32[]{:S(2)}, u32[]{:S(2)}) collective-permute-start(bf16[192,512]{1,0:T(8,128)(2,1)S(1)} %get-tuple-element.84.refs_0_), channel_id=1, source_target_pairs={{0,2},{1,3},{2,0},{3,1},{4,6},{5,7},{6,4},{7,5},{8,10},{9,11},{10,... | collective-permute-start | bytes 589832 | tf_op jit(solution)/shard_map/ppermute | solution.py:414
  77.4 3.8 %collective-permute-start.22 = (bf16[96,1024]{1,0:T(8,128)(2,1)S(1)}, bf16[96,1024]{1,0:T(8,128)(2,1)S(1)}, u32[]{:S(2)}, u32[]{:S(2)}) collective-permute-start(bf16[96,1024]{1,0:T(8,128)(2,1)S(1)} %get-tuple-element.100.refs_4_), channel_id=1, source_target_pairs={{0,12},{4,0},{8,4},{12,8},{1,13},{5,1},{9,5},{13,9},{2,14},{6,2},{... | collective-permute-start | bytes 589832 | tf_op jit(solution)/shard_map/ppermute | solution.py:433
  81.2 2.0 %collective-permute-done.15.refs_2_ = bf16[192,512]{1,0:T(8,128)(2,1)S(1)} collective-permute-done((bf16[192,512]{1,0:T(8,128)(2,1)S(1)}, bf16[192,512]{1,0:T(8,128)(2,1)S(1)}, u32[]{:S(2)}, u32[]{:S(2)}) %collective-permute-start.15) | collective-permute-done | bytes 196640 | tf_op jit(solution)/shard_map/ppermute | solution.py:414
  83.3 1.1 collective-permute-start.17
  84.3 2.6 %collective-permute-done.19.refs_1_ = bf16[96,1024]{1,0:T(8,128)(2,1)S(1)} collective-permute-done((bf16[96,1024]{1,0:T(8,128)(2,1)S(1)}, bf16[96,1024]{1,0:T(8,128)(2,1)S(1)}, u32[]{:S(2)}, u32[]{:S(2)}) %collective-permute-start.19) | collective-permute-done | bytes 196640 | tf_op jit(solution)/shard_map/ppermute | solution.py:433
  87.0 1.3 %collective-permute-done.22.refs_5_ = bf16[96,1024]{1,0:T(8,128)(2,1)S(1)} collective-permute-done((bf16[96,1024]{1,0:T(8,128)(2,1)S(1)}, bf16[96,1024]{1,0:T(8,128)(2,1)S(1)}, u32[]{:S(2)}, u32[]{:S(2)}) %collective-permute-start.22) | collective-permute-done | bytes 196640 | tf_op jit(solution)/shard_map/ppermute | solution.py:433
  88.3 2.5 %collective-permute-start.23 = (bf16[96,1024]{1,0:T(8,128)(2,1)S(1)}, bf16[96,1024]{1,0:T(8,128)(2,1)S(1)}, u32[]{:S(2)}, u32[]{:S(2)}) collective-permute-start(bf16[96,1024]{1,0:T(8,128)(2,1)S(1)} %collective-permute-done.22.refs_5_), channel_id=1, source_target_pairs={{0,12},{4,0},{8,4},{12,8},{1,13},{5,1},{9,5},{13,9},{2,14},{6,2},{... | collective-permute-start | bytes 589832 | tf_op jit(solution)/shard_map/ppermute | solution.py:433
  90.8 5.7 %collective-permute-done.20.refs_2_ = bf16[96,1024]{1,0:T(8,128)(2,1)S(1)} collective-permute-done((bf16[96,1024]{1,0:T(8,128)(2,1)S(1)}, bf16[96,1024]{1,0:T(8,128)(2,1)S(1)}, u32[]{:S(2)}, u32[]{:S(2)}) %collective-permute-start.20) | collective-permute-done | bytes 196640 | tf_op jit(solution)/shard_map/ppermute | solution.py:433
  96.5 3.4 %collective-permute-done.23.refs_6_ = bf16[96,1024]{1,0:T(8,128)(2,1)S(1)} collective-permute-done((bf16[96,1024]{1,0:T(8,128)(2,1)S(1)}, bf16[96,1024]{1,0:T(8,128)(2,1)S(1)}, u32[]{:S(2)}, u32[]{:S(2)}) %collective-permute-start.23) | collective-permute-done | bytes 196640 | tf_op jit(solution)/shard_map/ppermute | solution.py:433
  100.6 2.3 %inputs.1 = bf16[512,1024]{1,0:T(8,128)(2,1)} custom-call(bf16[192,512]{1,0:T(8,128)(2,1)S(1)} %get-tuple-element.84.refs_0_, bf16[192,512]{1,0:T(8,128)(2,1)S(1)} %collective-permute-done.14.refs_1_, bf16[192,512]{1,0:T(8,128)(2,1)S(1)} %collective-permute-done.15.refs_2_, bf16[192,512]{1,0:T(8,128)(2,1)S(1)} %collective-permute-done.16.refs_3_, ...), custom_call_target="tpu_custom_call" | custom-call | flops 805306368 | bytes 4194304 | tf_op jit(solution)/shard_map/inputs/pallas_call | solution.py:362
  102.9 2.7 %collective-permute-done.21.refs_3_ = bf16[96,1024]{1,0:T(8,128)(2,1)S(1)} collective-permute-done((bf16[96,1024]{1,0:T(8,128)(2,1)S(1)}, bf16[96,1024]{1,0:T(8,128)(2,1)S(1)}, u32[]{:S(2)}, u32[]{:S(2)}) %collective-permute-start.21) | collective-permute-done | bytes 196640 | tf_op jit(solution)/shard_map/ppermute | solution.py:433
  105.6 2.4 %collective-permute-done.24.refs_7_ = bf16[96,1024]{1,0:T(8,128)(2,1)S(1)} collective-permute-done((bf16[96,1024]{1,0:T(8,128)(2,1)S(1)}, bf16[96,1024]{1,0:T(8,128)(2,1)S(1)}, u32[]{:S(2)}, u32[]{:S(2)}) %collective-permute-start.24) | collective-permute-done | bytes 196640 | tf_op jit(solution)/shard_map/ppermute | solution.py:433
  108.0 2.3 %place.1 = f32[192,4096]{1,0:T(8,128)} custom-call(bf16[96,1024]{1,0:T(8,128)(2,1)S(1)} %get-tuple-element.96.refs_0_, bf16[96,1024]{1,0:T(8,128)(2,1)S(1)} %collective-permute-done.19.refs_1_, bf16[96,1024]{1,0:T(8,128)(2,1)S(1)} %collective-permute-done.20.refs_2_, bf16[96,1024]{1,0:T(8,128)(2,1)S(1)} %collective-permute-done.21.refs_3_, ...), custom_call_target="tpu_custom_call" | custom-call | bytes 6291456 | tf_op jit(solution)/shard_map/place/pallas_call | solution.py:398
  (63 shorter events, 10.6 us)
Async XLA Ops:
  0.6 13.2 %copy-start = (f32[64]{0:T(128)S(1)}, f32[64]{0:T(128)}, u32[]{:S(2)}) copy-start(f32[64]{0:T(128)} %param.13) | copy-start | bytes 772
  0.6 5.4 %collective-permute-start.1 = (bf16[512,1024]{1,0:T(8,128)(2,1)}, bf16[512,1024]{1,0:T(8,128)(2,1)S(1)}, u32[]{:S(2)}, u32[]{:S(2)}) collective-permute-start(bf16[512,1024]{1,0:T(8,128)(2,1)} %values_ref.1), channel_id=1, source_target_pairs={{0,1},{1,0},{2,3},{3,2},{4,5},{5,4},{6,7},{7,6},{8,9},{9,8},{10,11... | collective-permute-start | bytes 3145736 | tf_op jit(solution)/shard_map/ppermute | solution.py:414
  1.2 26.6 %collective-permute-start = (bf16[512,1024]{1,0:T(8,128)(2,1)}, bf16[512,1024]{1,0:T(8,128)(2,1)}, u32[]{:S(2)}, u32[]{:S(2)}) collective-permute-start(bf16[512,1024]{1,0:T(8,128)(2,1)} %values_ref.1), channel_id=1, source_target_pairs={{0,2},{1,3},{2,0},{3,1},{4,6},{5,7},{6,4},{7,5},{8,10},{9,11},{10,... | collective-permute-start | bytes 3145736 | tf_op jit(solution)/shard_map/ppermute | solution.py:414
  6.0 5.8 %copy-start.1 = (bf16[3,64,4096]{2,1,0:T(8,128)(2,1)S(1)}, bf16[3,64,4096]{2,1,0:T(8,128)(2,1)}, u32[]{:S(2)}) copy-start(bf16[3,64,4096]{2,1,0:T(8,128)(2,1)} %param.11) | copy-start | bytes 4718596
  7.0 37.1 %all-to-all-start = ((bf16[4,512,256]{2,1,0:T(8,128)(2,1)}), bf16[4,512,256]{2,1,0:T(8,128)(2,1)S(1)}, u32[]{:S(2)}, u32[]{:S(2)}) async-start(bf16[4,512,256]{2,1,0:T(8,128)(2,1)} %copy-done.2), calls=%async_computation | async-start | bytes 2097152 | tf_op jit(solution)/shard_map/all_to_all | solution.py:485
  12.9 4.1 %collective-permute-start.2 = (bf16[192,1024]{1,0:T(8,128)(2,1)}, bf16[192,1024]{1,0:T(8,128)(2,1)S(1)}, u32[]{:S(2)}, u32[]{:S(2)}) collective-permute-start(bf16[192,1024]{1,0:T(8,128)(2,1)} %get-tuple-element.107), channel_id=1, source_target_pairs={{0,1},{1,0},{2,3},{3,2},{4,5},{5,4},{6,7},{7,6},{8,9},{9,8},{10,11... | collective-permute-start | bytes 1179656 | tf_op jit(solution)/shard_map/ppermute | solution.py:414
  27.8 2.9 %copy-start.8 = (f32[64,512]{1,0:T(8,128)S(1)}, f32[64,512]{1,0:T(8,128)}, u32[]{:S(2)}) copy-start(f32[64,512]{1,0:T(8,128)} %filter_ref) | copy-start | bytes 393220
  27.8 2.9 %collective-permute-start.3 = (bf16[512,1024]{1,0:T(8,128)(2,1)}, bf16[512,1024]{1,0:T(8,128)(2,1)S(1)}, u32[]{:S(2)}, u32[]{:S(2)}) collective-permute-start(bf16[512,1024]{1,0:T(8,128)(2,1)} %collective-permute-done.refs_0_), channel_id=1, source_target_pairs={{0,1},{1,0},{2,3},{3,2},{4,5},{5,4},{6,7},{7,6},{8,9},{9,8},{10,11... | collective-permute-start | bytes 3145736 | tf_op jit(solution)/shard_map/ppermute | solution.py:414
  31.9 8.6 %collective-permute-start.4 = (bf16[80,512]{1,0:T(8,128)(2,1)S(1)}, bf16[80,512]{1,0:T(8,128)(2,1)S(1)}, u32[]{:S(2)}, u32[]{:S(2)}) collective-permute-start(bf16[80,512]{1,0:T(8,128)(2,1)S(1)} %get-tuple-element.59), channel_id=1, source_target_pairs={{0,4},{4,0},{8,12},{12,8},{1,5},{5,1},{9,13},{13,9},{2,6},{6,2},{1... | collective-permute-start | bytes 245768 | tf_op jit(solution)/shard_map/ppermute | solution.py:414
  33.7 10.4 %collective-permute-start.5 = (bf16[80,512]{1,0:T(8,128)(2,1)S(1)}, bf16[80,512]{1,0:T(8,128)(2,1)S(1)}, u32[]{:S(2)}, u32[]{:S(2)}) collective-permute-start(bf16[80,512]{1,0:T(8,128)(2,1)S(1)} %get-tuple-element.60), channel_id=1, source_target_pairs={{0,8},{4,12},{8,0},{12,4},{1,9},{5,13},{9,1},{13,5},{2,10},{6,14},... | collective-permute-start | bytes 245768 | tf_op jit(solution)/shard_map/ppermute | solution.py:414
  36.3 7.8 %collective-permute-start.6 = (bf16[80,512]{1,0:T(8,128)(2,1)S(1)}, bf16[80,512]{1,0:T(8,128)(2,1)S(1)}, u32[]{:S(2)}, u32[]{:S(2)}) collective-permute-start(bf16[80,512]{1,0:T(8,128)(2,1)S(1)} %get-tuple-element.61), channel_id=1, source_target_pairs={{0,12},{4,8},{8,4},{12,0},{1,13},{5,9},{9,5},{13,1},{2,14},{6,10},... | collective-permute-start | bytes 245768 | tf_op jit(solution)/shard_map/ppermute | solution.py:414
  40.5 5.0 %copy-start.12 = (bf16[80,512]{1,0:T(8,128)(2,1)}, bf16[80,512]{1,0:T(8,128)(2,1)S(1)}, u32[]{:S(2)}) copy-start(bf16[80,512]{1,0:T(8,128)(2,1)S(1)} %collective-permute-done.4.refs_2_) | copy-start | bytes 245764
  44.1 29.1 %collective-permute-start.7 = (bf16[2048,256]{1,0:T(8,128)(2,1)S(1)}, bf16[2048,256]{1,0:T(8,128)(2,1)S(1)}, u32[]{:S(2)}, u32[]{:S(2)}) collective-permute-start(bf16[2048,256]{1,0:T(8,128)(2,1)S(1)} %bitcast.9), channel_id=1, source_target_pairs={{0,2},{1,3},{2,0},{3,1},{4,6},{5,7},{6,4},{7,5},{8,10},{9,11},{10,... | collective-permute-start | bytes 3145736 | tf_op jit(solution)/shard_map/ppermute | solution.py:414
  51.4 13.9 %collective-permute-start.9 = (bf16[48,2432]{1,0:T(8,128)(2,1)}, bf16[48,2432]{1,0:T(8,128)(2,1)S(1)}, u32[]{:S(2)}, u32[]{:S(2)}) collective-permute-start(bf16[48,2432]{1,0:T(8,128)(2,1)} %get-tuple-element.71), channel_id=1, source_target_pairs={{0,8},{4,12},{8,0},{12,4},{1,9},{5,13},{9,1},{13,5},{2,10},{6,14},... | collective-permute-start | bytes 700424 | tf_op jit(solution)/shard_map/ppermute | solution.py:414
  53.9 12.8 %collective-permute-start.8 = (bf16[48,2432]{1,0:T(8,128)(2,1)}, bf16[48,2432]{1,0:T(8,128)(2,1)S(1)}, u32[]{:S(2)}, u32[]{:S(2)}) collective-permute-start(bf16[48,2432]{1,0:T(8,128)(2,1)} %get-tuple-element.70), channel_id=1, source_target_pairs={{0,4},{4,0},{8,12},{12,8},{1,5},{5,1},{9,13},{13,9},{2,6},{6,2},{1... | collective-permute-start | bytes 700424 | tf_op jit(solution)/shard_map/ppermute | solution.py:414
  54.5 12.1 %collective-permute-start.10 = (bf16[48,2432]{1,0:T(8,128)(2,1)}, bf16[48,2432]{1,0:T(8,128)(2,1)S(1)}, u32[]{:S(2)}, u32[]{:S(2)}) collective-permute-start(bf16[48,2432]{1,0:T(8,128)(2,1)} %get-tuple-element.72), channel_id=1, source_target_pairs={{4,8},{8,4},{5,9},{9,5},{6,10},{10,6},{7,11},{11,7},{20,24},{24,20... | collective-permute-start | bytes 700424 | tf_op jit(solution)/shard_map/ppermute | solution.py:505
  65.3 7.9 %collective-permute-start.11 = (bf16[48,2432]{1,0:T(8,128)(2,1)S(1)}, bf16[48,2432]{1,0:T(8,128)(2,1)S(1)}, u32[]{:S(2)}, u32[]{:S(2)}) collective-permute-start(bf16[48,2432]{1,0:T(8,128)(2,1)S(1)} %collective-permute-done.9.refs_2_), channel_id=1, source_target_pairs={{4,0},{8,12},{5,1},{9,13},{6,2},{10,14},{7,3},{11,15},{20,16},{24,... | collective-permute-start | bytes 700424 | tf_op jit(solution)/shard_map/ppermute | solution.py:506
  66.6 6.7 %collective-permute-start.12 = (bf16[2048,256]{1,0:T(8,128)(2,1)S(1)}, bf16[2048,256]{1,0:T(8,128)(2,1)S(1)}, u32[]{:S(2)}, u32[]{:S(2)}) collective-permute-start(bf16[2048,256]{1,0:T(8,128)(2,1)S(1)} %bitcast.10), channel_id=1, source_target_pairs={{0,1},{1,0},{2,3},{3,2},{4,5},{5,4},{6,7},{7,6},{8,9},{9,8},{10,11... | collective-permute-start | bytes 3145736 | tf_op jit(solution)/shard_map/ppermute | solution.py:414
  73.2 2.7 %collective-permute-start.13 = (bf16[2048,256]{1,0:T(8,128)(2,1)S(1)}, bf16[2048,256]{1,0:T(8,128)(2,1)S(1)}, u32[]{:S(2)}, u32[]{:S(2)}) collective-permute-start(bf16[2048,256]{1,0:T(8,128)(2,1)S(1)} %collective-permute-done.7.refs_7_), channel_id=1, source_target_pairs={{0,1},{1,0},{2,3},{3,2},{4,5},{5,4},{6,7},{7,6},{8,9},{9,8},{10,11... | collective-permute-start | bytes 3145736 | tf_op jit(solution)/shard_map/ppermute | solution.py:414
  75.5 7.8 %copy-start.11 = (bf16[192,1024]{1,0:T(8,128)(2,1)S(1)}, bf16[192,1024]{1,0:T(8,128)(2,1)}, u32[]{:S(2)}) copy-start(bf16[192,1024]{1,0:T(8,128)(2,1)} %get-tuple-element.91) | copy-start | bytes 1179652
  75.5 8.9 %copy-start.10 = (bf16[192,1024]{1,0:T(8,128)(2,1)S(1)}, bf16[192,1024]{1,0:T(8,128)(2,1)}, u32[]{:S(2)}) copy-start(bf16[192,1024]{1,0:T(8,128)(2,1)} %get-tuple-element.92) | copy-start | bytes 1179652
  76.3 7.0 %collective-permute-start.15 = (bf16[192,512]{1,0:T(8,128)(2,1)S(1)}, bf16[192,512]{1,0:T(8,128)(2,1)S(1)}, u32[]{:S(2)}, u32[]{:S(2)}) collective-permute-start(bf16[192,512]{1,0:T(8,128)(2,1)S(1)} %get-tuple-element.84.refs_0_), channel_id=1, source_target_pairs={{0,2},{1,3},{2,0},{3,1},{4,6},{5,7},{6,4},{7,5},{8,10},{9,11},{10,... | collective-permute-start | bytes 589832 | tf_op jit(solution)/shard_map/ppermute | solution.py:414
  77.4 9.6 %collective-permute-start.19 = (bf16[96,1024]{1,0:T(8,128)(2,1)S(1)}, bf16[96,1024]{1,0:T(8,128)(2,1)S(1)}, u32[]{:S(2)}, u32[]{:S(2)}) collective-permute-start(bf16[96,1024]{1,0:T(8,128)(2,1)S(1)} %get-tuple-element.96.refs_0_), channel_id=1, source_target_pairs={{0,4},{4,8},{8,12},{12,0},{1,5},{5,9},{9,13},{13,1},{2,6},{6,10},{... | collective-permute-start | bytes 589832 | tf_op jit(solution)/shard_map/ppermute | solution.py:433
  77.4 10.9 %collective-permute-start.22 = (bf16[96,1024]{1,0:T(8,128)(2,1)S(1)}, bf16[96,1024]{1,0:T(8,128)(2,1)S(1)}, u32[]{:S(2)}, u32[]{:S(2)}) collective-permute-start(bf16[96,1024]{1,0:T(8,128)(2,1)S(1)} %get-tuple-element.100.refs_4_), channel_id=1, source_target_pairs={{0,12},{4,0},{8,4},{12,8},{1,13},{5,1},{9,5},{13,9},{2,14},{6,2},{... | collective-permute-start | bytes 589832 | tf_op jit(solution)/shard_map/ppermute | solution.py:433
  81.2 9.6 %collective-permute-start.14 = (bf16[192,512]{1,0:T(8,128)(2,1)S(1)}, bf16[192,512]{1,0:T(8,128)(2,1)S(1)}, u32[]{:S(2)}, u32[]{:S(2)}) collective-permute-start(bf16[192,512]{1,0:T(8,128)(2,1)S(1)} %get-tuple-element.84.refs_0_), channel_id=1, source_target_pairs={{0,1},{1,0},{2,3},{3,2},{4,5},{5,4},{6,7},{7,6},{8,9},{9,8},{10,11... | collective-permute-start | bytes 589832 | tf_op jit(solution)/shard_map/ppermute | solution.py:414
  83.3 17.2 %collective-permute-start.17 = (bf16[192,1024]{1,0:T(8,128)(2,1)S(1)}, bf16[192,1024]{1,0:T(8,128)(2,1)S(1)}, u32[]{:S(2)}, u32[]{:S(2)}) collective-permute-start(bf16[192,1024]{1,0:T(8,128)(2,1)S(1)} %copy-done.11), channel_id=1, source_target_pairs={{0,2},{1,3},{2,0},{3,1},{4,6},{5,7},{6,4},{7,5},{8,10},{9,11},{10,... | collective-permute-start | bytes 1179656 | tf_op jit(solution)/shard_map/ppermute | solution.py:414
  84.3 16.3 %collective-permute-start.18 = (bf16[192,1024]{1,0:T(8,128)(2,1)S(1)}, bf16[192,1024]{1,0:T(8,128)(2,1)S(1)}, u32[]{:S(2)}, u32[]{:S(2)}) collective-permute-start(bf16[192,1024]{1,0:T(8,128)(2,1)S(1)} %copy-done.10), channel_id=1, source_target_pairs={{0,3},{1,2},{2,1},{3,0},{4,7},{5,6},{6,5},{7,4},{8,11},{9,10},{10,... | collective-permute-start | bytes 1179656 | tf_op jit(solution)/shard_map/ppermute | solution.py:414
  87.0 9.5 %collective-permute-start.20 = (bf16[96,1024]{1,0:T(8,128)(2,1)S(1)}, bf16[96,1024]{1,0:T(8,128)(2,1)S(1)}, u32[]{:S(2)}, u32[]{:S(2)}) collective-permute-start(bf16[96,1024]{1,0:T(8,128)(2,1)S(1)} %collective-permute-done.19.refs_1_), channel_id=1, source_target_pairs={{0,4},{4,8},{8,12},{12,0},{1,5},{5,9},{9,13},{13,1},{2,6},{6,10},{... | collective-permute-start | bytes 589832 | tf_op jit(solution)/shard_map/ppermute | solution.py:433
  88.3 11.6 %collective-permute-start.23 = (bf16[96,1024]{1,0:T(8,128)(2,1)S(1)}, bf16[96,1024]{1,0:T(8,128)(2,1)S(1)}, u32[]{:S(2)}, u32[]{:S(2)}) collective-permute-start(bf16[96,1024]{1,0:T(8,128)(2,1)S(1)} %collective-permute-done.22.refs_5_), channel_id=1, source_target_pairs={{0,12},{4,0},{8,4},{12,8},{1,13},{5,1},{9,5},{13,9},{2,14},{6,2},{... | collective-permute-start | bytes 589832 | tf_op jit(solution)/shard_map/ppermute | solution.py:433
  90.8 9.6 %collective-permute-start.16 = (bf16[192,512]{1,0:T(8,128)(2,1)S(1)}, bf16[192,512]{1,0:T(8,128)(2,1)S(1)}, u32[]{:S(2)}, u32[]{:S(2)}) collective-permute-start(bf16[192,512]{1,0:T(8,128)(2,1)S(1)} %collective-permute-done.15.refs_2_), channel_id=1, source_target_pairs={{0,1},{1,0},{2,3},{3,2},{4,5},{5,4},{6,7},{7,6},{8,9},{9,8},{10,11... | collective-permute-start | bytes 589832 | tf_op jit(solution)/shard_map/ppermute | solution.py:414
  96.5 9.1 %collective-permute-start.21 = (bf16[96,1024]{1,0:T(8,128)(2,1)S(1)}, bf16[96,1024]{1,0:T(8,128)(2,1)S(1)}, u32[]{:S(2)}, u32[]{:S(2)}) collective-permute-start(bf16[96,1024]{1,0:T(8,128)(2,1)S(1)} %collective-permute-done.20.refs_2_), channel_id=1, source_target_pairs={{0,4},{4,8},{8,12},{12,0},{1,5},{5,9},{9,13},{13,1},{2,6},{6,10},{... | collective-permute-start | bytes 589832 | tf_op jit(solution)/shard_map/ppermute | solution.py:433
  99.9 8.1 %collective-permute-start.24 = (bf16[96,1024]{1,0:T(8,128)(2,1)S(1)}, bf16[96,1024]{1,0:T(8,128)(2,1)S(1)}, u32[]{:S(2)}, u32[]{:S(2)}) collective-permute-start(bf16[96,1024]{1,0:T(8,128)(2,1)S(1)} %collective-permute-done.23.refs_6_), channel_id=1, source_target_pairs={{0,12},{4,0},{8,4},{12,8},{1,13},{5,1},{9,5},{13,9},{2,14},{6,2},{... | collective-permute-start | bytes 589832 | tf_op jit(solution)/shard_map/ppermute | solution.py:433
  (9 other events, 9.9 us)

commit v4 on v3

--- a/solution.py
+++ b/solution.py
@@ -151,7 +151,9 @@
                     for n in range(cuts)
                 ]
                 results[q, z, start : start + group, :] = jnp.concatenate(tiles, axis=1)
-    gain = gain_ref[...]
+    down = lax.broadcasted_iota(jnp.int32, (chans, chans), 0)
+    along = lax.broadcasted_iota(jnp.int32, (chans, chans), 1)
+    gain = jnp.sum(jnp.where(down == along, gain_ref[...], 0.0), axis=1, keepdims=True)
     for z in range(blocks):
         conv_out = results[0, z] + gain * series[1, z]
         grad_gated = results[1, z] + gain * series[2, z]
@@ -264,7 +266,7 @@
     for m in range(blocks):
         value = grad_refs[m][:, :tokens]
         if m == blocks - 1:
-            value = value + grad_refs[blocks][:, :tokens]
+            value = jnp.where(middle, value, grad_refs[blocks][:, :tokens])
         left_ref[m * rows : (m + 1) * rows, :] = value
         for k in range(kinds):
             to = pl.multiple_of(k * share * blocks + (place ^ m) * share, share)
@@ -477,7 +479,7 @@
         features = [swap(activations, "chan", m) for m in range(slabs)]
 
     along = [out_grad.astype(F32), long_filter]
-    gain = share_of(skip_gain, 0)[:, None]
+    gain = share_of(skip_gain, 0)[None, :]
 
     weight_cols = [lax.dynamic_slice_in_dim(weight_rows, (mine ^ m) * width, width, 1) for m in range(slabs)]
     if line:
@@ -502,8 +504,8 @@
 
     if line:
         messages = [messages[0], swap(messages[1], "ctx", 1), swap(messages[2], "ctx", 2), messages[3]]
-        messages[3] = lax.ppermute(messages[3], "ctx", [(1, 2), (2, 1)])
-        messages.append(lax.ppermute(messages[2], "ctx", [(1, 0), (2, 3)]))
+        messages[3] = lax.ppermute(messages[3], "ctx", [(1, 2), (2, 1), (0, 0), (3, 3)])
+        messages.append(swap(messages[2], "ctx", 1))
         far, messages = lax.optimization_barrier((turned[2], messages))
         far = swap(far, "chan", 1)
         left, some, grad_proj, grad_filter = weight_products(messages, turned, kinds, share)

time: 111 us -> 108 us (0.973)
  waiting for transfers between devices: 57 us -> 55.2 us
    ppermute x2 -> x1, waiting for transfers between devices: 6.56 us -> 0.01 us  [per_device(): lax.ppermute(messages[3], 'ctx', [(1, 2), (2, 1), (0, 0), (3, 3)])]
    ppermute x17 -> x18, waiting for transfers between devices: 32.3 us -> 37.1 us  [swap(): return lax.ppermute(values, axis, [(i, i ^ mask) for i in range(size)])]
    ppermute x17 -> x18, starting transfers between devices: 13.6 us -> 13.6 us  [swap(): return lax.ppermute(values, axis, [(i, i ^ mask) for i in range(size)])]
  transfers between devices with their start and end apart: 26 -> 26, of which waited for: 15 -> 15; matrix products, arithmetic and copies ran while one was open for 2% -> 2% of each run, Pallas kernels for 11% -> 12%
where the time goes in v4:
time: 108 us
  waiting for transfers between devices  55.2 us (51%)
  starting transfers between devices  26.9 us (25%)
  Pallas kernels  15.2 us (14%)
  local copies, waits for them, and re-layouts  8.92 us (8%)
    ppermute x18, waiting for transfers between devices, swap(): return lax.ppermute(values, axis, [(i, i ^ mask) for i in range(size)])  37.1 us
    ppermute x6, waiting for transfers between devices, ring(): lax.ppermute(found[-1], 'ctx', [(i, (i + step) % size) for i in range(siz...  18.1 us
    ppermute x18, starting transfers between devices, swap(): return lax.ppermute(values, axis, [(i, i ^ mask) for i in range(size)])  13.6 us
    unnamed x30, local copies, waits for them, and re-layouts  7.26 us
    ppermute x6, starting transfers between devices, ring(): lax.ppermute(found[-1], 'ctx', [(i, (i + step) % size) for i in range(siz...  6.83 us
    pallas_call x1, Pallas kernels, convolve(): pl.pallas_call(functools.partial(conv_kernel, blocks, chans, group, token...  5.87 us
    all_to_all x1, starting transfers between devices, per_device(): lax.all_to_all(turned, 'ctx', split_axis=0, concat_axis=0)  4.87 us
    pallas_call x3, Pallas kernels, project(): pl.pallas_call(body, out_shape=shape, in_specs=[VMEM] * (len(along) + 1 +...  2.99 us
  transfers between devices with their start and end apart: 26, of which 15 were waited for; matrix products, arithmetic and copies ran while one was open for 2% of the time, Pallas kernels for 12%

profile of v4, /device:TPU:0, one launch (start us, length us, event | category | flops | bytes accessed | tf_op | source)
XLA Modules:
  0.0 107.9 jit_solution(14583689985463198220)
XLA Ops:
  1.2 2.6 %collective-permute-start = (bf16[512,1024]{1,0:T(8,128)(2,1)}, bf16[512,1024]{1,0:T(8,128)(2,1)}, u32[]{:S(2)}, u32[]{:S(2)}) collective-permute-start(bf16[512,1024]{1,0:T(8,128)(2,1)} %values_ref.1), channel_id=1, source_target_pairs={{0,2},{1,3},{2,0},{3,1},{4,6},{5,7},{6,4},{7,5},{8,10},{9,11},{10,... | collective-permute-start | bytes 3145736 | tf_op jit(solution)/shard_map/ppermute | solution.py:416
  3.7 1.3 %copy-done.3 = bf16[512,1024]{1,0:T(8,128)(2,1)S(1)} copy-done((bf16[512,1024]{1,0:T(8,128)(2,1)S(1)}, bf16[512,1024]{1,0:T(8,128)(2,1)}, u32[]{:S(2)}) %copy-start.3) | copy-done | bytes 1048600
  7.0 4.9 %all-to-all-start = ((bf16[4,512,256]{2,1,0:T(8,128)(2,1)}), bf16[4,512,256]{2,1,0:T(8,128)(2,1)S(1)}, u32[]{:S(2)}, u32[]{:S(2)}) async-start(bf16[4,512,256]{2,1,0:T(8,128)(2,1)} %copy-done.2), calls=%async_computation | async-start | bytes 2097152 | tf_op jit(solution)/shard_map/all_to_all | solution.py:487
  11.9 1.1 constant_dynamic-slice_fusion
  14.4 1.2 %copy-done.4 = bf16[512,1024]{1,0:T(8,128)(2,1)S(1)} copy-done((bf16[512,1024]{1,0:T(8,128)(2,1)S(1)}, bf16[512,1024]{1,0:T(8,128)(2,1)}, u32[]{:S(2)}) %copy-start.4) | copy-done | bytes 1048600
  15.6 1.2 %copy-done.6 = bf16[512,1024]{1,0:T(8,128)(2,1)S(1)} copy-done((bf16[512,1024]{1,0:T(8,128)(2,1)S(1)}, bf16[512,1024]{1,0:T(8,128)(2,1)}, u32[]{:S(2)}) %copy-start.6) | copy-done | bytes 1048600
  17.6 10.2 %collective-permute-done.refs_0_ = bf16[512,1024]{1,0:T(8,128)(2,1)} collective-permute-done((bf16[512,1024]{1,0:T(8,128)(2,1)}, bf16[512,1024]{1,0:T(8,128)(2,1)}, u32[]{:S(2)}, u32[]{:S(2)}) %collective-permute-start) | collective-permute-done | bytes 1048608 | tf_op jit(solution)/shard_map/ppermute | solution.py:416
  27.8 1.7 %project.4.sum_ref = f32[512,192]{1,0:T(8,128)S(1)} custom-call(bf16[192,4096]{1,0:T(8,128)(2,1)S(1)} %bitcast.7, f32[512,192]{1,0:T(8,128)S(1)} %project.3.sum_ref, bf16[512,1024]{1,0:T(8,128)(2,1)} %collective-permute-done.refs_0_), custom_call_target="tpu_custom_call" | custom-call | flops 201326592 | bytes 1048576 | tf_op jit(solution)/shard_map/project/pallas_call | solution.py:244
  29.5 1.1 %collective-permute-done.3.refs_0_ = bf16[512,1024]{1,0:T(8,128)(2,1)S(1)} collective-permute-done((bf16[512,1024]{1,0:T(8,128)(2,1)}, bf16[512,1024]{1,0:T(8,128)(2,1)S(1)}, u32[]{:S(2)}, u32[]{:S(2)}) %collective-permute-start.3) | collective-permute-done | bytes 1048608 | tf_op jit(solution)/shard_map/ppermute | solution.py:416
  31.9 1.8 %collective-permute-start.4 = (bf16[80,512]{1,0:T(8,128)(2,1)S(1)}, bf16[80,512]{1,0:T(8,128)(2,1)S(1)}, u32[]{:S(2)}, u32[]{:S(2)}) collective-permute-start(bf16[80,512]{1,0:T(8,128)(2,1)S(1)} %get-tuple-element.59), channel_id=1, source_target_pairs={{0,4},{4,0},{8,12},{12,8},{1,5},{5,1},{9,13},{13,9},{2,6},{6,2},{1... | collective-permute-start | bytes 245768 | tf_op jit(solution)/shard_map/ppermute | solution.py:416
  33.7 2.6 %collective-permute-start.5 = (bf16[80,512]{1,0:T(8,128)(2,1)S(1)}, bf16[80,512]{1,0:T(8,128)(2,1)S(1)}, u32[]{:S(2)}, u32[]{:S(2)}) collective-permute-start(bf16[80,512]{1,0:T(8,128)(2,1)S(1)} %get-tuple-element.60), channel_id=1, source_target_pairs={{0,8},{4,12},{8,0},{12,4},{1,9},{5,13},{9,1},{13,5},{2,10},{6,14},... | collective-permute-start | bytes 245768 | tf_op jit(solution)/shard_map/ppermute | solution.py:416
  36.3 4.2 %collective-permute-done.4.refs_2_ = bf16[80,512]{1,0:T(8,128)(2,1)S(1)} collective-permute-done((bf16[80,512]{1,0:T(8,128)(2,1)S(1)}, bf16[80,512]{1,0:T(8,128)(2,1)S(1)}, u32[]{:S(2)}, u32[]{:S(2)}) %collective-permute-start.4) | collective-permute-done | bytes 81952 | tf_op jit(solution)/shard_map/ppermute | solution.py:416
  40.5 3.6 %collective-permute-done.5.refs_3_ = bf16[80,512]{1,0:T(8,128)(2,1)S(1)} collective-permute-done((bf16[80,512]{1,0:T(8,128)(2,1)S(1)}, bf16[80,512]{1,0:T(8,128)(2,1)S(1)}, u32[]{:S(2)}, u32[]{:S(2)}) %collective-permute-start.5) | collective-permute-done | bytes 81952 | tf_op jit(solution)/shard_map/ppermute | solution.py:416
  44.8 5.9 %conv.1 = (bf16[48,2432]{1,0:T(8,128)(2,1)}, bf16[48,2432]{1,0:T(8,128)(2,1)}, bf16[48,2432]{1,0:T(8,128)(2,1)}, bf16[48,2432]{1,0:T(8,128)(2,1)}) custom-call(f32[1,16]{1,0:T(1,128)} %dynamic-slice_bitcast_fusion.refs_0_, bf16[80,512]{1,0:T(8,128)(2,1)} %copy-done.9, bf16[80,512]{1,0:T(8,128)(2,1)} %copy-done.12, bf16[80,512]{1,0:T(8,128)(2,1)} %copy-done.13, ...), custom_call_target="tpu_custom_call" | custom-call | flops 962592768 | bytes 4194304 | tf_op jit(solution)/shard_map/conv/pallas_call | solution.py:184
  50.6 2.4 %collective-permute-start.9 = (bf16[48,2432]{1,0:T(8,128)(2,1)}, bf16[48,2432]{1,0:T(8,128)(2,1)S(1)}, u32[]{:S(2)}, u32[]{:S(2)}) collective-permute-start(bf16[48,2432]{1,0:T(8,128)(2,1)} %get-tuple-element.71), channel_id=1, source_target_pairs={{0,8},{4,12},{8,0},{12,4},{1,9},{5,13},{9,1},{13,5},{2,10},{6,14},... | collective-permute-start | bytes 700424 | tf_op jit(solution)/shard_map/ppermute | solution.py:416
  53.8 1.6 %collective-permute-start.10 = (bf16[48,2432]{1,0:T(8,128)(2,1)}, bf16[48,2432]{1,0:T(8,128)(2,1)S(1)}, u32[]{:S(2)}, u32[]{:S(2)}) collective-permute-start(bf16[48,2432]{1,0:T(8,128)(2,1)} %get-tuple-element.72), channel_id=1, source_target_pairs={{4,8},{8,4},{0,0},{12,12},{5,9},{9,5},{1,1},{13,13},{6,10},{10,6},... | collective-permute-start | bytes 700424 | tf_op jit(solution)/shard_map/ppermute | solution.py:507
  55.4 9.3 %collective-permute-done.9.refs_2_ = bf16[48,2432]{1,0:T(8,128)(2,1)S(1)} collective-permute-done((bf16[48,2432]{1,0:T(8,128)(2,1)}, bf16[48,2432]{1,0:T(8,128)(2,1)S(1)}, u32[]{:S(2)}, u32[]{:S(2)}) %collective-permute-start.9) | collective-permute-done | bytes 233504 | tf_op jit(solution)/shard_map/ppermute | solution.py:416
  64.7 6.0 %collective-permute-done.11.refs_4_ = bf16[48,2432]{1,0:T(8,128)(2,1)S(1)} collective-permute-done((bf16[48,2432]{1,0:T(8,128)(2,1)S(1)}, bf16[48,2432]{1,0:T(8,128)(2,1)S(1)}, u32[]{:S(2)}, u32[]{:S(2)}) %collective-permute-start.11) | collective-permute-done | bytes 233504 | tf_op jit(solution)/shard_map/ppermute | solution.py:416
  71.7 1.4 %products.2 = (bf16[192,2048]{1,0:T(8,128)(2,1)S(1)}, bf16[192,768]{1,0:T(8,128)(2,1)S(1)}, bf16[192,512]{1,0:T(8,128)(2,1)S(1)}, f32[64,512]{1,0:T(8,128)}) custom-call(bf16[48,2432]{1,0:T(8,128)(2,1)S(1)} %copy-done.7, bf16[48,2432]{1,0:T(8,128)(2,1)S(1)} %collective-permute-done.8.refs_1_, bf16[48,2432]{1,0:T(8,128)(2,1)S(1)} %collective-permute-done.9.refs_2_, ...), custom_call_target="tpu_custom_call" | custom-call | flops 603979776 | bytes 4194304 | tf_op jit(solution)/shard_map/products/pallas_call | solution.py:301
  73.8 1.2 %collective-permute-start.15 = (bf16[192,512]{1,0:T(8,128)(2,1)S(1)}, bf16[192,512]{1,0:T(8,128)(2,1)S(1)}, u32[]{:S(2)}, u32[]{:S(2)}) collective-permute-start(bf16[192,512]{1,0:T(8,128)(2,1)S(1)} %get-tuple-element.84.refs_0_), channel_id=1, source_target_pairs={{0,2},{1,3},{2,0},{3,1},{4,6},{5,7},{6,4},{7,5},{8,10},{9,11},{10,... | collective-permute-start | bytes 589832 | tf_op jit(solution)/shard_map/ppermute | solution.py:416
  75.0 3.8 %collective-permute-start.22 = (bf16[96,1024]{1,0:T(8,128)(2,1)S(1)}, bf16[96,1024]{1,0:T(8,128)(2,1)S(1)}, u32[]{:S(2)}, u32[]{:S(2)}) collective-permute-start(bf16[96,1024]{1,0:T(8,128)(2,1)S(1)} %get-tuple-element.100.refs_4_), channel_id=1, source_target_pairs={{0,12},{4,0},{8,4},{12,8},{1,13},{5,1},{9,5},{13,9},{2,14},{6,2},{... | collective-permute-start | bytes 589832 | tf_op jit(solution)/shard_map/ppermute | solution.py:435
  78.8 2.0 %collective-permute-done.15.refs_2_ = bf16[192,512]{1,0:T(8,128)(2,1)S(1)} collective-permute-done((bf16[192,512]{1,0:T(8,128)(2,1)S(1)}, bf16[192,512]{1,0:T(8,128)(2,1)S(1)}, u32[]{:S(2)}, u32[]{:S(2)}) %collective-permute-start.15) | collective-permute-done | bytes 196640 | tf_op jit(solution)/shard_map/ppermute | solution.py:416
  80.9 1.1 %collective-permute-start.17 = (bf16[192,1024]{1,0:T(8,128)(2,1)S(1)}, bf16[192,1024]{1,0:T(8,128)(2,1)S(1)}, u32[]{:S(2)}, u32[]{:S(2)}) collective-permute-start(bf16[192,1024]{1,0:T(8,128)(2,1)S(1)} %copy-done.11), channel_id=1, source_target_pairs={{0,2},{1,3},{2,0},{3,1},{4,6},{5,7},{6,4},{7,5},{8,10},{9,11},{10,... | collective-permute-start | bytes 1179656 | tf_op jit(solution)/shard_map/ppermute | solution.py:416
  82.0 2.6 %collective-permute-done.19.refs_1_ = bf16[96,1024]{1,0:T(8,128)(2,1)S(1)} collective-permute-done((bf16[96,1024]{1,0:T(8,128)(2,1)S(1)}, bf16[96,1024]{1,0:T(8,128)(2,1)S(1)}, u32[]{:S(2)}, u32[]{:S(2)}) %collective-permute-start.19) | collective-permute-done | bytes 196640 | tf_op jit(solution)/shard_map/ppermute | solution.py:435
  84.6 1.3 %collective-permute-done.22.refs_5_ = bf16[96,1024]{1,0:T(8,128)(2,1)S(1)} collective-permute-done((bf16[96,1024]{1,0:T(8,128)(2,1)S(1)}, bf16[96,1024]{1,0:T(8,128)(2,1)S(1)}, u32[]{:S(2)}, u32[]{:S(2)}) %collective-permute-start.22) | collective-permute-done | bytes 196640 | tf_op jit(solution)/shard_map/ppermute | solution.py:435
  85.9 2.5 %collective-permute-start.23 = (bf16[96,1024]{1,0:T(8,128)(2,1)S(1)}, bf16[96,1024]{1,0:T(8,128)(2,1)S(1)}, u32[]{:S(2)}, u32[]{:S(2)}) collective-permute-start(bf16[96,1024]{1,0:T(8,128)(2,1)S(1)} %collective-permute-done.22.refs_5_), channel_id=1, source_target_pairs={{0,12},{4,0},{8,4},{12,8},{1,13},{5,1},{9,5},{13,9},{2,14},{6,2},{... | collective-permute-start | bytes 589832 | tf_op jit(solution)/shard_map/ppermute | solution.py:435
  88.4 5.7 %collective-permute-done.20.refs_2_ = bf16[96,1024]{1,0:T(8,128)(2,1)S(1)} collective-permute-done((bf16[96,1024]{1,0:T(8,128)(2,1)S(1)}, bf16[96,1024]{1,0:T(8,128)(2,1)S(1)}, u32[]{:S(2)}, u32[]{:S(2)}) %collective-permute-start.20) | collective-permute-done | bytes 196640 | tf_op jit(solution)/shard_map/ppermute | solution.py:435
  94.1 3.4 %collective-permute-done.23.refs_6_ = bf16[96,1024]{1,0:T(8,128)(2,1)S(1)} collective-permute-done((bf16[96,1024]{1,0:T(8,128)(2,1)S(1)}, bf16[96,1024]{1,0:T(8,128)(2,1)S(1)}, u32[]{:S(2)}, u32[]{:S(2)}) %collective-permute-start.23) | collective-permute-done | bytes 196640 | tf_op jit(solution)/shard_map/ppermute | solution.py:435
  98.3 2.3 %inputs.1 = bf16[512,1024]{1,0:T(8,128)(2,1)} custom-call(bf16[192,512]{1,0:T(8,128)(2,1)S(1)} %get-tuple-element.84.refs_0_, bf16[192,512]{1,0:T(8,128)(2,1)S(1)} %collective-permute-done.14.refs_1_, bf16[192,512]{1,0:T(8,128)(2,1)S(1)} %collective-permute-done.15.refs_2_, bf16[192,512]{1,0:T(8,128)(2,1)S(1)} %collective-permute-done.16.refs_3_, ...), custom_call_target="tpu_custom_call" | custom-call | flops 805306368 | bytes 4194304 | tf_op jit(solution)/shard_map/inputs/pallas_call | solution.py:364
  100.6 2.6 %collective-permute-done.21.refs_3_ = bf16[96,1024]{1,0:T(8,128)(2,1)S(1)} collective-permute-done((bf16[96,1024]{1,0:T(8,128)(2,1)S(1)}, bf16[96,1024]{1,0:T(8,128)(2,1)S(1)}, u32[]{:S(2)}, u32[]{:S(2)}) %collective-permute-start.21) | collective-permute-done | bytes 196640 | tf_op jit(solution)/shard_map/ppermute | solution.py:435
  103.2 2.4 %collective-permute-done.24.refs_7_ = bf16[96,1024]{1,0:T(8,128)(2,1)S(1)} collective-permute-done((bf16[96,1024]{1,0:T(8,128)(2,1)S(1)}, bf16[96,1024]{1,0:T(8,128)(2,1)S(1)}, u32[]{:S(2)}, u32[]{:S(2)}) %collective-permute-start.24) | collective-permute-done | bytes 196640 | tf_op jit(solution)/shard_map/ppermute | solution.py:435
  105.6 2.3 %place.1 = f32[192,4096]{1,0:T(8,128)} custom-call(bf16[96,1024]{1,0:T(8,128)(2,1)S(1)} %get-tuple-element.96.refs_0_, bf16[96,1024]{1,0:T(8,128)(2,1)S(1)} %collective-permute-done.19.refs_1_, bf16[96,1024]{1,0:T(8,128)(2,1)S(1)} %collective-permute-done.20.refs_2_, bf16[96,1024]{1,0:T(8,128)(2,1)S(1)} %collective-permute-done.21.refs_3_, ...), custom_call_target="tpu_custom_call" | custom-call | bytes 6291456 | tf_op jit(solution)/shard_map/place/pallas_call | solution.py:400
  (62 shorter events, 9.7 us)
Async XLA Ops:
  0.6 13.2 %copy-start = (f32[64]{0:T(128)S(1)}, f32[64]{0:T(128)}, u32[]{:S(2)}) copy-start(f32[64]{0:T(128)} %param.13) | copy-start | bytes 772
  0.6 5.4 %collective-permute-start.1 = (bf16[512,1024]{1,0:T(8,128)(2,1)}, bf16[512,1024]{1,0:T(8,128)(2,1)S(1)}, u32[]{:S(2)}, u32[]{:S(2)}) collective-permute-start(bf16[512,1024]{1,0:T(8,128)(2,1)} %values_ref.1), channel_id=1, source_target_pairs={{0,1},{1,0},{2,3},{3,2},{4,5},{5,4},{6,7},{7,6},{8,9},{9,8},{10,11... | collective-permute-start | bytes 3145736 | tf_op jit(solution)/shard_map/ppermute | solution.py:416
  1.2 26.6 %collective-permute-start = (bf16[512,1024]{1,0:T(8,128)(2,1)}, bf16[512,1024]{1,0:T(8,128)(2,1)}, u32[]{:S(2)}, u32[]{:S(2)}) collective-permute-start(bf16[512,1024]{1,0:T(8,128)(2,1)} %values_ref.1), channel_id=1, source_target_pairs={{0,2},{1,3},{2,0},{3,1},{4,6},{5,7},{6,4},{7,5},{8,10},{9,11},{10,... | collective-permute-start | bytes 3145736 | tf_op jit(solution)/shard_map/ppermute | solution.py:416
  6.0 5.8 %copy-start.1 = (bf16[3,64,4096]{2,1,0:T(8,128)(2,1)S(1)}, bf16[3,64,4096]{2,1,0:T(8,128)(2,1)}, u32[]{:S(2)}) copy-start(bf16[3,64,4096]{2,1,0:T(8,128)(2,1)} %param.11) | copy-start | bytes 4718596
  7.0 37.1 %all-to-all-start = ((bf16[4,512,256]{2,1,0:T(8,128)(2,1)}), bf16[4,512,256]{2,1,0:T(8,128)(2,1)S(1)}, u32[]{:S(2)}, u32[]{:S(2)}) async-start(bf16[4,512,256]{2,1,0:T(8,128)(2,1)} %copy-done.2), calls=%async_computation | async-start | bytes 2097152 | tf_op jit(solution)/shard_map/all_to_all | solution.py:487
  12.9 4.7 %collective-permute-start.2 = (bf16[192,1024]{1,0:T(8,128)(2,1)}, bf16[192,1024]{1,0:T(8,128)(2,1)S(1)}, u32[]{:S(2)}, u32[]{:S(2)}) collective-permute-start(bf16[192,1024]{1,0:T(8,128)(2,1)} %get-tuple-element.107), channel_id=1, source_target_pairs={{0,1},{1,0},{2,3},{3,2},{4,5},{5,4},{6,7},{7,6},{8,9},{9,8},{10,11... | collective-permute-start | bytes 1179656 | tf_op jit(solution)/shard_map/ppermute | solution.py:416
  27.8 2.9 %copy-start.8 = (f32[64,512]{1,0:T(8,128)S(1)}, f32[64,512]{1,0:T(8,128)}, u32[]{:S(2)}) copy-start(f32[64,512]{1,0:T(8,128)} %filter_ref) | copy-start | bytes 393220
  27.8 2.9 %collective-permute-start.3 = (bf16[512,1024]{1,0:T(8,128)(2,1)}, bf16[512,1024]{1,0:T(8,128)(2,1)S(1)}, u32[]{:S(2)}, u32[]{:S(2)}) collective-permute-start(bf16[512,1024]{1,0:T(8,128)(2,1)} %collective-permute-done.refs_0_), channel_id=1, source_target_pairs={{0,1},{1,0},{2,3},{3,2},{4,5},{5,4},{6,7},{7,6},{8,9},{9,8},{10,11... | collective-permute-start | bytes 3145736 | tf_op jit(solution)/shard_map/ppermute | solution.py:416
  31.9 8.6 %collective-permute-start.4 = (bf16[80,512]{1,0:T(8,128)(2,1)S(1)}, bf16[80,512]{1,0:T(8,128)(2,1)S(1)}, u32[]{:S(2)}, u32[]{:S(2)}) collective-permute-start(bf16[80,512]{1,0:T(8,128)(2,1)S(1)} %get-tuple-element.59), channel_id=1, source_target_pairs={{0,4},{4,0},{8,12},{12,8},{1,5},{5,1},{9,13},{13,9},{2,6},{6,2},{1... | collective-permute-start | bytes 245768 | tf_op jit(solution)/shard_map/ppermute | solution.py:416
  33.7 10.4 %collective-permute-start.5 = (bf16[80,512]{1,0:T(8,128)(2,1)S(1)}, bf16[80,512]{1,0:T(8,128)(2,1)S(1)}, u32[]{:S(2)}, u32[]{:S(2)}) collective-permute-start(bf16[80,512]{1,0:T(8,128)(2,1)S(1)} %get-tuple-element.60), channel_id=1, source_target_pairs={{0,8},{4,12},{8,0},{12,4},{1,9},{5,13},{9,1},{13,5},{2,10},{6,14},... | collective-permute-start | bytes 245768 | tf_op jit(solution)/shard_map/ppermute | solution.py:416
  36.3 7.8 %collective-permute-start.6 = (bf16[80,512]{1,0:T(8,128)(2,1)S(1)}, bf16[80,512]{1,0:T(8,128)(2,1)S(1)}, u32[]{:S(2)}, u32[]{:S(2)}) collective-permute-start(bf16[80,512]{1,0:T(8,128)(2,1)S(1)} %get-tuple-element.61), channel_id=1, source_target_pairs={{0,12},{4,8},{8,4},{12,0},{1,13},{5,9},{9,5},{13,1},{2,14},{6,10},... | collective-permute-start | bytes 245768 | tf_op jit(solution)/shard_map/ppermute | solution.py:416
  40.5 4.3 %copy-start.12 = (bf16[80,512]{1,0:T(8,128)(2,1)}, bf16[80,512]{1,0:T(8,128)(2,1)S(1)}, u32[]{:S(2)}) copy-start(bf16[80,512]{1,0:T(8,128)(2,1)S(1)} %collective-permute-done.4.refs_2_) | copy-start | bytes 245764
  44.1 26.6 %collective-permute-start.7 = (bf16[2048,256]{1,0:T(8,128)(2,1)S(1)}, bf16[2048,256]{1,0:T(8,128)(2,1)S(1)}, u32[]{:S(2)}, u32[]{:S(2)}) collective-permute-start(bf16[2048,256]{1,0:T(8,128)(2,1)S(1)} %bitcast.9), channel_id=1, source_target_pairs={{0,2},{1,3},{2,0},{3,1},{4,6},{5,7},{6,4},{7,5},{8,10},{9,11},{10,... | collective-permute-start | bytes 3145736 | tf_op jit(solution)/shard_map/ppermute | solution.py:416
  50.6 14.0 %collective-permute-start.9 = (bf16[48,2432]{1,0:T(8,128)(2,1)}, bf16[48,2432]{1,0:T(8,128)(2,1)S(1)}, u32[]{:S(2)}, u32[]{:S(2)}) collective-permute-start(bf16[48,2432]{1,0:T(8,128)(2,1)} %get-tuple-element.71), channel_id=1, source_target_pairs={{0,8},{4,12},{8,0},{12,4},{1,9},{5,13},{9,1},{13,5},{2,10},{6,14},... | collective-permute-start | bytes 700424 | tf_op jit(solution)/shard_map/ppermute | solution.py:416
  53.1 11.6 %collective-permute-start.8 = (bf16[48,2432]{1,0:T(8,128)(2,1)}, bf16[48,2432]{1,0:T(8,128)(2,1)S(1)}, u32[]{:S(2)}, u32[]{:S(2)}) collective-permute-start(bf16[48,2432]{1,0:T(8,128)(2,1)} %get-tuple-element.70), channel_id=1, source_target_pairs={{0,4},{4,0},{8,12},{12,8},{1,5},{5,1},{9,13},{13,9},{2,6},{6,2},{1... | collective-permute-start | bytes 700424 | tf_op jit(solution)/shard_map/ppermute | solution.py:416
  53.8 10.9 %collective-permute-start.10 = (bf16[48,2432]{1,0:T(8,128)(2,1)}, bf16[48,2432]{1,0:T(8,128)(2,1)S(1)}, u32[]{:S(2)}, u32[]{:S(2)}) collective-permute-start(bf16[48,2432]{1,0:T(8,128)(2,1)} %get-tuple-element.72), channel_id=1, source_target_pairs={{4,8},{8,4},{0,0},{12,12},{5,9},{9,5},{1,1},{13,13},{6,10},{10,6},... | collective-permute-start | bytes 700424 | tf_op jit(solution)/shard_map/ppermute | solution.py:507
  64.7 6.1 %collective-permute-start.11 = (bf16[48,2432]{1,0:T(8,128)(2,1)S(1)}, bf16[48,2432]{1,0:T(8,128)(2,1)S(1)}, u32[]{:S(2)}, u32[]{:S(2)}) collective-permute-start(bf16[48,2432]{1,0:T(8,128)(2,1)S(1)} %collective-permute-done.9.refs_2_), channel_id=1, source_target_pairs={{0,4},{4,0},{8,12},{12,8},{1,5},{5,1},{9,13},{13,9},{2,6},{6,2},{1... | collective-permute-start | bytes 700424 | tf_op jit(solution)/shard_map/ppermute | solution.py:416
  64.7 6.1 %collective-permute-start.12 = (bf16[2048,256]{1,0:T(8,128)(2,1)S(1)}, bf16[2048,256]{1,0:T(8,128)(2,1)S(1)}, u32[]{:S(2)}, u32[]{:S(2)}) collective-permute-start(bf16[2048,256]{1,0:T(8,128)(2,1)S(1)} %bitcast.10), channel_id=1, source_target_pairs={{0,1},{1,0},{2,3},{3,2},{4,5},{5,4},{6,7},{7,6},{8,9},{9,8},{10,11... | collective-permute-start | bytes 3145736 | tf_op jit(solution)/shard_map/ppermute | solution.py:416
  70.8 2.7 %collective-permute-start.13 = (bf16[2048,256]{1,0:T(8,128)(2,1)S(1)}, bf16[2048,256]{1,0:T(8,128)(2,1)S(1)}, u32[]{:S(2)}, u32[]{:S(2)}) collective-permute-start(bf16[2048,256]{1,0:T(8,128)(2,1)S(1)} %collective-permute-done.7.refs_7_), channel_id=1, source_target_pairs={{0,1},{1,0},{2,3},{3,2},{4,5},{5,4},{6,7},{7,6},{8,9},{9,8},{10,11... | collective-permute-start | bytes 3145736 | tf_op jit(solution)/shard_map/ppermute | solution.py:416
  73.1 7.8 %copy-start.11 = (bf16[192,1024]{1,0:T(8,128)(2,1)S(1)}, bf16[192,1024]{1,0:T(8,128)(2,1)}, u32[]{:S(2)}) copy-start(bf16[192,1024]{1,0:T(8,128)(2,1)} %get-tuple-element.91) | copy-start | bytes 1179652
  73.1 8.9 %copy-start.10 = (bf16[192,1024]{1,0:T(8,128)(2,1)S(1)}, bf16[192,1024]{1,0:T(8,128)(2,1)}, u32[]{:S(2)}) copy-start(bf16[192,1024]{1,0:T(8,128)(2,1)} %get-tuple-element.92) | copy-start | bytes 1179652
  73.8 7.1 %collective-permute-start.15 = (bf16[192,512]{1,0:T(8,128)(2,1)S(1)}, bf16[192,512]{1,0:T(8,128)(2,1)S(1)}, u32[]{:S(2)}, u32[]{:S(2)}) collective-permute-start(bf16[192,512]{1,0:T(8,128)(2,1)S(1)} %get-tuple-element.84.refs_0_), channel_id=1, source_target_pairs={{0,2},{1,3},{2,0},{3,1},{4,6},{5,7},{6,4},{7,5},{8,10},{9,11},{10,... | collective-permute-start | bytes 589832 | tf_op jit(solution)/shard_map/ppermute | solution.py:416
  75.0 9.6 %collective-permute-start.19 = (bf16[96,1024]{1,0:T(8,128)(2,1)S(1)}, bf16[96,1024]{1,0:T(8,128)(2,1)S(1)}, u32[]{:S(2)}, u32[]{:S(2)}) collective-permute-start(bf16[96,1024]{1,0:T(8,128)(2,1)S(1)} %get-tuple-element.96.refs_0_), channel_id=1, source_target_pairs={{0,4},{4,8},{8,12},{12,0},{1,5},{5,9},{9,13},{13,1},{2,6},{6,10},{... | collective-permute-start | bytes 589832 | tf_op jit(solution)/shard_map/ppermute | solution.py:435
  75.0 10.9 %collective-permute-start.22 = (bf16[96,1024]{1,0:T(8,128)(2,1)S(1)}, bf16[96,1024]{1,0:T(8,128)(2,1)S(1)}, u32[]{:S(2)}, u32[]{:S(2)}) collective-permute-start(bf16[96,1024]{1,0:T(8,128)(2,1)S(1)} %get-tuple-element.100.refs_4_), channel_id=1, source_target_pairs={{0,12},{4,0},{8,4},{12,8},{1,13},{5,1},{9,5},{13,9},{2,14},{6,2},{... | collective-permute-start | bytes 589832 | tf_op jit(solution)/shard_map/ppermute | solution.py:435
  78.8 9.6 %collective-permute-start.14 = (bf16[192,512]{1,0:T(8,128)(2,1)S(1)}, bf16[192,512]{1,0:T(8,128)(2,1)S(1)}, u32[]{:S(2)}, u32[]{:S(2)}) collective-permute-start(bf16[192,512]{1,0:T(8,128)(2,1)S(1)} %get-tuple-element.84.refs_0_), channel_id=1, source_target_pairs={{0,1},{1,0},{2,3},{3,2},{4,5},{5,4},{6,7},{7,6},{8,9},{9,8},{10,11... | collective-permute-start | bytes 589832 | tf_op jit(solution)/shard_map/ppermute | solution.py:416
  80.9 17.2 %collective-permute-start.17 = (bf16[192,1024]{1,0:T(8,128)(2,1)S(1)}, bf16[192,1024]{1,0:T(8,128)(2,1)S(1)}, u32[]{:S(2)}, u32[]{:S(2)}) collective-permute-start(bf16[192,1024]{1,0:T(8,128)(2,1)S(1)} %copy-done.11), channel_id=1, source_target_pairs={{0,2},{1,3},{2,0},{3,1},{4,6},{5,7},{6,4},{7,5},{8,10},{9,11},{10,... | collective-permute-start | bytes 1179656 | tf_op jit(solution)/shard_map/ppermute | solution.py:416
  82.0 16.3 %collective-permute-start.18 = (bf16[192,1024]{1,0:T(8,128)(2,1)S(1)}, bf16[192,1024]{1,0:T(8,128)(2,1)S(1)}, u32[]{:S(2)}, u32[]{:S(2)}) collective-permute-start(bf16[192,1024]{1,0:T(8,128)(2,1)S(1)} %copy-done.10), channel_id=1, source_target_pairs={{0,3},{1,2},{2,1},{3,0},{4,7},{5,6},{6,5},{7,4},{8,11},{9,10},{10,... | collective-permute-start | bytes 1179656 | tf_op jit(solution)/shard_map/ppermute | solution.py:416
  84.6 9.5 %collective-permute-start.20 = (bf16[96,1024]{1,0:T(8,128)(2,1)S(1)}, bf16[96,1024]{1,0:T(8,128)(2,1)S(1)}, u32[]{:S(2)}, u32[]{:S(2)}) collective-permute-start(bf16[96,1024]{1,0:T(8,128)(2,1)S(1)} %collective-permute-done.19.refs_1_), channel_id=1, source_target_pairs={{0,4},{4,8},{8,12},{12,0},{1,5},{5,9},{9,13},{13,1},{2,6},{6,10},{... | collective-permute-start | bytes 589832 | tf_op jit(solution)/shard_map/ppermute | solution.py:435
  85.9 11.6 %collective-permute-start.23 = (bf16[96,1024]{1,0:T(8,128)(2,1)S(1)}, bf16[96,1024]{1,0:T(8,128)(2,1)S(1)}, u32[]{:S(2)}, u32[]{:S(2)}) collective-permute-start(bf16[96,1024]{1,0:T(8,128)(2,1)S(1)} %collective-permute-done.22.refs_5_), channel_id=1, source_target_pairs={{0,12},{4,0},{8,4},{12,8},{1,13},{5,1},{9,5},{13,9},{2,14},{6,2},{... | collective-permute-start | bytes 589832 | tf_op jit(solution)/shard_map/ppermute | solution.py:435
  88.4 9.6 %collective-permute-start.16 = (bf16[192,512]{1,0:T(8,128)(2,1)S(1)}, bf16[192,512]{1,0:T(8,128)(2,1)S(1)}, u32[]{:S(2)}, u32[]{:S(2)}) collective-permute-start(bf16[192,512]{1,0:T(8,128)(2,1)S(1)} %collective-permute-done.15.refs_2_), channel_id=1, source_target_pairs={{0,1},{1,0},{2,3},{3,2},{4,5},{5,4},{6,7},{7,6},{8,9},{9,8},{10,11... | collective-permute-start | bytes 589832 | tf_op jit(solution)/shard_map/ppermute | solution.py:416
  94.1 9.1 %collective-permute-start.21 = (bf16[96,1024]{1,0:T(8,128)(2,1)S(1)}, bf16[96,1024]{1,0:T(8,128)(2,1)S(1)}, u32[]{:S(2)}, u32[]{:S(2)}) collective-permute-start(bf16[96,1024]{1,0:T(8,128)(2,1)S(1)} %collective-permute-done.20.refs_2_), channel_id=1, source_target_pairs={{0,4},{4,8},{8,12},{12,0},{1,5},{5,9},{9,13},{13,1},{2,6},{6,10},{... | collective-permute-start | bytes 589832 | tf_op jit(solution)/shard_map/ppermute | solution.py:435
  97.6 8.1 %collective-permute-start.24 = (bf16[96,1024]{1,0:T(8,128)(2,1)S(1)}, bf16[96,1024]{1,0:T(8,128)(2,1)S(1)}, u32[]{:S(2)}, u32[]{:S(2)}) collective-permute-start(bf16[96,1024]{1,0:T(8,128)(2,1)S(1)} %collective-permute-done.23.refs_6_), channel_id=1, source_target_pairs={{0,12},{4,0},{8,4},{12,8},{1,13},{5,1},{9,5},{13,9},{2,14},{6,2},{... | collective-permute-start | bytes 589832 | tf_op jit(solution)/shard_map/ppermute | solution.py:435
  (9 other events, 8.5 us)

commit v5 on v4

--- a/solution.py
+++ b/solution.py
@@ -376,30 +376,57 @@
 
 def place_kernel(kinds, share, factor, *refs):
     out_ref = refs[-1]
-    blocks = (len(refs) - 1) // 2
+    some = (len(refs) - 1) // 2
+    blocks = some + 1
     place = lax.axis_index("ctx")
     slab = lax.axis_index("chan") ^ pl.program_id(0)
     width = out_ref.shape[1] // blocks
     source = pl.ds(pl.multiple_of(slab * width, width), width)
+    for i, ref in enumerate(refs[:-1]):
+        a, r = divmod(i, some)
+        sender = lax.rem(place + (r if a else blocks - r), blocks)
+        columns = pl.ds(pl.multiple_of(sender * width, width), width)
+        for b in range(2):
+            for k in range(kinds):
+                row = (b * kinds + k) * share
+                value = ref[row : row + share, source].astype(F32) * factor
+                to = pl.multiple_of(k * share * blocks + (sender ^ (2 * a + b)) * share, share)
+                out_ref[pl.ds(to, share), columns] = value
+
+
+def place_last_kernel(kinds, share, blocks, slabs, factor, *refs):
+    out_ref, held, sems = refs[-3:]
+    place = lax.axis_index("ctx")
+    mine = lax.axis_index("chan")
+    width = refs[0].shape[1] // slabs
+    copies = []
     for a in range(2):
-        for r in range(blocks):
-            sender = lax.rem(place + (r if a else blocks - r), blocks)
-            columns = pl.ds(pl.multiple_of(sender * width, width), width)
+        sender = lax.rem(place + (blocks - 1 if a else 1), blocks)
+        base = (sender ^ (2 * a)) // 2 * 2 * share
+        for k in range(kinds):
             for b in range(2):
-                for k in range(kinds):
-                    row = (b * kinds + k) * share
-                    value = refs[a * blocks + r][row : row + share, source].astype(F32) * factor
-                    to = pl.multiple_of(k * share * blocks + (sender ^ (2 * a + b)) * share, share)
-                    out_ref[pl.ds(to, share), columns] = value
+                row = (b * kinds + k) * share
+                to = pl.multiple_of((2 * k + lax.rem(sender + b, 2)) * share, share)
+                held[a, pl.ds(to, share), :] = refs[a][row : row + share, :].astype(F32) * factor
+            rows = pl.ds(pl.multiple_of(k * share * blocks + base, 2 * share), 2 * share)
+            for i in range(slabs):
+                columns = pl.ds(pl.multiple_of(((mine ^ i) * blocks + sender) * width, width), width)
+                source = held.at[a, 2 * k * share : 2 * (k + 1) * share, i * width : (i + 1) * width]
+                copies.append(pltpu.make_async_copy(source, out_ref.at[rows, columns], sems.at[len(copies)]))
+                copies[-1].start()
+    for copy in copies:
+        copy.wait()
 
 
 def place_weights(pieces, kinds, share, slabs, factor):
-    flat = [piece for group in pieces for piece in group]
-    depth = flat[0].shape[1]
-    rows = kinds * share * len(pieces[0])
-    return pl.pallas_call(
+    flat = [piece for group in pieces for piece in group[:-1]]
+    last = [group[-1] for group in pieces]
+    blocks, depth = len(pieces[0]), flat[0].shape[1]
+    rows = kinds * share * blocks
+    shape = jax.ShapeDtypeStruct((rows, depth * slabs), F32)
+    most = pl.pallas_call(
         functools.partial(place_kernel, kinds, share, factor),
-        out_shape=jax.ShapeDtypeStruct((rows, depth * slabs), F32),
+        out_shape=shape,
         grid=(slabs,),
         in_specs=[pl.BlockSpec(flat[0].shape, lambda i: (0, 0))] * len(flat),
         out_specs=pl.BlockSpec((rows, depth), lambda i: (0, i)),
@@ -407,6 +434,20 @@
         cost_estimate=pl.CostEstimate(flops=0, bytes_accessed=6 * 2**20, transcendentals=0),
         name="place",
     )(*flat)
+    return pl.pallas_call(
+        functools.partial(place_last_kernel, kinds, share, blocks, slabs, factor),
+        out_shape=shape,
+        in_specs=[VMEM, VMEM, ANY],
+        out_specs=ANY,
+        scratch_shapes=[
+            pltpu.VMEM((2, 2 * kinds * share, depth), F32),
+            pltpu.SemaphoreType.DMA((2 * kinds * slabs,)),
+        ],
+        input_output_aliases={2: 0},
+        compiler_params=pltpu.CompilerParams(vmem_limit_bytes=VMEM_BYTES),
+        cost_estimate=pl.CostEstimate(flops=0, bytes_accessed=2**20, transcendentals=0),
+        name="place",
+    )(*last, most)
 
 
 def swap(values, axis, mask):
@@ -516,7 +557,9 @@
         weight_cols = after(weight_cols, gathered[2])
         weight_cols = [*weight_cols[:2], swap(weight_cols[2], "chan", 2), swap(weight_cols[3], "chan", 3)]
         grad_rows = input_gradient(gathered, weight_cols)
-        grad_rows, pieces = lax.optimization_barrier((grad_rows, pieces))
+        grad_rows, pieces[0][-1], pieces[1][-1] = lax.optimization_barrier(
+            (grad_rows, pieces[0][-1], pieces[1][-1])
+        )
         grad_weight = place_weights(pieces, kinds, share, slabs, factor)
     else:
         grad_proj, grad_weight, grad_filter = general_tail(messages, features, place, mine, kinds, share, factor)

time: 108 us -> 107 us (level)
  waiting for transfers between devices: 55.2 us -> 53.1 us
    ppermute x6, waiting for transfers between devices: 18.1 us -> 16.1 us  [ring(): lax.ppermute(found[-1], 'ctx', [(i, (i + step) % size) for i in range(siz...]
    pallas_call x0 -> x1, Pallas kernels: none -> 1.13 us  [place_weights(): pl.pallas_call(functools.partial(place_last_kernel, kinds, share, blocks,...]
  transfers between devices with their start and end apart: 26 -> 26, of which waited for: 15 -> 14; matrix products, arithmetic and copies ran while one was open for 2% -> 2% of each run, Pallas kernels for 12% -> 14%
where the time goes in v5:
time: 107 us
  waiting for transfers between devices  53.1 us (50%)
  starting transfers between devices  26.9 us (25%)
  Pallas kernels  16.2 us (15%)
  local copies, waits for them, and re-layouts  8.92 us (8%)
    ppermute x18, waiting for transfers between devices, swap(): return lax.ppermute(values, axis, [(i, i ^ mask) for i in range(size)])  36.9 us
    ppermute x6, waiting for transfers between devices, ring(): lax.ppermute(found[-1], 'ctx', [(i, (i + step) % size) for i in range(siz...  16.1 us
    ppermute x18, starting transfers between devices, swap(): return lax.ppermute(values, axis, [(i, i ^ mask) for i in range(size)])  13.6 us
    unnamed x30, local copies, waits for them, and re-layouts  7.26 us
    ppermute x6, starting transfers between devices, ring(): lax.ppermute(found[-1], 'ctx', [(i, (i + step) % size) for i in range(siz...  6.83 us
    pallas_call x1, Pallas kernels, convolve(): pl.pallas_call(functools.partial(conv_kernel, blocks, chans, group, token...  5.87 us
    all_to_all x1, starting transfers between devices, per_device(): lax.all_to_all(turned, 'ctx', split_axis=0, concat_axis=0)  4.87 us
    pallas_call x3, Pallas kernels, project(): pl.pallas_call(body, out_shape=shape, in_specs=[VMEM] * (len(along) + 1 +...  2.95 us
  transfers between devices with their start and end apart: 26, of which 14 were waited for; matrix products, arithmetic and copies ran while one was open for 2% of the time, Pallas kernels for 14%

profile of v5, /device:TPU:0, one launch (start us, length us, event | category | flops | bytes accessed | tf_op | source)
XLA Modules:
  0.0 106.8 jit_solution(12886510709432226227)
XLA Ops:
  1.2 2.6 %collective-permute-start = (bf16[512,1024]{1,0:T(8,128)(2,1)}, bf16[512,1024]{1,0:T(8,128)(2,1)}, u32[]{:S(2)}, u32[]{:S(2)}) collective-permute-start(bf16[512,1024]{1,0:T(8,128)(2,1)} %values_ref.1), channel_id=1, source_target_pairs={{0,2},{1,3},{2,0},{3,1},{4,6},{5,7},{6,4},{7,5},{8,10},{9,11},{10,... | collective-permute-start | bytes 3145736 | tf_op jit(solution)/shard_map/ppermute | solution.py:457
  3.7 1.3 %copy-done.3 = bf16[512,1024]{1,0:T(8,128)(2,1)S(1)} copy-done((bf16[512,1024]{1,0:T(8,128)(2,1)S(1)}, bf16[512,1024]{1,0:T(8,128)(2,1)}, u32[]{:S(2)}) %copy-start.3) | copy-done | bytes 1048600
  7.0 4.9 %all-to-all-start = ((bf16[4,512,256]{2,1,0:T(8,128)(2,1)}), bf16[4,512,256]{2,1,0:T(8,128)(2,1)S(1)}, u32[]{:S(2)}, u32[]{:S(2)}) async-start(bf16[4,512,256]{2,1,0:T(8,128)(2,1)} %copy-done.2), calls=%async_computation | async-start | bytes 2097152 | tf_op jit(solution)/shard_map/all_to_all | solution.py:528
  11.9 1.1 constant_dynamic-slice_fusion
  14.4 1.2 %copy-done.4 = bf16[512,1024]{1,0:T(8,128)(2,1)S(1)} copy-done((bf16[512,1024]{1,0:T(8,128)(2,1)S(1)}, bf16[512,1024]{1,0:T(8,128)(2,1)}, u32[]{:S(2)}) %copy-start.4) | copy-done | bytes 1048600
  15.6 1.2 %copy-done.6 = bf16[512,1024]{1,0:T(8,128)(2,1)S(1)} copy-done((bf16[512,1024]{1,0:T(8,128)(2,1)S(1)}, bf16[512,1024]{1,0:T(8,128)(2,1)}, u32[]{:S(2)}) %copy-start.6) | copy-done | bytes 1048600
  17.6 10.2 %collective-permute-done.refs_0_ = bf16[512,1024]{1,0:T(8,128)(2,1)} collective-permute-done((bf16[512,1024]{1,0:T(8,128)(2,1)}, bf16[512,1024]{1,0:T(8,128)(2,1)}, u32[]{:S(2)}, u32[]{:S(2)}) %collective-permute-start) | collective-permute-done | bytes 1048608 | tf_op jit(solution)/shard_map/ppermute | solution.py:457
  27.8 1.7 %project.4.sum_ref = f32[512,192]{1,0:T(8,128)S(1)} custom-call(bf16[192,4096]{1,0:T(8,128)(2,1)S(1)} %bitcast.7, f32[512,192]{1,0:T(8,128)S(1)} %project.3.sum_ref, bf16[512,1024]{1,0:T(8,128)(2,1)} %collective-permute-done.refs_0_), custom_call_target="tpu_custom_call" | custom-call | flops 201326592 | bytes 1048576 | tf_op jit(solution)/shard_map/project/pallas_call | solution.py:244
  29.5 1.2 %collective-permute-done.3.refs_0_ = bf16[512,1024]{1,0:T(8,128)(2,1)S(1)} collective-permute-done((bf16[512,1024]{1,0:T(8,128)(2,1)}, bf16[512,1024]{1,0:T(8,128)(2,1)S(1)}, u32[]{:S(2)}, u32[]{:S(2)}) %collective-permute-start.3) | collective-permute-done | bytes 1048608 | tf_op jit(solution)/shard_map/ppermute | solution.py:457
  31.9 1.8 %collective-permute-start.4 = (bf16[80,512]{1,0:T(8,128)(2,1)S(1)}, bf16[80,512]{1,0:T(8,128)(2,1)S(1)}, u32[]{:S(2)}, u32[]{:S(2)}) collective-permute-start(bf16[80,512]{1,0:T(8,128)(2,1)S(1)} %get-tuple-element.53), channel_id=1, source_target_pairs={{0,4},{4,0},{8,12},{12,8},{1,5},{5,1},{9,13},{13,9},{2,6},{6,2},{1... | collective-permute-start | bytes 245768 | tf_op jit(solution)/shard_map/ppermute | solution.py:457
  33.7 2.6 %collective-permute-start.5 = (bf16[80,512]{1,0:T(8,128)(2,1)S(1)}, bf16[80,512]{1,0:T(8,128)(2,1)S(1)}, u32[]{:S(2)}, u32[]{:S(2)}) collective-permute-start(bf16[80,512]{1,0:T(8,128)(2,1)S(1)} %get-tuple-element.54), channel_id=1, source_target_pairs={{0,8},{4,12},{8,0},{12,4},{1,9},{5,13},{9,1},{13,5},{2,10},{6,14},... | collective-permute-start | bytes 245768 | tf_op jit(solution)/shard_map/ppermute | solution.py:457
  36.3 4.2 %collective-permute-done.4.refs_2_ = bf16[80,512]{1,0:T(8,128)(2,1)S(1)} collective-permute-done((bf16[80,512]{1,0:T(8,128)(2,1)S(1)}, bf16[80,512]{1,0:T(8,128)(2,1)S(1)}, u32[]{:S(2)}, u32[]{:S(2)}) %collective-permute-start.4) | collective-permute-done | bytes 81952 | tf_op jit(solution)/shard_map/ppermute | solution.py:457
  40.5 3.6 %collective-permute-done.5.refs_3_ = bf16[80,512]{1,0:T(8,128)(2,1)S(1)} collective-permute-done((bf16[80,512]{1,0:T(8,128)(2,1)S(1)}, bf16[80,512]{1,0:T(8,128)(2,1)S(1)}, u32[]{:S(2)}, u32[]{:S(2)}) %collective-permute-start.5) | collective-permute-done | bytes 81952 | tf_op jit(solution)/shard_map/ppermute | solution.py:457
  44.8 5.9 %conv.1 = (bf16[48,2432]{1,0:T(8,128)(2,1)}, bf16[48,2432]{1,0:T(8,128)(2,1)}, bf16[48,2432]{1,0:T(8,128)(2,1)}, bf16[48,2432]{1,0:T(8,128)(2,1)}) custom-call(f32[1,16]{1,0:T(1,128)} %dynamic-slice_bitcast_fusion.refs_0_, bf16[80,512]{1,0:T(8,128)(2,1)} %copy-done.9, bf16[80,512]{1,0:T(8,128)(2,1)} %copy-done.12, bf16[80,512]{1,0:T(8,128)(2,1)} %copy-done.13, ...), custom_call_target="tpu_custom_call" | custom-call | flops 962592768 | bytes 4194304 | tf_op jit(solution)/shard_map/conv/pallas_call | solution.py:184
  50.7 2.4 %collective-permute-start.9 = (bf16[48,2432]{1,0:T(8,128)(2,1)}, bf16[48,2432]{1,0:T(8,128)(2,1)S(1)}, u32[]{:S(2)}, u32[]{:S(2)}) collective-permute-start(bf16[48,2432]{1,0:T(8,128)(2,1)} %get-tuple-element.65), channel_id=1, source_target_pairs={{0,8},{4,12},{8,0},{12,4},{1,9},{5,13},{9,1},{13,5},{2,10},{6,14},... | collective-permute-start | bytes 700424 | tf_op jit(solution)/shard_map/ppermute | solution.py:457
  53.8 1.6 %collective-permute-start.10 = (bf16[48,2432]{1,0:T(8,128)(2,1)}, bf16[48,2432]{1,0:T(8,128)(2,1)S(1)}, u32[]{:S(2)}, u32[]{:S(2)}) collective-permute-start(bf16[48,2432]{1,0:T(8,128)(2,1)} %get-tuple-element.66), channel_id=1, source_target_pairs={{4,8},{8,4},{0,0},{12,12},{5,9},{9,5},{1,1},{13,13},{6,10},{10,6},... | collective-permute-start | bytes 700424 | tf_op jit(solution)/shard_map/ppermute | solution.py:548
  55.4 9.3 %collective-permute-done.9.refs_2_ = bf16[48,2432]{1,0:T(8,128)(2,1)S(1)} collective-permute-done((bf16[48,2432]{1,0:T(8,128)(2,1)}, bf16[48,2432]{1,0:T(8,128)(2,1)S(1)}, u32[]{:S(2)}, u32[]{:S(2)}) %collective-permute-start.9) | collective-permute-done | bytes 233504 | tf_op jit(solution)/shard_map/ppermute | solution.py:457
  64.7 6.0 %collective-permute-done.11.refs_4_ = bf16[48,2432]{1,0:T(8,128)(2,1)S(1)} collective-permute-done((bf16[48,2432]{1,0:T(8,128)(2,1)S(1)}, bf16[48,2432]{1,0:T(8,128)(2,1)S(1)}, u32[]{:S(2)}, u32[]{:S(2)}) %collective-permute-start.11) | collective-permute-done | bytes 233504 | tf_op jit(solution)/shard_map/ppermute | solution.py:457
  71.7 1.4 %products.2 = (bf16[192,2048]{1,0:T(8,128)(2,1)S(1)}, bf16[192,768]{1,0:T(8,128)(2,1)S(1)}, bf16[192,512]{1,0:T(8,128)(2,1)S(1)}, f32[64,512]{1,0:T(8,128)}) custom-call(bf16[48,2432]{1,0:T(8,128)(2,1)S(1)} %copy-done.7, bf16[48,2432]{1,0:T(8,128)(2,1)S(1)} %collective-permute-done.8.refs_1_, bf16[48,2432]{1,0:T(8,128)(2,1)S(1)} %collective-permute-done.9.refs_2_, ...), custom_call_target="tpu_custom_call" | custom-call | flops 603979776 | bytes 4194304 | tf_op jit(solution)/shard_map/products/pallas_call | solution.py:301
  73.8 1.2 %collective-permute-start.15 = (bf16[192,512]{1,0:T(8,128)(2,1)S(1)}, bf16[192,512]{1,0:T(8,128)(2,1)S(1)}, u32[]{:S(2)}, u32[]{:S(2)}) collective-permute-start(bf16[192,512]{1,0:T(8,128)(2,1)S(1)} %get-tuple-element.78.refs_0_), channel_id=1, source_target_pairs={{0,2},{1,3},{2,0},{3,1},{4,6},{5,7},{6,4},{7,5},{8,10},{9,11},{10,... | collective-permute-start | bytes 589832 | tf_op jit(solution)/shard_map/ppermute | solution.py:457
  75.0 3.8 %collective-permute-start.22 = (bf16[96,1024]{1,0:T(8,128)(2,1)S(1)}, bf16[96,1024]{1,0:T(8,128)(2,1)S(1)}, u32[]{:S(2)}, u32[]{:S(2)}) collective-permute-start(bf16[96,1024]{1,0:T(8,128)(2,1)S(1)} %get-tuple-element.88.refs_3_), channel_id=1, source_target_pairs={{0,12},{4,0},{8,4},{12,8},{1,13},{5,1},{9,5},{13,9},{2,14},{6,2},{... | collective-permute-start | bytes 589832 | tf_op jit(solution)/shard_map/ppermute | solution.py:476
  78.8 2.0 %collective-permute-done.15.refs_2_ = bf16[192,512]{1,0:T(8,128)(2,1)S(1)} collective-permute-done((bf16[192,512]{1,0:T(8,128)(2,1)S(1)}, bf16[192,512]{1,0:T(8,128)(2,1)S(1)}, u32[]{:S(2)}, u32[]{:S(2)}) %collective-permute-start.15) | collective-permute-done | bytes 196640 | tf_op jit(solution)/shard_map/ppermute | solution.py:457
  80.9 1.1 %collective-permute-start.17 = (bf16[192,1024]{1,0:T(8,128)(2,1)S(1)}, bf16[192,1024]{1,0:T(8,128)(2,1)S(1)}, u32[]{:S(2)}, u32[]{:S(2)}) collective-permute-start(bf16[192,1024]{1,0:T(8,128)(2,1)S(1)} %copy-done.11), channel_id=1, source_target_pairs={{0,2},{1,3},{2,0},{3,1},{4,6},{5,7},{6,4},{7,5},{8,10},{9,11},{10,... | collective-permute-start | bytes 1179656 | tf_op jit(solution)/shard_map/ppermute | solution.py:457
  82.0 2.6 %collective-permute-done.19.refs_1_ = bf16[96,1024]{1,0:T(8,128)(2,1)S(1)} collective-permute-done((bf16[96,1024]{1,0:T(8,128)(2,1)S(1)}, bf16[96,1024]{1,0:T(8,128)(2,1)S(1)}, u32[]{:S(2)}, u32[]{:S(2)}) %collective-permute-start.19) | collective-permute-done | bytes 196640 | tf_op jit(solution)/shard_map/ppermute | solution.py:476
  84.6 1.3 %collective-permute-done.22.refs_4_ = bf16[96,1024]{1,0:T(8,128)(2,1)S(1)} collective-permute-done((bf16[96,1024]{1,0:T(8,128)(2,1)S(1)}, bf16[96,1024]{1,0:T(8,128)(2,1)S(1)}, u32[]{:S(2)}, u32[]{:S(2)}) %collective-permute-start.22) | collective-permute-done | bytes 196640 | tf_op jit(solution)/shard_map/ppermute | solution.py:476
  85.9 2.5 %collective-permute-start.23 = (bf16[96,1024]{1,0:T(8,128)(2,1)S(1)}, bf16[96,1024]{1,0:T(8,128)(2,1)S(1)}, u32[]{:S(2)}, u32[]{:S(2)}) collective-permute-start(bf16[96,1024]{1,0:T(8,128)(2,1)S(1)} %collective-permute-done.22.refs_4_), channel_id=1, source_target_pairs={{0,12},{4,0},{8,4},{12,8},{1,13},{5,1},{9,5},{13,9},{2,14},{6,2},{... | collective-permute-start | bytes 589832 | tf_op jit(solution)/shard_map/ppermute | solution.py:476
  88.4 5.7 %collective-permute-done.20.refs_2_ = bf16[96,1024]{1,0:T(8,128)(2,1)S(1)} collective-permute-done((bf16[96,1024]{1,0:T(8,128)(2,1)S(1)}, bf16[96,1024]{1,0:T(8,128)(2,1)S(1)}, u32[]{:S(2)}, u32[]{:S(2)}) %collective-permute-start.20) | collective-permute-done | bytes 196640 | tf_op jit(solution)/shard_map/ppermute | solution.py:476
  94.1 3.4 %collective-permute-done.23.refs_5_ = bf16[96,1024]{1,0:T(8,128)(2,1)S(1)} collective-permute-done((bf16[96,1024]{1,0:T(8,128)(2,1)S(1)}, bf16[96,1024]{1,0:T(8,128)(2,1)S(1)}, u32[]{:S(2)}, u32[]{:S(2)}) %collective-permute-start.23) | collective-permute-done | bytes 196640 | tf_op jit(solution)/shard_map/ppermute | solution.py:476
  98.1 2.2 %place.2.refs_2_ = f32[192,4096]{1,0:T(8,128)} custom-call(bf16[96,1024]{1,0:T(8,128)(2,1)S(1)} %get-tuple-element.87.refs_0_, bf16[96,1024]{1,0:T(8,128)(2,1)S(1)} %collective-permute-done.19.refs_1_, bf16[96,1024]{1,0:T(8,128)(2,1)S(1)} %collective-permute-done.20.refs_2_, bf16[96,1024]{1,0:T(8,128)(2,1)S(1)} %get-tuple-element.88.refs_3_, ...), custom_call_target="tpu_custom_call" | custom-call | bytes 6291456 | tf_op jit(solution)/shard_map/place/pallas_call | solution.py:427
  100.3 2.3 %inputs.1 = bf16[512,1024]{1,0:T(8,128)(2,1)} custom-call(bf16[192,512]{1,0:T(8,128)(2,1)S(1)} %get-tuple-element.78.refs_0_, bf16[192,512]{1,0:T(8,128)(2,1)S(1)} %collective-permute-done.14.refs_1_, bf16[192,512]{1,0:T(8,128)(2,1)S(1)} %collective-permute-done.15.refs_2_, bf16[192,512]{1,0:T(8,128)(2,1)S(1)} %collective-permute-done.16.refs_3_, ...), custom_call_target="tpu_custom_call" | custom-call | flops 805306368 | bytes 4194304 | tf_op jit(solution)/shard_map/inputs/pallas_call | solution.py:364
  103.2 2.4 %collective-permute-done.24.refs_1_ = bf16[96,1024]{1,0:T(8,128)(2,1)S(1)} collective-permute-done((bf16[96,1024]{1,0:T(8,128)(2,1)S(1)}, bf16[96,1024]{1,0:T(8,128)(2,1)S(1)}, u32[]{:S(2)}, u32[]{:S(2)}) %collective-permute-start.24) | collective-permute-done | bytes 196640 | tf_op jit(solution)/shard_map/ppermute | solution.py:476
  105.6 1.1 %place.3 = f32[192,4096]{1,0:T(8,128)} custom-call(bf16[96,1024]{1,0:T(8,128)(2,1)S(1)} %collective-permute-done.21.refs_0_, bf16[96,1024]{1,0:T(8,128)(2,1)S(1)} %collective-permute-done.24.refs_1_, f32[192,4096]{1,0:T(8,128)} %place.2.refs_2_), custom_call_target="tpu_custom_call", output_to_operand_aliasing={{}: (2, {})} | custom-call | bytes 1048576 | tf_op jit(solution)/shard_map/place/pallas_call | solution.py:437
  (63 shorter events, 10.1 us)
Async XLA Ops:
  0.6 13.2 %copy-start = (f32[64]{0:T(128)S(1)}, f32[64]{0:T(128)}, u32[]{:S(2)}) copy-start(f32[64]{0:T(128)} %param.13) | copy-start | bytes 772
  0.6 11.2 %copy-start.1 = (bf16[3,64,4096]{2,1,0:T(8,128)(2,1)S(1)}, bf16[3,64,4096]{2,1,0:T(8,128)(2,1)}, u32[]{:S(2)}) copy-start(bf16[3,64,4096]{2,1,0:T(8,128)(2,1)} %param.11) | copy-start | bytes 4718596
  0.7 5.4 %collective-permute-start.1 = (bf16[512,1024]{1,0:T(8,128)(2,1)}, bf16[512,1024]{1,0:T(8,128)(2,1)S(1)}, u32[]{:S(2)}, u32[]{:S(2)}) collective-permute-start(bf16[512,1024]{1,0:T(8,128)(2,1)} %values_ref.1), channel_id=1, source_target_pairs={{0,1},{1,0},{2,3},{3,2},{4,5},{5,4},{6,7},{7,6},{8,9},{9,8},{10,11... | collective-permute-start | bytes 3145736 | tf_op jit(solution)/shard_map/ppermute | solution.py:457
  1.2 26.6 %collective-permute-start = (bf16[512,1024]{1,0:T(8,128)(2,1)}, bf16[512,1024]{1,0:T(8,128)(2,1)}, u32[]{:S(2)}, u32[]{:S(2)}) collective-permute-start(bf16[512,1024]{1,0:T(8,128)(2,1)} %values_ref.1), channel_id=1, source_target_pairs={{0,2},{1,3},{2,0},{3,1},{4,6},{5,7},{6,4},{7,5},{8,10},{9,11},{10,... | collective-permute-start | bytes 3145736 | tf_op jit(solution)/shard_map/ppermute | solution.py:457
  7.0 37.1 %all-to-all-start = ((bf16[4,512,256]{2,1,0:T(8,128)(2,1)}), bf16[4,512,256]{2,1,0:T(8,128)(2,1)S(1)}, u32[]{:S(2)}, u32[]{:S(2)}) async-start(bf16[4,512,256]{2,1,0:T(8,128)(2,1)} %copy-done.2), calls=%async_computation | async-start | bytes 2097152 | tf_op jit(solution)/shard_map/all_to_all | solution.py:528
  13.0 4.7 %collective-permute-start.2 = (bf16[192,1024]{1,0:T(8,128)(2,1)}, bf16[192,1024]{1,0:T(8,128)(2,1)S(1)}, u32[]{:S(2)}, u32[]{:S(2)}) collective-permute-start(bf16[192,1024]{1,0:T(8,128)(2,1)} %get-tuple-element.95), channel_id=1, source_target_pairs={{0,1},{1,0},{2,3},{3,2},{4,5},{5,4},{6,7},{7,6},{8,9},{9,8},{10,11... | collective-permute-start | bytes 1179656 | tf_op jit(solution)/shard_map/ppermute | solution.py:457
  16.9 13.8 %copy-start.8 = (f32[64,512]{1,0:T(8,128)S(1)}, f32[64,512]{1,0:T(8,128)}, u32[]{:S(2)}) copy-start(f32[64,512]{1,0:T(8,128)} %filter_ref) | copy-start | bytes 393220
  27.8 2.9 %collective-permute-start.3 = (bf16[512,1024]{1,0:T(8,128)(2,1)}, bf16[512,1024]{1,0:T(8,128)(2,1)S(1)}, u32[]{:S(2)}, u32[]{:S(2)}) collective-permute-start(bf16[512,1024]{1,0:T(8,128)(2,1)} %collective-permute-done.refs_0_), channel_id=1, source_target_pairs={{0,1},{1,0},{2,3},{3,2},{4,5},{5,4},{6,7},{7,6},{8,9},{9,8},{10,11... | collective-permute-start | bytes 3145736 | tf_op jit(solution)/shard_map/ppermute | solution.py:457
  31.9 8.6 %collective-permute-start.4 = (bf16[80,512]{1,0:T(8,128)(2,1)S(1)}, bf16[80,512]{1,0:T(8,128)(2,1)S(1)}, u32[]{:S(2)}, u32[]{:S(2)}) collective-permute-start(bf16[80,512]{1,0:T(8,128)(2,1)S(1)} %get-tuple-element.53), channel_id=1, source_target_pairs={{0,4},{4,0},{8,12},{12,8},{1,5},{5,1},{9,13},{13,9},{2,6},{6,2},{1... | collective-permute-start | bytes 245768 | tf_op jit(solution)/shard_map/ppermute | solution.py:457
  33.7 10.4 %collective-permute-start.5 = (bf16[80,512]{1,0:T(8,128)(2,1)S(1)}, bf16[80,512]{1,0:T(8,128)(2,1)S(1)}, u32[]{:S(2)}, u32[]{:S(2)}) collective-permute-start(bf16[80,512]{1,0:T(8,128)(2,1)S(1)} %get-tuple-element.54), channel_id=1, source_target_pairs={{0,8},{4,12},{8,0},{12,4},{1,9},{5,13},{9,1},{13,5},{2,10},{6,14},... | collective-permute-start | bytes 245768 | tf_op jit(solution)/shard_map/ppermute | solution.py:457
  36.3 7.8 %collective-permute-start.6 = (bf16[80,512]{1,0:T(8,128)(2,1)S(1)}, bf16[80,512]{1,0:T(8,128)(2,1)S(1)}, u32[]{:S(2)}, u32[]{:S(2)}) collective-permute-start(bf16[80,512]{1,0:T(8,128)(2,1)S(1)} %get-tuple-element.55), channel_id=1, source_target_pairs={{0,12},{4,8},{8,4},{12,0},{1,13},{5,9},{9,5},{13,1},{2,14},{6,10},... | collective-permute-start | bytes 245768 | tf_op jit(solution)/shard_map/ppermute | solution.py:457
  40.5 4.3 %copy-start.12 = (bf16[80,512]{1,0:T(8,128)(2,1)}, bf16[80,512]{1,0:T(8,128)(2,1)S(1)}, u32[]{:S(2)}) copy-start(bf16[80,512]{1,0:T(8,128)(2,1)S(1)} %collective-permute-done.4.refs_2_) | copy-start | bytes 245764
  44.1 26.6 %collective-permute-start.7 = (bf16[2048,256]{1,0:T(8,128)(2,1)S(1)}, bf16[2048,256]{1,0:T(8,128)(2,1)S(1)}, u32[]{:S(2)}, u32[]{:S(2)}) collective-permute-start(bf16[2048,256]{1,0:T(8,128)(2,1)S(1)} %bitcast.9), channel_id=1, source_target_pairs={{0,2},{1,3},{2,0},{3,1},{4,6},{5,7},{6,4},{7,5},{8,10},{9,11},{10,... | collective-permute-start | bytes 3145736 | tf_op jit(solution)/shard_map/ppermute | solution.py:457
  50.7 14.0 %collective-permute-start.9 = (bf16[48,2432]{1,0:T(8,128)(2,1)}, bf16[48,2432]{1,0:T(8,128)(2,1)S(1)}, u32[]{:S(2)}, u32[]{:S(2)}) collective-permute-start(bf16[48,2432]{1,0:T(8,128)(2,1)} %get-tuple-element.65), channel_id=1, source_target_pairs={{0,8},{4,12},{8,0},{12,4},{1,9},{5,13},{9,1},{13,5},{2,10},{6,14},... | collective-permute-start | bytes 700424 | tf_op jit(solution)/shard_map/ppermute | solution.py:457
  53.1 11.6 %collective-permute-start.8 = (bf16[48,2432]{1,0:T(8,128)(2,1)}, bf16[48,2432]{1,0:T(8,128)(2,1)S(1)}, u32[]{:S(2)}, u32[]{:S(2)}) collective-permute-start(bf16[48,2432]{1,0:T(8,128)(2,1)} %get-tuple-element.64), channel_id=1, source_target_pairs={{0,4},{4,0},{8,12},{12,8},{1,5},{5,1},{9,13},{13,9},{2,6},{6,2},{1... | collective-permute-start | bytes 700424 | tf_op jit(solution)/shard_map/ppermute | solution.py:457
  53.8 10.9 %collective-permute-start.10 = (bf16[48,2432]{1,0:T(8,128)(2,1)}, bf16[48,2432]{1,0:T(8,128)(2,1)S(1)}, u32[]{:S(2)}, u32[]{:S(2)}) collective-permute-start(bf16[48,2432]{1,0:T(8,128)(2,1)} %get-tuple-element.66), channel_id=1, source_target_pairs={{4,8},{8,4},{0,0},{12,12},{5,9},{9,5},{1,1},{13,13},{6,10},{10,6},... | collective-permute-start | bytes 700424 | tf_op jit(solution)/shard_map/ppermute | solution.py:548
  64.7 6.1 %collective-permute-start.11 = (bf16[48,2432]{1,0:T(8,128)(2,1)S(1)}, bf16[48,2432]{1,0:T(8,128)(2,1)S(1)}, u32[]{:S(2)}, u32[]{:S(2)}) collective-permute-start(bf16[48,2432]{1,0:T(8,128)(2,1)S(1)} %collective-permute-done.9.refs_2_), channel_id=1, source_target_pairs={{0,4},{4,0},{8,12},{12,8},{1,5},{5,1},{9,13},{13,9},{2,6},{6,2},{1... | collective-permute-start | bytes 700424 | tf_op jit(solution)/shard_map/ppermute | solution.py:457
  64.7 6.1 %collective-permute-start.12 = (bf16[2048,256]{1,0:T(8,128)(2,1)S(1)}, bf16[2048,256]{1,0:T(8,128)(2,1)S(1)}, u32[]{:S(2)}, u32[]{:S(2)}) collective-permute-start(bf16[2048,256]{1,0:T(8,128)(2,1)S(1)} %bitcast.10), channel_id=1, source_target_pairs={{0,1},{1,0},{2,3},{3,2},{4,5},{5,4},{6,7},{7,6},{8,9},{9,8},{10,11... | collective-permute-start | bytes 3145736 | tf_op jit(solution)/shard_map/ppermute | solution.py:457
  70.8 2.7 %collective-permute-start.13 = (bf16[2048,256]{1,0:T(8,128)(2,1)S(1)}, bf16[2048,256]{1,0:T(8,128)(2,1)S(1)}, u32[]{:S(2)}, u32[]{:S(2)}) collective-permute-start(bf16[2048,256]{1,0:T(8,128)(2,1)S(1)} %collective-permute-done.7.refs_7_), channel_id=1, source_target_pairs={{0,1},{1,0},{2,3},{3,2},{4,5},{5,4},{6,7},{7,6},{8,9},{9,8},{10,11... | collective-permute-start | bytes 3145736 | tf_op jit(solution)/shard_map/ppermute | solution.py:457
  71.7 9.1 %copy-start.11 = (bf16[192,1024]{1,0:T(8,128)(2,1)S(1)}, bf16[192,1024]{1,0:T(8,128)(2,1)}, u32[]{:S(2)}) copy-start(bf16[192,1024]{1,0:T(8,128)(2,1)} %get-tuple-element.85) | copy-start | bytes 1179652
  71.7 10.3 %copy-start.10 = (bf16[192,1024]{1,0:T(8,128)(2,1)S(1)}, bf16[192,1024]{1,0:T(8,128)(2,1)}, u32[]{:S(2)}) copy-start(bf16[192,1024]{1,0:T(8,128)(2,1)} %get-tuple-element.86) | copy-start | bytes 1179652
  73.8 7.1 %collective-permute-start.15 = (bf16[192,512]{1,0:T(8,128)(2,1)S(1)}, bf16[192,512]{1,0:T(8,128)(2,1)S(1)}, u32[]{:S(2)}, u32[]{:S(2)}) collective-permute-start(bf16[192,512]{1,0:T(8,128)(2,1)S(1)} %get-tuple-element.78.refs_0_), channel_id=1, source_target_pairs={{0,2},{1,3},{2,0},{3,1},{4,6},{5,7},{6,4},{7,5},{8,10},{9,11},{10,... | collective-permute-start | bytes 589832 | tf_op jit(solution)/shard_map/ppermute | solution.py:457
  75.0 9.6 %collective-permute-start.19 = (bf16[96,1024]{1,0:T(8,128)(2,1)S(1)}, bf16[96,1024]{1,0:T(8,128)(2,1)S(1)}, u32[]{:S(2)}, u32[]{:S(2)}) collective-permute-start(bf16[96,1024]{1,0:T(8,128)(2,1)S(1)} %get-tuple-element.87.refs_0_), channel_id=1, source_target_pairs={{0,4},{4,8},{8,12},{12,0},{1,5},{5,9},{9,13},{13,1},{2,6},{6,10},{... | collective-permute-start | bytes 589832 | tf_op jit(solution)/shard_map/ppermute | solution.py:476
  75.0 10.9 %collective-permute-start.22 = (bf16[96,1024]{1,0:T(8,128)(2,1)S(1)}, bf16[96,1024]{1,0:T(8,128)(2,1)S(1)}, u32[]{:S(2)}, u32[]{:S(2)}) collective-permute-start(bf16[96,1024]{1,0:T(8,128)(2,1)S(1)} %get-tuple-element.88.refs_3_), channel_id=1, source_target_pairs={{0,12},{4,0},{8,4},{12,8},{1,13},{5,1},{9,5},{13,9},{2,14},{6,2},{... | collective-permute-start | bytes 589832 | tf_op jit(solution)/shard_map/ppermute | solution.py:476
  78.8 9.6 %collective-permute-start.14 = (bf16[192,512]{1,0:T(8,128)(2,1)S(1)}, bf16[192,512]{1,0:T(8,128)(2,1)S(1)}, u32[]{:S(2)}, u32[]{:S(2)}) collective-permute-start(bf16[192,512]{1,0:T(8,128)(2,1)S(1)} %get-tuple-element.78.refs_0_), channel_id=1, source_target_pairs={{0,1},{1,0},{2,3},{3,2},{4,5},{5,4},{6,7},{7,6},{8,9},{9,8},{10,11... | collective-permute-start | bytes 589832 | tf_op jit(solution)/shard_map/ppermute | solution.py:457
  80.9 19.4 %collective-permute-start.17 = (bf16[192,1024]{1,0:T(8,128)(2,1)S(1)}, bf16[192,1024]{1,0:T(8,128)(2,1)S(1)}, u32[]{:S(2)}, u32[]{:S(2)}) collective-permute-start(bf16[192,1024]{1,0:T(8,128)(2,1)S(1)} %copy-done.11), channel_id=1, source_target_pairs={{0,2},{1,3},{2,0},{3,1},{4,6},{5,7},{6,4},{7,5},{8,10},{9,11},{10,... | collective-permute-start | bytes 1179656 | tf_op jit(solution)/shard_map/ppermute | solution.py:457
  82.0 18.3 %collective-permute-start.18 = (bf16[192,1024]{1,0:T(8,128)(2,1)S(1)}, bf16[192,1024]{1,0:T(8,128)(2,1)S(1)}, u32[]{:S(2)}, u32[]{:S(2)}) collective-permute-start(bf16[192,1024]{1,0:T(8,128)(2,1)S(1)} %copy-done.10), channel_id=1, source_target_pairs={{0,3},{1,2},{2,1},{3,0},{4,7},{5,6},{6,5},{7,4},{8,11},{9,10},{10,... | collective-permute-start | bytes 1179656 | tf_op jit(solution)/shard_map/ppermute | solution.py:457
  84.6 9.5 %collective-permute-start.20 = (bf16[96,1024]{1,0:T(8,128)(2,1)S(1)}, bf16[96,1024]{1,0:T(8,128)(2,1)S(1)}, u32[]{:S(2)}, u32[]{:S(2)}) collective-permute-start(bf16[96,1024]{1,0:T(8,128)(2,1)S(1)} %collective-permute-done.19.refs_1_), channel_id=1, source_target_pairs={{0,4},{4,8},{8,12},{12,0},{1,5},{5,9},{9,13},{13,1},{2,6},{6,10},{... | collective-permute-start | bytes 589832 | tf_op jit(solution)/shard_map/ppermute | solution.py:476
  85.9 11.6 %collective-permute-start.23 = (bf16[96,1024]{1,0:T(8,128)(2,1)S(1)}, bf16[96,1024]{1,0:T(8,128)(2,1)S(1)}, u32[]{:S(2)}, u32[]{:S(2)}) collective-permute-start(bf16[96,1024]{1,0:T(8,128)(2,1)S(1)} %collective-permute-done.22.refs_4_), channel_id=1, source_target_pairs={{0,12},{4,0},{8,4},{12,8},{1,13},{5,1},{9,5},{13,9},{2,14},{6,2},{... | collective-permute-start | bytes 589832 | tf_op jit(solution)/shard_map/ppermute | solution.py:476
  88.4 11.8 %collective-permute-start.16 = (bf16[192,512]{1,0:T(8,128)(2,1)S(1)}, bf16[192,512]{1,0:T(8,128)(2,1)S(1)}, u32[]{:S(2)}, u32[]{:S(2)}) collective-permute-start(bf16[192,512]{1,0:T(8,128)(2,1)S(1)} %collective-permute-done.15.refs_2_), channel_id=1, source_target_pairs={{0,1},{1,0},{2,3},{3,2},{4,5},{5,4},{6,7},{7,6},{8,9},{9,8},{10,11... | collective-permute-start | bytes 589832 | tf_op jit(solution)/shard_map/ppermute | solution.py:457
  94.1 9.1 %collective-permute-start.21 = (bf16[96,1024]{1,0:T(8,128)(2,1)S(1)}, bf16[96,1024]{1,0:T(8,128)(2,1)S(1)}, u32[]{:S(2)}, u32[]{:S(2)}) collective-permute-start(bf16[96,1024]{1,0:T(8,128)(2,1)S(1)} %collective-permute-done.20.refs_2_), channel_id=1, source_target_pairs={{0,4},{4,8},{8,12},{12,0},{1,5},{5,9},{9,13},{13,1},{2,6},{6,10},{... | collective-permute-start | bytes 589832 | tf_op jit(solution)/shard_map/ppermute | solution.py:476
  97.6 8.1 %collective-permute-start.24 = (bf16[96,1024]{1,0:T(8,128)(2,1)S(1)}, bf16[96,1024]{1,0:T(8,128)(2,1)S(1)}, u32[]{:S(2)}, u32[]{:S(2)}) collective-permute-start(bf16[96,1024]{1,0:T(8,128)(2,1)S(1)} %collective-permute-done.23.refs_5_), channel_id=1, source_target_pairs={{0,12},{4,0},{8,4},{12,8},{1,13},{5,1},{9,5},{13,9},{2,14},{6,2},{... | collective-permute-start | bytes 589832 | tf_op jit(solution)/shard_map/ppermute | solution.py:476
  (9 other events, 8.5 us)

commit v6 on v5

--- a/solution.py
+++ b/solution.py
@@ -330,6 +330,22 @@
     )(left, some, turned)
 
 
+def keep_kernel(values_ref, out_ref):
+    out_ref[...] = values_ref[...]
+
+
+def keep(values):
+    return pl.pallas_call(
+        keep_kernel,
+        out_shape=jax.ShapeDtypeStruct(values.shape, values.dtype),
+        in_specs=[VMEM],
+        out_specs=VMEM,
+        compiler_params=pltpu.CompilerParams(vmem_limit_bytes=VMEM_BYTES),
+        cost_estimate=pl.CostEstimate(flops=0, bytes_accessed=2**19, transcendentals=0),
+        name="keep",
+    )(values)
+
+
 def piece_kernel(values_ref, out_ref):
     width = out_ref.shape[2]
     for i in range(out_ref.shape[0]):
@@ -544,16 +560,19 @@
     messages = convolve(signals, gain)
 
     if line:
-        messages = [messages[0], swap(messages[1], "ctx", 1), swap(messages[2], "ctx", 2), messages[3]]
+        messages = [keep(messages[0]), swap(messages[1], "ctx", 1), swap(messages[2], "ctx", 2), messages[3]]
         messages[3] = lax.ppermute(messages[3], "ctx", [(1, 2), (2, 1), (0, 0), (3, 3)])
         messages.append(swap(messages[2], "ctx", 1))
         far, messages = lax.optimization_barrier((turned[2], messages))
         far = swap(far, "chan", 1)
         left, some, grad_proj, grad_filter = weight_products(messages, turned, kinds, share)
         first, second = last_products(left, some, far)
+        far_grads = swap(grad_proj, "chan", 2)
         first, second, grad_proj = lax.optimization_barrier((first, second, grad_proj))
         pieces = [ring(first, 1), ring(second, -1)]
-        gathered = gather_chan(grad_proj)
+        gathered = [grad_proj, swap(grad_proj, "chan", 1)]
+        far_grads, gathered[1] = lax.optimization_barrier((far_grads, gathered[1]))
+        gathered += [far_grads, swap(far_grads, "chan", 1)]
         weight_cols = after(weight_cols, gathered[2])
         weight_cols = [*weight_cols[:2], swap(weight_cols[2], "chan", 2), swap(weight_cols[3], "chan", 3)]
         grad_rows = input_gradient(gathered, weight_cols)

time: 107 us -> 107 us (level)
    ppermute x18, waiting for transfers between devices: 36.9 us -> 35.3 us  [swap(): return lax.ppermute(values, axis, [(i, i ^ mask) for i in range(size)])]
    ppermute x6, waiting for transfers between devices: 16.1 us -> 17.7 us  [ring(): lax.ppermute(found[-1], 'ctx', [(i, (i + step) % size) for i in range(siz...]
where the time goes in v6:
time: 107 us
  waiting for transfers between devices  53 us (50%)
  starting transfers between devices  26.6 us (25%)
  Pallas kernels  16.3 us (15%)
  local copies, waits for them, and re-layouts  8.93 us (8%)
    ppermute x18, waiting for transfers between devices, swap(): return lax.ppermute(values, axis, [(i, i ^ mask) for i in range(size)])  35.3 us
    ppermute x6, waiting for transfers between devices, ring(): lax.ppermute(found[-1], 'ctx', [(i, (i + step) % size) for i in range(siz...  17.7 us
    ppermute x18, starting transfers between devices, swap(): return lax.ppermute(values, axis, [(i, i ^ mask) for i in range(size)])  13.8 us
    unnamed x30, local copies, waits for them, and re-layouts  7.27 us
    ppermute x6, starting transfers between devices, ring(): lax.ppermute(found[-1], 'ctx', [(i, (i + step) % size) for i in range(siz...  6.41 us
    pallas_call x1, Pallas kernels, convolve(): pl.pallas_call(functools.partial(conv_kernel, blocks, chans, group, token...  5.87 us
    all_to_all x1, starting transfers between devices, per_device(): lax.all_to_all(turned, 'ctx', split_axis=0, concat_axis=0)  4.87 us
    pallas_call x3, Pallas kernels, project(): pl.pallas_call(body, out_shape=shape, in_specs=[VMEM] * (len(along) + 1 +...  2.95 us
  transfers between devices with their start and end apart: 26, of which 14 were waited for; matrix products, arithmetic and copies ran while one was open for 2% of the time, Pallas kernels for 14%

profile of v6, /device:TPU:0, one launch (start us, length us, event | category | flops | bytes accessed | tf_op | source)
XLA Modules:
  0.0 106.5 jit_solution(7608315574314485713)
XLA Ops:
  1.2 2.6 %collective-permute-start = (bf16[512,1024]{1,0:T(8,128)(2,1)}, bf16[512,1024]{1,0:T(8,128)(2,1)}, u32[]{:S(2)}, u32[]{:S(2)}) collective-permute-start(bf16[512,1024]{1,0:T(8,128)(2,1)} %values_ref.1), channel_id=1, source_target_pairs={{0,2},{1,3},{2,0},{3,1},{4,6},{5,7},{6,4},{7,5},{8,10},{9,11},{10,... | collective-permute-start | bytes 3145736 | tf_op jit(solution)/shard_map/ppermute | solution.py:473
  3.7 1.3 %copy-done.3 = bf16[512,1024]{1,0:T(8,128)(2,1)S(1)} copy-done((bf16[512,1024]{1,0:T(8,128)(2,1)S(1)}, bf16[512,1024]{1,0:T(8,128)(2,1)}, u32[]{:S(2)}) %copy-start.3) | copy-done | bytes 1048600
  7.0 4.9 %all-to-all-start = ((bf16[4,512,256]{2,1,0:T(8,128)(2,1)}), bf16[4,512,256]{2,1,0:T(8,128)(2,1)S(1)}, u32[]{:S(2)}, u32[]{:S(2)}) async-start(bf16[4,512,256]{2,1,0:T(8,128)(2,1)} %copy-done.2), calls=%async_computation | async-start | bytes 2097152 | tf_op jit(solution)/shard_map/all_to_all | solution.py:544
  11.9 1.1 constant_dynamic-slice_fusion
  14.4 1.2 %copy-done.4 = bf16[512,1024]{1,0:T(8,128)(2,1)S(1)} copy-done((bf16[512,1024]{1,0:T(8,128)(2,1)S(1)}, bf16[512,1024]{1,0:T(8,128)(2,1)}, u32[]{:S(2)}) %copy-start.4) | copy-done | bytes 1048600
  15.6 1.2 %copy-done.6 = bf16[512,1024]{1,0:T(8,128)(2,1)S(1)} copy-done((bf16[512,1024]{1,0:T(8,128)(2,1)S(1)}, bf16[512,1024]{1,0:T(8,128)(2,1)}, u32[]{:S(2)}) %copy-start.6) | copy-done | bytes 1048600
  17.6 10.2 %collective-permute-done.refs_0_ = bf16[512,1024]{1,0:T(8,128)(2,1)} collective-permute-done((bf16[512,1024]{1,0:T(8,128)(2,1)}, bf16[512,1024]{1,0:T(8,128)(2,1)}, u32[]{:S(2)}, u32[]{:S(2)}) %collective-permute-start) | collective-permute-done | bytes 1048608 | tf_op jit(solution)/shard_map/ppermute | solution.py:473
  27.8 1.7 %project.4.sum_ref = f32[512,192]{1,0:T(8,128)S(1)} custom-call(bf16[192,4096]{1,0:T(8,128)(2,1)S(1)} %bitcast.7, f32[512,192]{1,0:T(8,128)S(1)} %project.3.sum_ref, bf16[512,1024]{1,0:T(8,128)(2,1)} %collective-permute-done.refs_0_), custom_call_target="tpu_custom_call" | custom-call | flops 201326592 | bytes 1048576 | tf_op jit(solution)/shard_map/project/pallas_call | solution.py:244
  29.5 1.2 %collective-permute-done.3.refs_0_ = bf16[512,1024]{1,0:T(8,128)(2,1)S(1)} collective-permute-done((bf16[512,1024]{1,0:T(8,128)(2,1)}, bf16[512,1024]{1,0:T(8,128)(2,1)S(1)}, u32[]{:S(2)}, u32[]{:S(2)}) %collective-permute-start.3) | collective-permute-done | bytes 1048608 | tf_op jit(solution)/shard_map/ppermute | solution.py:473
  31.9 1.8 %collective-permute-start.4 = (bf16[80,512]{1,0:T(8,128)(2,1)S(1)}, bf16[80,512]{1,0:T(8,128)(2,1)S(1)}, u32[]{:S(2)}, u32[]{:S(2)}) collective-permute-start(bf16[80,512]{1,0:T(8,128)(2,1)S(1)} %get-tuple-element.55), channel_id=1, source_target_pairs={{0,4},{4,0},{8,12},{12,8},{1,5},{5,1},{9,13},{13,9},{2,6},{6,2},{1... | collective-permute-start | bytes 245768 | tf_op jit(solution)/shard_map/ppermute | solution.py:473
  33.7 2.6 %collective-permute-start.5 = (bf16[80,512]{1,0:T(8,128)(2,1)S(1)}, bf16[80,512]{1,0:T(8,128)(2,1)S(1)}, u32[]{:S(2)}, u32[]{:S(2)}) collective-permute-start(bf16[80,512]{1,0:T(8,128)(2,1)S(1)} %get-tuple-element.56), channel_id=1, source_target_pairs={{0,8},{4,12},{8,0},{12,4},{1,9},{5,13},{9,1},{13,5},{2,10},{6,14},... | collective-permute-start | bytes 245768 | tf_op jit(solution)/shard_map/ppermute | solution.py:473
  36.3 4.2 %collective-permute-done.4.refs_2_ = bf16[80,512]{1,0:T(8,128)(2,1)S(1)} collective-permute-done((bf16[80,512]{1,0:T(8,128)(2,1)S(1)}, bf16[80,512]{1,0:T(8,128)(2,1)S(1)}, u32[]{:S(2)}, u32[]{:S(2)}) %collective-permute-start.4) | collective-permute-done | bytes 81952 | tf_op jit(solution)/shard_map/ppermute | solution.py:473
  40.5 3.6 %collective-permute-done.5.refs_3_ = bf16[80,512]{1,0:T(8,128)(2,1)S(1)} collective-permute-done((bf16[80,512]{1,0:T(8,128)(2,1)S(1)}, bf16[80,512]{1,0:T(8,128)(2,1)S(1)}, u32[]{:S(2)}, u32[]{:S(2)}) %collective-permute-start.5) | collective-permute-done | bytes 81952 | tf_op jit(solution)/shard_map/ppermute | solution.py:473
  44.8 5.9 %conv.1 = (bf16[48,2432]{1,0:T(8,128)(2,1)}, bf16[48,2432]{1,0:T(8,128)(2,1)}, bf16[48,2432]{1,0:T(8,128)(2,1)}, bf16[48,2432]{1,0:T(8,128)(2,1)}) custom-call(f32[1,16]{1,0:T(1,128)} %dynamic-slice_bitcast_fusion.refs_0_, bf16[80,512]{1,0:T(8,128)(2,1)} %copy-done.9, bf16[80,512]{1,0:T(8,128)(2,1)} %copy-done.12, bf16[80,512]{1,0:T(8,128)(2,1)} %copy-done.13, ...), custom_call_target="tpu_custom_call" | custom-call | flops 962592768 | bytes 4194304 | tf_op jit(solution)/shard_map/conv/pallas_call | solution.py:184
  50.7 2.4 %collective-permute-start.9 = (bf16[48,2432]{1,0:T(8,128)(2,1)}, bf16[48,2432]{1,0:T(8,128)(2,1)S(1)}, u32[]{:S(2)}, u32[]{:S(2)}) collective-permute-start(bf16[48,2432]{1,0:T(8,128)(2,1)} %get-tuple-element.67), channel_id=1, source_target_pairs={{0,8},{4,12},{8,0},{12,4},{1,9},{5,13},{9,1},{13,5},{2,10},{6,14},... | collective-permute-start | bytes 700424 | tf_op jit(solution)/shard_map/ppermute | solution.py:473
  53.8 1.6 %collective-permute-start.10 = (bf16[48,2432]{1,0:T(8,128)(2,1)}, bf16[48,2432]{1,0:T(8,128)(2,1)S(1)}, u32[]{:S(2)}, u32[]{:S(2)}) collective-permute-start(bf16[48,2432]{1,0:T(8,128)(2,1)} %get-tuple-element.68), channel_id=1, source_target_pairs={{4,8},{8,4},{0,0},{12,12},{5,9},{9,5},{1,1},{13,13},{6,10},{10,6},... | collective-permute-start | bytes 700424 | tf_op jit(solution)/shard_map/ppermute | solution.py:564
  55.4 9.3 %collective-permute-done.9.refs_2_ = bf16[48,2432]{1,0:T(8,128)(2,1)S(1)} collective-permute-done((bf16[48,2432]{1,0:T(8,128)(2,1)}, bf16[48,2432]{1,0:T(8,128)(2,1)S(1)}, u32[]{:S(2)}, u32[]{:S(2)}) %collective-permute-start.9) | collective-permute-done | bytes 233504 | tf_op jit(solution)/shard_map/ppermute | solution.py:473
  65.7 5.1 %collective-permute-done.11.refs_4_ = bf16[48,2432]{1,0:T(8,128)(2,1)S(1)} collective-permute-done((bf16[48,2432]{1,0:T(8,128)(2,1)S(1)}, bf16[48,2432]{1,0:T(8,128)(2,1)S(1)}, u32[]{:S(2)}, u32[]{:S(2)}) %collective-permute-start.11) | collective-permute-done | bytes 233504 | tf_op jit(solution)/shard_map/ppermute | solution.py:473
  70.8 1.4 %products.2 = (bf16[192,2048]{1,0:T(8,128)(2,1)S(1)}, bf16[192,768]{1,0:T(8,128)(2,1)S(1)}, bf16[192,512]{1,0:T(8,128)(2,1)S(1)}, f32[64,512]{1,0:T(8,128)}) custom-call(bf16[48,2432]{1,0:T(8,128)(2,1)S(1)} %keep.1.refs_0_, bf16[48,2432]{1,0:T(8,128)(2,1)S(1)} %collective-permute-done.8.refs_1_, bf16[48,2432]{1,0:T(8,128)(2,1)S(1)} %collective-permute-done.9.refs_2_, ...), custom_call_target="tpu_custom_call" | custom-call | flops 603979776 | bytes 4194304 | tf_op jit(solution)/shard_map/products/pallas_call | solution.py:301
  72.2 1.1 %collective-permute-start.14 = (bf16[192,512]{1,0:T(8,128)(2,1)S(1)}, bf16[192,512]{1,0:T(8,128)(2,1)S(1)}, u32[]{:S(2)}, u32[]{:S(2)}) collective-permute-start(bf16[192,512]{1,0:T(8,128)(2,1)S(1)} %get-tuple-element.80.refs_0_), channel_id=1, source_target_pairs={{0,2},{1,3},{2,0},{3,1},{4,6},{5,7},{6,4},{7,5},{8,10},{9,11},{10,... | collective-permute-start | bytes 589832 | tf_op jit(solution)/shard_map/ppermute | solution.py:473
  74.0 3.8 %collective-permute-start.22 = (bf16[96,1024]{1,0:T(8,128)(2,1)S(1)}, bf16[96,1024]{1,0:T(8,128)(2,1)S(1)}, u32[]{:S(2)}, u32[]{:S(2)}) collective-permute-start(bf16[96,1024]{1,0:T(8,128)(2,1)S(1)} %get-tuple-element.92.refs_3_), channel_id=1, source_target_pairs={{0,12},{4,0},{8,4},{12,8},{1,13},{5,1},{9,5},{13,9},{2,14},{6,2},{... | collective-permute-start | bytes 589832 | tf_op jit(solution)/shard_map/ppermute | solution.py:492
  77.9 1.6 %collective-permute-done.14.refs_2_ = bf16[192,512]{1,0:T(8,128)(2,1)S(1)} collective-permute-done((bf16[192,512]{1,0:T(8,128)(2,1)S(1)}, bf16[192,512]{1,0:T(8,128)(2,1)S(1)}, u32[]{:S(2)}, u32[]{:S(2)}) %collective-permute-start.14) | collective-permute-done | bytes 196640 | tf_op jit(solution)/shard_map/ppermute | solution.py:473
  79.5 1.1 %collective-permute-start.17 = (bf16[192,1024]{1,0:T(8,128)(2,1)S(1)}, bf16[192,1024]{1,0:T(8,128)(2,1)S(1)}, u32[]{:S(2)}, u32[]{:S(2)}) collective-permute-start(bf16[192,1024]{1,0:T(8,128)(2,1)S(1)} %copy-done.11), channel_id=1, source_target_pairs={{0,2},{1,3},{2,0},{3,1},{4,6},{5,7},{6,4},{7,5},{8,10},{9,11},{10,... | collective-permute-start | bytes 1179656 | tf_op jit(solution)/shard_map/ppermute | solution.py:473
  80.6 3.0 %collective-permute-done.19.refs_1_ = bf16[96,1024]{1,0:T(8,128)(2,1)S(1)} collective-permute-done((bf16[96,1024]{1,0:T(8,128)(2,1)S(1)}, bf16[96,1024]{1,0:T(8,128)(2,1)S(1)}, u32[]{:S(2)}, u32[]{:S(2)}) %collective-permute-start.19) | collective-permute-done | bytes 196640 | tf_op jit(solution)/shard_map/ppermute | solution.py:492
  83.6 1.8 %collective-permute-done.22.refs_4_ = bf16[96,1024]{1,0:T(8,128)(2,1)S(1)} collective-permute-done((bf16[96,1024]{1,0:T(8,128)(2,1)S(1)}, bf16[96,1024]{1,0:T(8,128)(2,1)S(1)}, u32[]{:S(2)}, u32[]{:S(2)}) %collective-permute-start.22) | collective-permute-done | bytes 196640 | tf_op jit(solution)/shard_map/ppermute | solution.py:492
  85.4 2.3 %collective-permute-start.23 = (bf16[96,1024]{1,0:T(8,128)(2,1)S(1)}, bf16[96,1024]{1,0:T(8,128)(2,1)S(1)}, u32[]{:S(2)}, u32[]{:S(2)}) collective-permute-start(bf16[96,1024]{1,0:T(8,128)(2,1)S(1)} %collective-permute-done.22.refs_4_), channel_id=1, source_target_pairs={{0,12},{4,0},{8,4},{12,8},{1,13},{5,1},{9,5},{13,9},{2,14},{6,2},{... | collective-permute-start | bytes 589832 | tf_op jit(solution)/shard_map/ppermute | solution.py:492
  87.7 5.5 %collective-permute-done.20.refs_2_ = bf16[96,1024]{1,0:T(8,128)(2,1)S(1)} collective-permute-done((bf16[96,1024]{1,0:T(8,128)(2,1)S(1)}, bf16[96,1024]{1,0:T(8,128)(2,1)S(1)}, u32[]{:S(2)}, u32[]{:S(2)}) %collective-permute-start.20) | collective-permute-done | bytes 196640 | tf_op jit(solution)/shard_map/ppermute | solution.py:492
  93.2 3.9 %collective-permute-done.23.refs_5_ = bf16[96,1024]{1,0:T(8,128)(2,1)S(1)} collective-permute-done((bf16[96,1024]{1,0:T(8,128)(2,1)S(1)}, bf16[96,1024]{1,0:T(8,128)(2,1)S(1)}, u32[]{:S(2)}, u32[]{:S(2)}) %collective-permute-start.23) | collective-permute-done | bytes 196640 | tf_op jit(solution)/shard_map/ppermute | solution.py:492
  97.4 2.2 %place.2.refs_2_ = f32[192,4096]{1,0:T(8,128)} custom-call(bf16[96,1024]{1,0:T(8,128)(2,1)S(1)} %get-tuple-element.91.refs_0_, bf16[96,1024]{1,0:T(8,128)(2,1)S(1)} %collective-permute-done.19.refs_1_, bf16[96,1024]{1,0:T(8,128)(2,1)S(1)} %collective-permute-done.20.refs_2_, bf16[96,1024]{1,0:T(8,128)(2,1)S(1)} %get-tuple-element.92.refs_3_, ...), custom_call_target="tpu_custom_call" | custom-call | bytes 6291456 | tf_op jit(solution)/shard_map/place/pallas_call | solution.py:443
  99.6 2.3 %inputs.1 = bf16[512,1024]{1,0:T(8,128)(2,1)} custom-call(bf16[192,512]{1,0:T(8,128)(2,1)S(1)} %get-tuple-element.80.refs_0_, bf16[192,512]{1,0:T(8,128)(2,1)S(1)} %collective-permute-done.15.refs_1_, bf16[192,512]{1,0:T(8,128)(2,1)S(1)} %collective-permute-done.14.refs_2_, bf16[192,512]{1,0:T(8,128)(2,1)S(1)} %collective-permute-done.16.refs_3_, ...), custom_call_target="tpu_custom_call" | custom-call | flops 805306368 | bytes 4194304 | tf_op jit(solution)/shard_map/inputs/pallas_call | solution.py:380
  102.5 2.9 %collective-permute-done.24.refs_1_ = bf16[96,1024]{1,0:T(8,128)(2,1)S(1)} collective-permute-done((bf16[96,1024]{1,0:T(8,128)(2,1)S(1)}, bf16[96,1024]{1,0:T(8,128)(2,1)S(1)}, u32[]{:S(2)}, u32[]{:S(2)}) %collective-permute-start.24) | collective-permute-done | bytes 196640 | tf_op jit(solution)/shard_map/ppermute | solution.py:492
  105.4 1.1 %place.3 = f32[192,4096]{1,0:T(8,128)} custom-call(bf16[96,1024]{1,0:T(8,128)(2,1)S(1)} %collective-permute-done.21.refs_0_, bf16[96,1024]{1,0:T(8,128)(2,1)S(1)} %collective-permute-done.24.refs_1_, f32[192,4096]{1,0:T(8,128)} %place.2.refs_2_), custom_call_target="tpu_custom_call", output_to_operand_aliasing={{}: (2, {})} | custom-call | bytes 1048576 | tf_op jit(solution)/shard_map/place/pallas_call | solution.py:453
  (64 shorter events, 9.9 us)
Async XLA Ops:
  0.6 13.2 %copy-start = (f32[64]{0:T(128)S(1)}, f32[64]{0:T(128)}, u32[]{:S(2)}) copy-start(f32[64]{0:T(128)} %param.13) | copy-start | bytes 772
  0.6 11.2 %copy-start.1 = (bf16[3,64,4096]{2,1,0:T(8,128)(2,1)S(1)}, bf16[3,64,4096]{2,1,0:T(8,128)(2,1)}, u32[]{:S(2)}) copy-start(bf16[3,64,4096]{2,1,0:T(8,128)(2,1)} %param.11) | copy-start | bytes 4718596
  0.7 5.4 %collective-permute-start.1 = (bf16[512,1024]{1,0:T(8,128)(2,1)}, bf16[512,1024]{1,0:T(8,128)(2,1)S(1)}, u32[]{:S(2)}, u32[]{:S(2)}) collective-permute-start(bf16[512,1024]{1,0:T(8,128)(2,1)} %values_ref.1), channel_id=1, source_target_pairs={{0,1},{1,0},{2,3},{3,2},{4,5},{5,4},{6,7},{7,6},{8,9},{9,8},{10,11... | collective-permute-start | bytes 3145736 | tf_op jit(solution)/shard_map/ppermute | solution.py:473
  1.2 26.6 %collective-permute-start = (bf16[512,1024]{1,0:T(8,128)(2,1)}, bf16[512,1024]{1,0:T(8,128)(2,1)}, u32[]{:S(2)}, u32[]{:S(2)}) collective-permute-start(bf16[512,1024]{1,0:T(8,128)(2,1)} %values_ref.1), channel_id=1, source_target_pairs={{0,2},{1,3},{2,0},{3,1},{4,6},{5,7},{6,4},{7,5},{8,10},{9,11},{10,... | collective-permute-start | bytes 3145736 | tf_op jit(solution)/shard_map/ppermute | solution.py:473
  7.0 37.1 %all-to-all-start = ((bf16[4,512,256]{2,1,0:T(8,128)(2,1)}), bf16[4,512,256]{2,1,0:T(8,128)(2,1)S(1)}, u32[]{:S(2)}, u32[]{:S(2)}) async-start(bf16[4,512,256]{2,1,0:T(8,128)(2,1)} %copy-done.2), calls=%async_computation | async-start | bytes 2097152 | tf_op jit(solution)/shard_map/all_to_all | solution.py:544
  13.0 4.7 %collective-permute-start.2 = (bf16[192,1024]{1,0:T(8,128)(2,1)}, bf16[192,1024]{1,0:T(8,128)(2,1)S(1)}, u32[]{:S(2)}, u32[]{:S(2)}) collective-permute-start(bf16[192,1024]{1,0:T(8,128)(2,1)} %get-tuple-element.99), channel_id=1, source_target_pairs={{0,1},{1,0},{2,3},{3,2},{4,5},{5,4},{6,7},{7,6},{8,9},{9,8},{10,11... | collective-permute-start | bytes 1179656 | tf_op jit(solution)/shard_map/ppermute | solution.py:473
  16.9 13.8 %copy-start.8 = (f32[64,512]{1,0:T(8,128)S(1)}, f32[64,512]{1,0:T(8,128)}, u32[]{:S(2)}) copy-start(f32[64,512]{1,0:T(8,128)} %filter_ref) | copy-start | bytes 393220
  27.8 2.9 %collective-permute-start.3 = (bf16[512,1024]{1,0:T(8,128)(2,1)}, bf16[512,1024]{1,0:T(8,128)(2,1)S(1)}, u32[]{:S(2)}, u32[]{:S(2)}) collective-permute-start(bf16[512,1024]{1,0:T(8,128)(2,1)} %collective-permute-done.refs_0_), channel_id=1, source_target_pairs={{0,1},{1,0},{2,3},{3,2},{4,5},{5,4},{6,7},{7,6},{8,9},{9,8},{10,11... | collective-permute-start | bytes 3145736 | tf_op jit(solution)/shard_map/ppermute | solution.py:473
  31.9 8.6 %collective-permute-start.4 = (bf16[80,512]{1,0:T(8,128)(2,1)S(1)}, bf16[80,512]{1,0:T(8,128)(2,1)S(1)}, u32[]{:S(2)}, u32[]{:S(2)}) collective-permute-start(bf16[80,512]{1,0:T(8,128)(2,1)S(1)} %get-tuple-element.55), channel_id=1, source_target_pairs={{0,4},{4,0},{8,12},{12,8},{1,5},{5,1},{9,13},{13,9},{2,6},{6,2},{1... | collective-permute-start | bytes 245768 | tf_op jit(solution)/shard_map/ppermute | solution.py:473
  33.7 10.4 %collective-permute-start.5 = (bf16[80,512]{1,0:T(8,128)(2,1)S(1)}, bf16[80,512]{1,0:T(8,128)(2,1)S(1)}, u32[]{:S(2)}, u32[]{:S(2)}) collective-permute-start(bf16[80,512]{1,0:T(8,128)(2,1)S(1)} %get-tuple-element.56), channel_id=1, source_target_pairs={{0,8},{4,12},{8,0},{12,4},{1,9},{5,13},{9,1},{13,5},{2,10},{6,14},... | collective-permute-start | bytes 245768 | tf_op jit(solution)/shard_map/ppermute | solution.py:473
  36.3 7.8 %collective-permute-start.6 = (bf16[80,512]{1,0:T(8,128)(2,1)S(1)}, bf16[80,512]{1,0:T(8,128)(2,1)S(1)}, u32[]{:S(2)}, u32[]{:S(2)}) collective-permute-start(bf16[80,512]{1,0:T(8,128)(2,1)S(1)} %get-tuple-element.57), channel_id=1, source_target_pairs={{0,12},{4,8},{8,4},{12,0},{1,13},{5,9},{9,5},{13,1},{2,14},{6,10},... | collective-permute-start | bytes 245768 | tf_op jit(solution)/shard_map/ppermute | solution.py:473
  40.5 4.3 %copy-start.12 = (bf16[80,512]{1,0:T(8,128)(2,1)}, bf16[80,512]{1,0:T(8,128)(2,1)S(1)}, u32[]{:S(2)}) copy-start(bf16[80,512]{1,0:T(8,128)(2,1)S(1)} %collective-permute-done.4.refs_2_) | copy-start | bytes 245764
  44.1 26.6 %collective-permute-start.7 = (bf16[2048,256]{1,0:T(8,128)(2,1)S(1)}, bf16[2048,256]{1,0:T(8,128)(2,1)S(1)}, u32[]{:S(2)}, u32[]{:S(2)}) collective-permute-start(bf16[2048,256]{1,0:T(8,128)(2,1)S(1)} %bitcast.9), channel_id=1, source_target_pairs={{0,2},{1,3},{2,0},{3,1},{4,6},{5,7},{6,4},{7,5},{8,10},{9,11},{10,... | collective-permute-start | bytes 3145736 | tf_op jit(solution)/shard_map/ppermute | solution.py:473
  50.7 14.0 %collective-permute-start.9 = (bf16[48,2432]{1,0:T(8,128)(2,1)}, bf16[48,2432]{1,0:T(8,128)(2,1)S(1)}, u32[]{:S(2)}, u32[]{:S(2)}) collective-permute-start(bf16[48,2432]{1,0:T(8,128)(2,1)} %get-tuple-element.67), channel_id=1, source_target_pairs={{0,8},{4,12},{8,0},{12,4},{1,9},{5,13},{9,1},{13,5},{2,10},{6,14},... | collective-permute-start | bytes 700424 | tf_op jit(solution)/shard_map/ppermute | solution.py:473
  53.1 12.6 %collective-permute-start.8 = (bf16[48,2432]{1,0:T(8,128)(2,1)}, bf16[48,2432]{1,0:T(8,128)(2,1)S(1)}, u32[]{:S(2)}, u32[]{:S(2)}) collective-permute-start(bf16[48,2432]{1,0:T(8,128)(2,1)} %get-tuple-element.66), channel_id=1, source_target_pairs={{0,4},{4,0},{8,12},{12,8},{1,5},{5,1},{9,13},{13,9},{2,6},{6,2},{1... | collective-permute-start | bytes 700424 | tf_op jit(solution)/shard_map/ppermute | solution.py:473
  53.8 11.9 %collective-permute-start.10 = (bf16[48,2432]{1,0:T(8,128)(2,1)}, bf16[48,2432]{1,0:T(8,128)(2,1)S(1)}, u32[]{:S(2)}, u32[]{:S(2)}) collective-permute-start(bf16[48,2432]{1,0:T(8,128)(2,1)} %get-tuple-element.68), channel_id=1, source_target_pairs={{4,8},{8,4},{0,0},{12,12},{5,9},{9,5},{1,1},{13,13},{6,10},{10,6},... | collective-permute-start | bytes 700424 | tf_op jit(solution)/shard_map/ppermute | solution.py:564
  64.7 6.1 %collective-permute-start.11 = (bf16[48,2432]{1,0:T(8,128)(2,1)S(1)}, bf16[48,2432]{1,0:T(8,128)(2,1)S(1)}, u32[]{:S(2)}, u32[]{:S(2)}) collective-permute-start(bf16[48,2432]{1,0:T(8,128)(2,1)S(1)} %collective-permute-done.9.refs_2_), channel_id=1, source_target_pairs={{0,4},{4,0},{8,12},{12,8},{1,5},{5,1},{9,13},{13,9},{2,6},{6,2},{1... | collective-permute-start | bytes 700424 | tf_op jit(solution)/shard_map/ppermute | solution.py:473
  64.7 6.1 %collective-permute-start.12 = (bf16[2048,256]{1,0:T(8,128)(2,1)S(1)}, bf16[2048,256]{1,0:T(8,128)(2,1)S(1)}, u32[]{:S(2)}, u32[]{:S(2)}) collective-permute-start(bf16[2048,256]{1,0:T(8,128)(2,1)S(1)} %bitcast.10), channel_id=1, source_target_pairs={{0,1},{1,0},{2,3},{3,2},{4,5},{5,4},{6,7},{7,6},{8,9},{9,8},{10,11... | collective-permute-start | bytes 3145736 | tf_op jit(solution)/shard_map/ppermute | solution.py:473
  65.7 13.8 %copy-start.11 = (bf16[192,1024]{1,0:T(8,128)(2,1)S(1)}, bf16[192,1024]{1,0:T(8,128)(2,1)}, u32[]{:S(2)}) copy-start(bf16[192,1024]{1,0:T(8,128)(2,1)} %get-tuple-element.89) | copy-start | bytes 1179652
  65.7 14.9 %copy-start.10 = (bf16[192,1024]{1,0:T(8,128)(2,1)S(1)}, bf16[192,1024]{1,0:T(8,128)(2,1)}, u32[]{:S(2)}) copy-start(bf16[192,1024]{1,0:T(8,128)(2,1)} %get-tuple-element.90) | copy-start | bytes 1179652
  70.8 2.7 %collective-permute-start.13 = (bf16[2048,256]{1,0:T(8,128)(2,1)S(1)}, bf16[2048,256]{1,0:T(8,128)(2,1)S(1)}, u32[]{:S(2)}, u32[]{:S(2)}) collective-permute-start(bf16[2048,256]{1,0:T(8,128)(2,1)S(1)} %collective-permute-done.7.refs_7_), channel_id=1, source_target_pairs={{0,1},{1,0},{2,3},{3,2},{4,5},{5,4},{6,7},{7,6},{8,9},{9,8},{10,11... | collective-permute-start | bytes 3145736 | tf_op jit(solution)/shard_map/ppermute | solution.py:473
  72.2 7.3 %collective-permute-start.14 = (bf16[192,512]{1,0:T(8,128)(2,1)S(1)}, bf16[192,512]{1,0:T(8,128)(2,1)S(1)}, u32[]{:S(2)}, u32[]{:S(2)}) collective-permute-start(bf16[192,512]{1,0:T(8,128)(2,1)S(1)} %get-tuple-element.80.refs_0_), channel_id=1, source_target_pairs={{0,2},{1,3},{2,0},{3,1},{4,6},{5,7},{6,4},{7,5},{8,10},{9,11},{10,... | collective-permute-start | bytes 589832 | tf_op jit(solution)/shard_map/ppermute | solution.py:473
  73.8 5.7 %collective-permute-start.15 = (bf16[192,512]{1,0:T(8,128)(2,1)S(1)}, bf16[192,512]{1,0:T(8,128)(2,1)S(1)}, u32[]{:S(2)}, u32[]{:S(2)}) collective-permute-start(bf16[192,512]{1,0:T(8,128)(2,1)S(1)} %get-tuple-element.80.refs_0_), channel_id=1, source_target_pairs={{0,1},{1,0},{2,3},{3,2},{4,5},{5,4},{6,7},{7,6},{8,9},{9,8},{10,11... | collective-permute-start | bytes 589832 | tf_op jit(solution)/shard_map/ppermute | solution.py:473
  74.0 9.6 %collective-permute-start.19 = (bf16[96,1024]{1,0:T(8,128)(2,1)S(1)}, bf16[96,1024]{1,0:T(8,128)(2,1)S(1)}, u32[]{:S(2)}, u32[]{:S(2)}) collective-permute-start(bf16[96,1024]{1,0:T(8,128)(2,1)S(1)} %get-tuple-element.91.refs_0_), channel_id=1, source_target_pairs={{0,4},{4,8},{8,12},{12,0},{1,5},{5,9},{9,13},{13,1},{2,6},{6,10},{... | collective-permute-start | bytes 589832 | tf_op jit(solution)/shard_map/ppermute | solution.py:492
  74.0 11.4 %collective-permute-start.22 = (bf16[96,1024]{1,0:T(8,128)(2,1)S(1)}, bf16[96,1024]{1,0:T(8,128)(2,1)S(1)}, u32[]{:S(2)}, u32[]{:S(2)}) collective-permute-start(bf16[96,1024]{1,0:T(8,128)(2,1)S(1)} %get-tuple-element.92.refs_3_), channel_id=1, source_target_pairs={{0,12},{4,0},{8,4},{12,8},{1,13},{5,1},{9,5},{13,9},{2,14},{6,2},{... | collective-permute-start | bytes 589832 | tf_op jit(solution)/shard_map/ppermute | solution.py:492
  79.5 20.1 %collective-permute-start.17 = (bf16[192,1024]{1,0:T(8,128)(2,1)S(1)}, bf16[192,1024]{1,0:T(8,128)(2,1)S(1)}, u32[]{:S(2)}, u32[]{:S(2)}) collective-permute-start(bf16[192,1024]{1,0:T(8,128)(2,1)S(1)} %copy-done.11), channel_id=1, source_target_pairs={{0,2},{1,3},{2,0},{3,1},{4,6},{5,7},{6,4},{7,5},{8,10},{9,11},{10,... | collective-permute-start | bytes 1179656 | tf_op jit(solution)/shard_map/ppermute | solution.py:473
  80.6 18.9 %collective-permute-start.18 = (bf16[192,1024]{1,0:T(8,128)(2,1)S(1)}, bf16[192,1024]{1,0:T(8,128)(2,1)S(1)}, u32[]{:S(2)}, u32[]{:S(2)}) collective-permute-start(bf16[192,1024]{1,0:T(8,128)(2,1)S(1)} %copy-done.10), channel_id=1, source_target_pairs={{0,3},{1,2},{2,1},{3,0},{4,7},{5,6},{6,5},{7,4},{8,11},{9,10},{10,... | collective-permute-start | bytes 1179656 | tf_op jit(solution)/shard_map/ppermute | solution.py:473
  83.6 9.6 %collective-permute-start.20 = (bf16[96,1024]{1,0:T(8,128)(2,1)S(1)}, bf16[96,1024]{1,0:T(8,128)(2,1)S(1)}, u32[]{:S(2)}, u32[]{:S(2)}) collective-permute-start(bf16[96,1024]{1,0:T(8,128)(2,1)S(1)} %collective-permute-done.19.refs_1_), channel_id=1, source_target_pairs={{0,4},{4,8},{8,12},{12,0},{1,5},{5,9},{9,13},{13,1},{2,6},{6,10},{... | collective-permute-start | bytes 589832 | tf_op jit(solution)/shard_map/ppermute | solution.py:492
  85.4 11.7 %collective-permute-start.23 = (bf16[96,1024]{1,0:T(8,128)(2,1)S(1)}, bf16[96,1024]{1,0:T(8,128)(2,1)S(1)}, u32[]{:S(2)}, u32[]{:S(2)}) collective-permute-start(bf16[96,1024]{1,0:T(8,128)(2,1)S(1)} %collective-permute-done.22.refs_4_), channel_id=1, source_target_pairs={{0,12},{4,0},{8,4},{12,8},{1,13},{5,1},{9,5},{13,9},{2,14},{6,2},{... | collective-permute-start | bytes 589832 | tf_op jit(solution)/shard_map/ppermute | solution.py:492
  87.7 11.8 %collective-permute-start.16 = (bf16[192,512]{1,0:T(8,128)(2,1)S(1)}, bf16[192,512]{1,0:T(8,128)(2,1)S(1)}, u32[]{:S(2)}, u32[]{:S(2)}) collective-permute-start(bf16[192,512]{1,0:T(8,128)(2,1)S(1)} %collective-permute-done.14.refs_2_), channel_id=1, source_target_pairs={{0,1},{1,0},{2,3},{3,2},{4,5},{5,4},{6,7},{7,6},{8,9},{9,8},{10,11... | collective-permute-start | bytes 589832 | tf_op jit(solution)/shard_map/ppermute | solution.py:473
  93.2 9.2 %collective-permute-start.21 = (bf16[96,1024]{1,0:T(8,128)(2,1)S(1)}, bf16[96,1024]{1,0:T(8,128)(2,1)S(1)}, u32[]{:S(2)}, u32[]{:S(2)}) collective-permute-start(bf16[96,1024]{1,0:T(8,128)(2,1)S(1)} %collective-permute-done.20.refs_2_), channel_id=1, source_target_pairs={{0,4},{4,8},{8,12},{12,0},{1,5},{5,9},{9,13},{13,1},{2,6},{6,10},{... | collective-permute-start | bytes 589832 | tf_op jit(solution)/shard_map/ppermute | solution.py:492
  97.1 8.3 %collective-permute-start.24 = (bf16[96,1024]{1,0:T(8,128)(2,1)S(1)}, bf16[96,1024]{1,0:T(8,128)(2,1)S(1)}, u32[]{:S(2)}, u32[]{:S(2)}) collective-permute-start(bf16[96,1024]{1,0:T(8,128)(2,1)S(1)} %collective-permute-done.23.refs_5_), channel_id=1, source_target_pairs={{0,12},{4,0},{8,4},{12,8},{1,13},{5,1},{9,5},{13,9},{2,14},{6,2},{... | collective-permute-start | bytes 589832 | tf_op jit(solution)/shard_map/ppermute | solution.py:492
  (9 other events, 8.5 us)

commit v7 on v6

--- a/solution.py
+++ b/solution.py
@@ -107,8 +107,10 @@
         copy.wait()
     part = twiddle_ref.shape[1]
     cos, sin = twiddle_ref[0], twiddle_ref[1]
-    for start in range(0, chans, group):
-        picked = []
+    starts = range(0, chans, group)
+    sets = 3 * len(starts)
+    picked = []
+    for start in starts:
         for q in range(3):
             tiles = []
             for z in range(blocks):
@@ -117,38 +119,35 @@
                 for n in range(cuts):
                     tiles.append(loaded[:, n * LANES : (n + 1) * LANES])
             picked.append(jnp.concatenate(tiles, axis=0))
-        first = table_left(fwd_ref, jnp.concatenate(picked, axis=1))
-        turned = []
+    first = table_left(fwd_ref, jnp.concatenate(picked, axis=1))
+    turned = []
+    for i in range(sets):
+        re = first[:part, i * LANES : (i + 1) * LANES]
+        im = first[part:, i * LANES : (i + 1) * LANES]
+        turned.append(jnp.concatenate([re * cos + im * sin, im * cos - re * sin], axis=1))
+    spectra = table_right(jnp.concatenate(turned, axis=0), second_ref)
+    products = []
+    for g in range(0, sets, 3):
+        (fr, fi), (gr, gi), (ur, ui) = [
+            (spectra[i * part : (i + 1) * part, :LANES], spectra[i * part : (i + 1) * part, LANES:])
+            for i in range(g, g + 3)
+        ]
+        products.append(jnp.concatenate([fr * gr - fi * gi, fr * gi + fi * gr], axis=1))
+        products.append(jnp.concatenate([fr * ur + fi * ui, fr * ui - fi * ur], axis=1))
+        products.append(jnp.concatenate([gr * ur + gi * ui, gr * ui - gi * ur], axis=1))
+    back = table_right(jnp.concatenate(products, axis=0), back_ref)
+    turned = []
+    for i in range(sets):
+        re = back[i * part : (i + 1) * part, :LANES]
+        im = back[i * part : (i + 1) * part, LANES:]
+        turned.append(jnp.concatenate([re * cos - im * sin, im * cos + re * sin], axis=0))
+    final = table_left(inv_ref, jnp.concatenate(turned, axis=1))
+    for g, start in enumerate(starts):
         for q in range(3):
-            re = first[:part, q * LANES : (q + 1) * LANES]
-            im = first[part:, q * LANES : (q + 1) * LANES]
-            turned.append(jnp.concatenate([re * cos + im * sin, im * cos - re * sin], axis=1))
-        spectra = table_right(jnp.concatenate(turned, axis=0), second_ref)
-        parts = [
-            (spectra[q * part : (q + 1) * part, :LANES], spectra[q * part : (q + 1) * part, LANES:])
-            for q in range(3)
-        ]
-        (fr, fi), (gr, gi), (ur, ui) = parts
-        products = jnp.concatenate(
-            [
-                jnp.concatenate([fr * gr - fi * gi, fr * gi + fi * gr], axis=1),
-                jnp.concatenate([fr * ur + fi * ui, fr * ui - fi * ur], axis=1),
-                jnp.concatenate([gr * ur + gi * ui, gr * ui - gi * ur], axis=1),
-            ],
-            axis=0,
-        )
-        back = table_right(products, back_ref)
-        turned = []
-        for q in range(3):
-            re = back[q * part : (q + 1) * part, :LANES]
-            im = back[q * part : (q + 1) * part, LANES:]
-            turned.append(jnp.concatenate([re * cos - im * sin, im * cos + re * sin], axis=0))
-        final = table_left(inv_ref, jnp.concatenate(turned, axis=1))
-        for q in range(3):
+            at = (3 * g + q) * LANES
             for z in range(blocks):
                 tiles = [
-                    final[(z * cuts + n) * group : (z * cuts + n + 1) * group, q * LANES : (q + 1) * LANES]
-                    for n in range(cuts)
+                    final[(z * cuts + n) * group : (z * cuts + n + 1) * group, at : at + LANES] for n in range(cuts)
                 ]
                 results[q, z, start : start + group, :] = jnp.concatenate(tiles, axis=1)
     down = lax.broadcasted_iota(jnp.int32, (chans, chans), 0)

time: 107 us -> 106 us (level)
  no operation moved by 1% of the time
where the time goes in v7:
time: 106 us
  waiting for transfers between devices  53 us (50%)
  starting transfers between devices  26.6 us (25%)
  Pallas kernels  15.7 us (15%)
  local copies, waits for them, and re-layouts  8.93 us (8%)
    ppermute x18, waiting for transfers between devices, swap(): return lax.ppermute(values, axis, [(i, i ^ mask) for i in range(size)])  35.3 us
    ppermute x6, waiting for transfers between devices, ring(): lax.ppermute(found[-1], 'ctx', [(i, (i + step) % size) for i in range(siz...  17.7 us
    ppermute x18, starting transfers between devices, swap(): return lax.ppermute(values, axis, [(i, i ^ mask) for i in range(size)])  13.8 us
    unnamed x30, local copies, waits for them, and re-layouts  7.27 us
    ppermute x6, starting transfers between devices, ring(): lax.ppermute(found[-1], 'ctx', [(i, (i + step) % size) for i in range(siz...  6.42 us
    pallas_call x1, Pallas kernels, convolve(): pl.pallas_call(functools.partial(conv_kernel, blocks, chans, group, token...  5.34 us
    all_to_all x1, starting transfers between devices, per_device(): lax.all_to_all(turned, 'ctx', split_axis=0, concat_axis=0)  4.87 us
    pallas_call x3, Pallas kernels, project(): pl.pallas_call(body, out_shape=shape, in_specs=[VMEM] * (len(along) + 1 +...  2.95 us
  transfers between devices with their start and end apart: 26, of which 14 were waited for; matrix products, arithmetic and copies ran while one was open for 2% of the time, Pallas kernels for 14%

profile of v7, /device:TPU:0, one launch (start us, length us, event | category | flops | bytes accessed | tf_op | source)
XLA Modules:
  0.0 106.0 jit_solution(14806097479241894021)
XLA Ops:
  1.2 2.6 %collective-permute-start = (bf16[512,1024]{1,0:T(8,128)(2,1)}, bf16[512,1024]{1,0:T(8,128)(2,1)}, u32[]{:S(2)}, u32[]{:S(2)}) collective-permute-start(bf16[512,1024]{1,0:T(8,128)(2,1)} %values_ref.1), channel_id=1, source_target_pairs={{0,2},{1,3},{2,0},{3,1},{4,6},{5,7},{6,4},{7,5},{8,10},{9,11},{10,... | collective-permute-start | bytes 3145736 | tf_op jit(solution)/shard_map/ppermute | solution.py:472
  3.7 1.3 %copy-done.3 = bf16[512,1024]{1,0:T(8,128)(2,1)S(1)} copy-done((bf16[512,1024]{1,0:T(8,128)(2,1)S(1)}, bf16[512,1024]{1,0:T(8,128)(2,1)}, u32[]{:S(2)}) %copy-start.3) | copy-done | bytes 1048600
  7.0 4.9 %all-to-all-start = ((bf16[4,512,256]{2,1,0:T(8,128)(2,1)}), bf16[4,512,256]{2,1,0:T(8,128)(2,1)S(1)}, u32[]{:S(2)}, u32[]{:S(2)}) async-start(bf16[4,512,256]{2,1,0:T(8,128)(2,1)} %copy-done.2), calls=%async_computation | async-start | bytes 2097152 | tf_op jit(solution)/shard_map/all_to_all | solution.py:543
  11.9 1.1 constant_dynamic-slice_fusion
  14.4 1.2 %copy-done.4 = bf16[512,1024]{1,0:T(8,128)(2,1)S(1)} copy-done((bf16[512,1024]{1,0:T(8,128)(2,1)S(1)}, bf16[512,1024]{1,0:T(8,128)(2,1)}, u32[]{:S(2)}) %copy-start.4) | copy-done | bytes 1048600
  15.6 1.2 %copy-done.6 = bf16[512,1024]{1,0:T(8,128)(2,1)S(1)} copy-done((bf16[512,1024]{1,0:T(8,128)(2,1)S(1)}, bf16[512,1024]{1,0:T(8,128)(2,1)}, u32[]{:S(2)}) %copy-start.6) | copy-done | bytes 1048600
  17.6 10.2 %collective-permute-done.refs_0_ = bf16[512,1024]{1,0:T(8,128)(2,1)} collective-permute-done((bf16[512,1024]{1,0:T(8,128)(2,1)}, bf16[512,1024]{1,0:T(8,128)(2,1)}, u32[]{:S(2)}, u32[]{:S(2)}) %collective-permute-start) | collective-permute-done | bytes 1048608 | tf_op jit(solution)/shard_map/ppermute | solution.py:472
  27.8 1.7 %project.4.sum_ref = f32[512,192]{1,0:T(8,128)S(1)} custom-call(bf16[192,4096]{1,0:T(8,128)(2,1)S(1)} %bitcast.7, f32[512,192]{1,0:T(8,128)S(1)} %project.3.sum_ref, bf16[512,1024]{1,0:T(8,128)(2,1)} %collective-permute-done.refs_0_), custom_call_target="tpu_custom_call" | custom-call | flops 201326592 | bytes 1048576 | tf_op jit(solution)/shard_map/project/pallas_call | solution.py:243
  29.5 1.2 %collective-permute-done.3.refs_0_ = bf16[512,1024]{1,0:T(8,128)(2,1)S(1)} collective-permute-done((bf16[512,1024]{1,0:T(8,128)(2,1)}, bf16[512,1024]{1,0:T(8,128)(2,1)S(1)}, u32[]{:S(2)}, u32[]{:S(2)}) %collective-permute-start.3) | collective-permute-done | bytes 1048608 | tf_op jit(solution)/shard_map/ppermute | solution.py:472
  31.9 1.8 %collective-permute-start.4 = (bf16[80,512]{1,0:T(8,128)(2,1)S(1)}, bf16[80,512]{1,0:T(8,128)(2,1)S(1)}, u32[]{:S(2)}, u32[]{:S(2)}) collective-permute-start(bf16[80,512]{1,0:T(8,128)(2,1)S(1)} %get-tuple-element.55), channel_id=1, source_target_pairs={{0,4},{4,0},{8,12},{12,8},{1,5},{5,1},{9,13},{13,9},{2,6},{6,2},{1... | collective-permute-start | bytes 245768 | tf_op jit(solution)/shard_map/ppermute | solution.py:472
  33.7 2.6 %collective-permute-start.5 = (bf16[80,512]{1,0:T(8,128)(2,1)S(1)}, bf16[80,512]{1,0:T(8,128)(2,1)S(1)}, u32[]{:S(2)}, u32[]{:S(2)}) collective-permute-start(bf16[80,512]{1,0:T(8,128)(2,1)S(1)} %get-tuple-element.56), channel_id=1, source_target_pairs={{0,8},{4,12},{8,0},{12,4},{1,9},{5,13},{9,1},{13,5},{2,10},{6,14},... | collective-permute-start | bytes 245768 | tf_op jit(solution)/shard_map/ppermute | solution.py:472
  36.3 4.2 %collective-permute-done.4.refs_2_ = bf16[80,512]{1,0:T(8,128)(2,1)S(1)} collective-permute-done((bf16[80,512]{1,0:T(8,128)(2,1)S(1)}, bf16[80,512]{1,0:T(8,128)(2,1)S(1)}, u32[]{:S(2)}, u32[]{:S(2)}) %collective-permute-start.4) | collective-permute-done | bytes 81952 | tf_op jit(solution)/shard_map/ppermute | solution.py:472
  40.5 3.6 %collective-permute-done.5.refs_3_ = bf16[80,512]{1,0:T(8,128)(2,1)S(1)} collective-permute-done((bf16[80,512]{1,0:T(8,128)(2,1)S(1)}, bf16[80,512]{1,0:T(8,128)(2,1)S(1)}, u32[]{:S(2)}, u32[]{:S(2)}) %collective-permute-start.5) | collective-permute-done | bytes 81952 | tf_op jit(solution)/shard_map/ppermute | solution.py:472
  44.8 5.3 %conv.1 = (bf16[48,2432]{1,0:T(8,128)(2,1)}, bf16[48,2432]{1,0:T(8,128)(2,1)}, bf16[48,2432]{1,0:T(8,128)(2,1)}, bf16[48,2432]{1,0:T(8,128)(2,1)}) custom-call(f32[1,16]{1,0:T(1,128)} %dynamic-slice_bitcast_fusion.refs_0_, bf16[80,512]{1,0:T(8,128)(2,1)} %copy-done.9, bf16[80,512]{1,0:T(8,128)(2,1)} %copy-done.12, bf16[80,512]{1,0:T(8,128)(2,1)} %copy-done.13, ...), custom_call_target="tpu_custom_call" | custom-call | flops 962592768 | bytes 4194304 | tf_op jit(solution)/shard_map/conv/pallas_call | solution.py:183
  50.1 2.4 %collective-permute-start.9 = (bf16[48,2432]{1,0:T(8,128)(2,1)}, bf16[48,2432]{1,0:T(8,128)(2,1)S(1)}, u32[]{:S(2)}, u32[]{:S(2)}) collective-permute-start(bf16[48,2432]{1,0:T(8,128)(2,1)} %get-tuple-element.67), channel_id=1, source_target_pairs={{0,8},{4,12},{8,0},{12,4},{1,9},{5,13},{9,1},{13,5},{2,10},{6,14},... | collective-permute-start | bytes 700424 | tf_op jit(solution)/shard_map/ppermute | solution.py:472
  53.2 1.6 %collective-permute-start.10 = (bf16[48,2432]{1,0:T(8,128)(2,1)}, bf16[48,2432]{1,0:T(8,128)(2,1)S(1)}, u32[]{:S(2)}, u32[]{:S(2)}) collective-permute-start(bf16[48,2432]{1,0:T(8,128)(2,1)} %get-tuple-element.68), channel_id=1, source_target_pairs={{4,8},{8,4},{0,0},{12,12},{5,9},{9,5},{1,1},{13,13},{6,10},{10,6},... | collective-permute-start | bytes 700424 | tf_op jit(solution)/shard_map/ppermute | solution.py:563
  54.8 9.3 %collective-permute-done.9.refs_2_ = bf16[48,2432]{1,0:T(8,128)(2,1)S(1)} collective-permute-done((bf16[48,2432]{1,0:T(8,128)(2,1)}, bf16[48,2432]{1,0:T(8,128)(2,1)S(1)}, u32[]{:S(2)}, u32[]{:S(2)}) %collective-permute-start.9) | collective-permute-done | bytes 233504 | tf_op jit(solution)/shard_map/ppermute | solution.py:472
  65.2 5.1 %collective-permute-done.11.refs_4_ = bf16[48,2432]{1,0:T(8,128)(2,1)S(1)} collective-permute-done((bf16[48,2432]{1,0:T(8,128)(2,1)S(1)}, bf16[48,2432]{1,0:T(8,128)(2,1)S(1)}, u32[]{:S(2)}, u32[]{:S(2)}) %collective-permute-start.11) | collective-permute-done | bytes 233504 | tf_op jit(solution)/shard_map/ppermute | solution.py:472
  70.2 1.4 %products.2 = (bf16[192,2048]{1,0:T(8,128)(2,1)S(1)}, bf16[192,768]{1,0:T(8,128)(2,1)S(1)}, bf16[192,512]{1,0:T(8,128)(2,1)S(1)}, f32[64,512]{1,0:T(8,128)}) custom-call(bf16[48,2432]{1,0:T(8,128)(2,1)S(1)} %keep.1.refs_0_, bf16[48,2432]{1,0:T(8,128)(2,1)S(1)} %collective-permute-done.8.refs_1_, bf16[48,2432]{1,0:T(8,128)(2,1)S(1)} %collective-permute-done.9.refs_2_, ...), custom_call_target="tpu_custom_call" | custom-call | flops 603979776 | bytes 4194304 | tf_op jit(solution)/shard_map/products/pallas_call | solution.py:300
  71.6 1.1 %collective-permute-start.14 = (bf16[192,512]{1,0:T(8,128)(2,1)S(1)}, bf16[192,512]{1,0:T(8,128)(2,1)S(1)}, u32[]{:S(2)}, u32[]{:S(2)}) collective-permute-start(bf16[192,512]{1,0:T(8,128)(2,1)S(1)} %get-tuple-element.80.refs_0_), channel_id=1, source_target_pairs={{0,2},{1,3},{2,0},{3,1},{4,6},{5,7},{6,4},{7,5},{8,10},{9,11},{10,... | collective-permute-start | bytes 589832 | tf_op jit(solution)/shard_map/ppermute | solution.py:472
  73.5 3.8 %collective-permute-start.22 = (bf16[96,1024]{1,0:T(8,128)(2,1)S(1)}, bf16[96,1024]{1,0:T(8,128)(2,1)S(1)}, u32[]{:S(2)}, u32[]{:S(2)}) collective-permute-start(bf16[96,1024]{1,0:T(8,128)(2,1)S(1)} %get-tuple-element.92.refs_3_), channel_id=1, source_target_pairs={{0,12},{4,0},{8,4},{12,8},{1,13},{5,1},{9,5},{13,9},{2,14},{6,2},{... | collective-permute-start | bytes 589832 | tf_op jit(solution)/shard_map/ppermute | solution.py:491
  77.3 1.6 %collective-permute-done.14.refs_2_ = bf16[192,512]{1,0:T(8,128)(2,1)S(1)} collective-permute-done((bf16[192,512]{1,0:T(8,128)(2,1)S(1)}, bf16[192,512]{1,0:T(8,128)(2,1)S(1)}, u32[]{:S(2)}, u32[]{:S(2)}) %collective-permute-start.14) | collective-permute-done | bytes 196640 | tf_op jit(solution)/shard_map/ppermute | solution.py:472
  78.9 1.1 %collective-permute-start.17 = (bf16[192,1024]{1,0:T(8,128)(2,1)S(1)}, bf16[192,1024]{1,0:T(8,128)(2,1)S(1)}, u32[]{:S(2)}, u32[]{:S(2)}) collective-permute-start(bf16[192,1024]{1,0:T(8,128)(2,1)S(1)} %copy-done.11), channel_id=1, source_target_pairs={{0,2},{1,3},{2,0},{3,1},{4,6},{5,7},{6,4},{7,5},{8,10},{9,11},{10,... | collective-permute-start | bytes 1179656 | tf_op jit(solution)/shard_map/ppermute | solution.py:472
  80.1 3.0 %collective-permute-done.19.refs_1_ = bf16[96,1024]{1,0:T(8,128)(2,1)S(1)} collective-permute-done((bf16[96,1024]{1,0:T(8,128)(2,1)S(1)}, bf16[96,1024]{1,0:T(8,128)(2,1)S(1)}, u32[]{:S(2)}, u32[]{:S(2)}) %collective-permute-start.19) | collective-permute-done | bytes 196640 | tf_op jit(solution)/shard_map/ppermute | solution.py:491
  83.1 1.8 %collective-permute-done.22.refs_4_ = bf16[96,1024]{1,0:T(8,128)(2,1)S(1)} collective-permute-done((bf16[96,1024]{1,0:T(8,128)(2,1)S(1)}, bf16[96,1024]{1,0:T(8,128)(2,1)S(1)}, u32[]{:S(2)}, u32[]{:S(2)}) %collective-permute-start.22) | collective-permute-done | bytes 196640 | tf_op jit(solution)/shard_map/ppermute | solution.py:491
  84.9 2.3 %collective-permute-start.23 = (bf16[96,1024]{1,0:T(8,128)(2,1)S(1)}, bf16[96,1024]{1,0:T(8,128)(2,1)S(1)}, u32[]{:S(2)}, u32[]{:S(2)}) collective-permute-start(bf16[96,1024]{1,0:T(8,128)(2,1)S(1)} %collective-permute-done.22.refs_4_), channel_id=1, source_target_pairs={{0,12},{4,0},{8,4},{12,8},{1,13},{5,1},{9,5},{13,9},{2,14},{6,2},{... | collective-permute-start | bytes 589832 | tf_op jit(solution)/shard_map/ppermute | solution.py:491
  87.2 5.5 %collective-permute-done.20.refs_2_ = bf16[96,1024]{1,0:T(8,128)(2,1)S(1)} collective-permute-done((bf16[96,1024]{1,0:T(8,128)(2,1)S(1)}, bf16[96,1024]{1,0:T(8,128)(2,1)S(1)}, u32[]{:S(2)}, u32[]{:S(2)}) %collective-permute-start.20) | collective-permute-done | bytes 196640 | tf_op jit(solution)/shard_map/ppermute | solution.py:491
  92.7 3.9 %collective-permute-done.23.refs_5_ = bf16[96,1024]{1,0:T(8,128)(2,1)S(1)} collective-permute-done((bf16[96,1024]{1,0:T(8,128)(2,1)S(1)}, bf16[96,1024]{1,0:T(8,128)(2,1)S(1)}, u32[]{:S(2)}, u32[]{:S(2)}) %collective-permute-start.23) | collective-permute-done | bytes 196640 | tf_op jit(solution)/shard_map/ppermute | solution.py:491
  96.8 2.2 %place.2.refs_2_ = f32[192,4096]{1,0:T(8,128)} custom-call(bf16[96,1024]{1,0:T(8,128)(2,1)S(1)} %get-tuple-element.91.refs_0_, bf16[96,1024]{1,0:T(8,128)(2,1)S(1)} %collective-permute-done.19.refs_1_, bf16[96,1024]{1,0:T(8,128)(2,1)S(1)} %collective-permute-done.20.refs_2_, bf16[96,1024]{1,0:T(8,128)(2,1)S(1)} %get-tuple-element.92.refs_3_, ...), custom_call_target="tpu_custom_call" | custom-call | bytes 6291456 | tf_op jit(solution)/shard_map/place/pallas_call | solution.py:442
  99.0 2.3 %inputs.1 = bf16[512,1024]{1,0:T(8,128)(2,1)} custom-call(bf16[192,512]{1,0:T(8,128)(2,1)S(1)} %get-tuple-element.80.refs_0_, bf16[192,512]{1,0:T(8,128)(2,1)S(1)} %collective-permute-done.15.refs_1_, bf16[192,512]{1,0:T(8,128)(2,1)S(1)} %collective-permute-done.14.refs_2_, bf16[192,512]{1,0:T(8,128)(2,1)S(1)} %collective-permute-done.16.refs_3_, ...), custom_call_target="tpu_custom_call" | custom-call | flops 805306368 | bytes 4194304 | tf_op jit(solution)/shard_map/inputs/pallas_call | solution.py:379
  101.9 2.9 %collective-permute-done.24.refs_1_ = bf16[96,1024]{1,0:T(8,128)(2,1)S(1)} collective-permute-done((bf16[96,1024]{1,0:T(8,128)(2,1)S(1)}, bf16[96,1024]{1,0:T(8,128)(2,1)S(1)}, u32[]{:S(2)}, u32[]{:S(2)}) %collective-permute-start.24) | collective-permute-done | bytes 196640 | tf_op jit(solution)/shard_map/ppermute | solution.py:491
  104.8 1.1 %place.3 = f32[192,4096]{1,0:T(8,128)} custom-call(bf16[96,1024]{1,0:T(8,128)(2,1)S(1)} %collective-permute-done.21.refs_0_, bf16[96,1024]{1,0:T(8,128)(2,1)S(1)} %collective-permute-done.24.refs_1_, f32[192,4096]{1,0:T(8,128)} %place.2.refs_2_), custom_call_target="tpu_custom_call", output_to_operand_aliasing={{}: (2, {})} | custom-call | bytes 1048576 | tf_op jit(solution)/shard_map/place/pallas_call | solution.py:452
  (64 shorter events, 9.8 us)
Async XLA Ops:
  0.6 13.2 %copy-start = (f32[64]{0:T(128)S(1)}, f32[64]{0:T(128)}, u32[]{:S(2)}) copy-start(f32[64]{0:T(128)} %param.13) | copy-start | bytes 772
  0.6 11.2 %copy-start.1 = (bf16[3,64,4096]{2,1,0:T(8,128)(2,1)S(1)}, bf16[3,64,4096]{2,1,0:T(8,128)(2,1)}, u32[]{:S(2)}) copy-start(bf16[3,64,4096]{2,1,0:T(8,128)(2,1)} %param.11) | copy-start | bytes 4718596
  0.7 5.4 %collective-permute-start.1 = (bf16[512,1024]{1,0:T(8,128)(2,1)}, bf16[512,1024]{1,0:T(8,128)(2,1)S(1)}, u32[]{:S(2)}, u32[]{:S(2)}) collective-permute-start(bf16[512,1024]{1,0:T(8,128)(2,1)} %values_ref.1), channel_id=1, source_target_pairs={{0,1},{1,0},{2,3},{3,2},{4,5},{5,4},{6,7},{7,6},{8,9},{9,8},{10,11... | collective-permute-start | bytes 3145736 | tf_op jit(solution)/shard_map/ppermute | solution.py:472
  1.2 26.6 %collective-permute-start = (bf16[512,1024]{1,0:T(8,128)(2,1)}, bf16[512,1024]{1,0:T(8,128)(2,1)}, u32[]{:S(2)}, u32[]{:S(2)}) collective-permute-start(bf16[512,1024]{1,0:T(8,128)(2,1)} %values_ref.1), channel_id=1, source_target_pairs={{0,2},{1,3},{2,0},{3,1},{4,6},{5,7},{6,4},{7,5},{8,10},{9,11},{10,... | collective-permute-start | bytes 3145736 | tf_op jit(solution)/shard_map/ppermute | solution.py:472
  7.0 37.1 %all-to-all-start = ((bf16[4,512,256]{2,1,0:T(8,128)(2,1)}), bf16[4,512,256]{2,1,0:T(8,128)(2,1)S(1)}, u32[]{:S(2)}, u32[]{:S(2)}) async-start(bf16[4,512,256]{2,1,0:T(8,128)(2,1)} %copy-done.2), calls=%async_computation | async-start | bytes 2097152 | tf_op jit(solution)/shard_map/all_to_all | solution.py:543
  13.0 4.7 %collective-permute-start.2 = (bf16[192,1024]{1,0:T(8,128)(2,1)}, bf16[192,1024]{1,0:T(8,128)(2,1)S(1)}, u32[]{:S(2)}, u32[]{:S(2)}) collective-permute-start(bf16[192,1024]{1,0:T(8,128)(2,1)} %get-tuple-element.99), channel_id=1, source_target_pairs={{0,1},{1,0},{2,3},{3,2},{4,5},{5,4},{6,7},{7,6},{8,9},{9,8},{10,11... | collective-permute-start | bytes 1179656 | tf_op jit(solution)/shard_map/ppermute | solution.py:472
  16.9 13.8 %copy-start.8 = (f32[64,512]{1,0:T(8,128)S(1)}, f32[64,512]{1,0:T(8,128)}, u32[]{:S(2)}) copy-start(f32[64,512]{1,0:T(8,128)} %filter_ref) | copy-start | bytes 393220
  27.8 2.9 %collective-permute-start.3 = (bf16[512,1024]{1,0:T(8,128)(2,1)}, bf16[512,1024]{1,0:T(8,128)(2,1)S(1)}, u32[]{:S(2)}, u32[]{:S(2)}) collective-permute-start(bf16[512,1024]{1,0:T(8,128)(2,1)} %collective-permute-done.refs_0_), channel_id=1, source_target_pairs={{0,1},{1,0},{2,3},{3,2},{4,5},{5,4},{6,7},{7,6},{8,9},{9,8},{10,11... | collective-permute-start | bytes 3145736 | tf_op jit(solution)/shard_map/ppermute | solution.py:472
  31.9 8.6 %collective-permute-start.4 = (bf16[80,512]{1,0:T(8,128)(2,1)S(1)}, bf16[80,512]{1,0:T(8,128)(2,1)S(1)}, u32[]{:S(2)}, u32[]{:S(2)}) collective-permute-start(bf16[80,512]{1,0:T(8,128)(2,1)S(1)} %get-tuple-element.55), channel_id=1, source_target_pairs={{0,4},{4,0},{8,12},{12,8},{1,5},{5,1},{9,13},{13,9},{2,6},{6,2},{1... | collective-permute-start | bytes 245768 | tf_op jit(solution)/shard_map/ppermute | solution.py:472
  33.7 10.4 %collective-permute-start.5 = (bf16[80,512]{1,0:T(8,128)(2,1)S(1)}, bf16[80,512]{1,0:T(8,128)(2,1)S(1)}, u32[]{:S(2)}, u32[]{:S(2)}) collective-permute-start(bf16[80,512]{1,0:T(8,128)(2,1)S(1)} %get-tuple-element.56), channel_id=1, source_target_pairs={{0,8},{4,12},{8,0},{12,4},{1,9},{5,13},{9,1},{13,5},{2,10},{6,14},... | collective-permute-start | bytes 245768 | tf_op jit(solution)/shard_map/ppermute | solution.py:472
  36.3 7.8 %collective-permute-start.6 = (bf16[80,512]{1,0:T(8,128)(2,1)S(1)}, bf16[80,512]{1,0:T(8,128)(2,1)S(1)}, u32[]{:S(2)}, u32[]{:S(2)}) collective-permute-start(bf16[80,512]{1,0:T(8,128)(2,1)S(1)} %get-tuple-element.57), channel_id=1, source_target_pairs={{0,12},{4,8},{8,4},{12,0},{1,13},{5,9},{9,5},{13,1},{2,14},{6,10},... | collective-permute-start | bytes 245768 | tf_op jit(solution)/shard_map/ppermute | solution.py:472
  40.5 4.3 %copy-start.12 = (bf16[80,512]{1,0:T(8,128)(2,1)}, bf16[80,512]{1,0:T(8,128)(2,1)S(1)}, u32[]{:S(2)}) copy-start(bf16[80,512]{1,0:T(8,128)(2,1)S(1)} %collective-permute-done.4.refs_2_) | copy-start | bytes 245764
  44.1 26.1 %collective-permute-start.7 = (bf16[2048,256]{1,0:T(8,128)(2,1)S(1)}, bf16[2048,256]{1,0:T(8,128)(2,1)S(1)}, u32[]{:S(2)}, u32[]{:S(2)}) collective-permute-start(bf16[2048,256]{1,0:T(8,128)(2,1)S(1)} %bitcast.9), channel_id=1, source_target_pairs={{0,2},{1,3},{2,0},{3,1},{4,6},{5,7},{6,4},{7,5},{8,10},{9,11},{10,... | collective-permute-start | bytes 3145736 | tf_op jit(solution)/shard_map/ppermute | solution.py:472
  50.1 14.0 %collective-permute-start.9 = (bf16[48,2432]{1,0:T(8,128)(2,1)}, bf16[48,2432]{1,0:T(8,128)(2,1)S(1)}, u32[]{:S(2)}, u32[]{:S(2)}) collective-permute-start(bf16[48,2432]{1,0:T(8,128)(2,1)} %get-tuple-element.67), channel_id=1, source_target_pairs={{0,8},{4,12},{8,0},{12,4},{1,9},{5,13},{9,1},{13,5},{2,10},{6,14},... | collective-permute-start | bytes 700424 | tf_op jit(solution)/shard_map/ppermute | solution.py:472
  52.6 12.6 %collective-permute-start.8 = (bf16[48,2432]{1,0:T(8,128)(2,1)}, bf16[48,2432]{1,0:T(8,128)(2,1)S(1)}, u32[]{:S(2)}, u32[]{:S(2)}) collective-permute-start(bf16[48,2432]{1,0:T(8,128)(2,1)} %get-tuple-element.66), channel_id=1, source_target_pairs={{0,4},{4,0},{8,12},{12,8},{1,5},{5,1},{9,13},{13,9},{2,6},{6,2},{1... | collective-permute-start | bytes 700424 | tf_op jit(solution)/shard_map/ppermute | solution.py:472
  53.2 11.9 %collective-permute-start.10 = (bf16[48,2432]{1,0:T(8,128)(2,1)}, bf16[48,2432]{1,0:T(8,128)(2,1)S(1)}, u32[]{:S(2)}, u32[]{:S(2)}) collective-permute-start(bf16[48,2432]{1,0:T(8,128)(2,1)} %get-tuple-element.68), channel_id=1, source_target_pairs={{4,8},{8,4},{0,0},{12,12},{5,9},{9,5},{1,1},{13,13},{6,10},{10,6},... | collective-permute-start | bytes 700424 | tf_op jit(solution)/shard_map/ppermute | solution.py:563
  64.2 6.1 %collective-permute-start.11 = (bf16[48,2432]{1,0:T(8,128)(2,1)S(1)}, bf16[48,2432]{1,0:T(8,128)(2,1)S(1)}, u32[]{:S(2)}, u32[]{:S(2)}) collective-permute-start(bf16[48,2432]{1,0:T(8,128)(2,1)S(1)} %collective-permute-done.9.refs_2_), channel_id=1, source_target_pairs={{0,4},{4,0},{8,12},{12,8},{1,5},{5,1},{9,13},{13,9},{2,6},{6,2},{1... | collective-permute-start | bytes 700424 | tf_op jit(solution)/shard_map/ppermute | solution.py:472
  64.2 6.1 %collective-permute-start.12 = (bf16[2048,256]{1,0:T(8,128)(2,1)S(1)}, bf16[2048,256]{1,0:T(8,128)(2,1)S(1)}, u32[]{:S(2)}, u32[]{:S(2)}) collective-permute-start(bf16[2048,256]{1,0:T(8,128)(2,1)S(1)} %bitcast.10), channel_id=1, source_target_pairs={{0,1},{1,0},{2,3},{3,2},{4,5},{5,4},{6,7},{7,6},{8,9},{9,8},{10,11... | collective-permute-start | bytes 3145736 | tf_op jit(solution)/shard_map/ppermute | solution.py:472
  65.1 13.8 %copy-start.11 = (bf16[192,1024]{1,0:T(8,128)(2,1)S(1)}, bf16[192,1024]{1,0:T(8,128)(2,1)}, u32[]{:S(2)}) copy-start(bf16[192,1024]{1,0:T(8,128)(2,1)} %get-tuple-element.89) | copy-start | bytes 1179652
  65.1 14.9 %copy-start.10 = (bf16[192,1024]{1,0:T(8,128)(2,1)S(1)}, bf16[192,1024]{1,0:T(8,128)(2,1)}, u32[]{:S(2)}) copy-start(bf16[192,1024]{1,0:T(8,128)(2,1)} %get-tuple-element.90) | copy-start | bytes 1179652
  70.2 2.7 %collective-permute-start.13 = (bf16[2048,256]{1,0:T(8,128)(2,1)S(1)}, bf16[2048,256]{1,0:T(8,128)(2,1)S(1)}, u32[]{:S(2)}, u32[]{:S(2)}) collective-permute-start(bf16[2048,256]{1,0:T(8,128)(2,1)S(1)} %collective-permute-done.7.refs_7_), channel_id=1, source_target_pairs={{0,1},{1,0},{2,3},{3,2},{4,5},{5,4},{6,7},{7,6},{8,9},{9,8},{10,11... | collective-permute-start | bytes 3145736 | tf_op jit(solution)/shard_map/ppermute | solution.py:472
  71.6 7.3 %collective-permute-start.14 = (bf16[192,512]{1,0:T(8,128)(2,1)S(1)}, bf16[192,512]{1,0:T(8,128)(2,1)S(1)}, u32[]{:S(2)}, u32[]{:S(2)}) collective-permute-start(bf16[192,512]{1,0:T(8,128)(2,1)S(1)} %get-tuple-element.80.refs_0_), channel_id=1, source_target_pairs={{0,2},{1,3},{2,0},{3,1},{4,6},{5,7},{6,4},{7,5},{8,10},{9,11},{10,... | collective-permute-start | bytes 589832 | tf_op jit(solution)/shard_map/ppermute | solution.py:472
  73.3 5.7 %collective-permute-start.15 = (bf16[192,512]{1,0:T(8,128)(2,1)S(1)}, bf16[192,512]{1,0:T(8,128)(2,1)S(1)}, u32[]{:S(2)}, u32[]{:S(2)}) collective-permute-start(bf16[192,512]{1,0:T(8,128)(2,1)S(1)} %get-tuple-element.80.refs_0_), channel_id=1, source_target_pairs={{0,1},{1,0},{2,3},{3,2},{4,5},{5,4},{6,7},{7,6},{8,9},{9,8},{10,11... | collective-permute-start | bytes 589832 | tf_op jit(solution)/shard_map/ppermute | solution.py:472
  73.5 9.6 %collective-permute-start.19 = (bf16[96,1024]{1,0:T(8,128)(2,1)S(1)}, bf16[96,1024]{1,0:T(8,128)(2,1)S(1)}, u32[]{:S(2)}, u32[]{:S(2)}) collective-permute-start(bf16[96,1024]{1,0:T(8,128)(2,1)S(1)} %get-tuple-element.91.refs_0_), channel_id=1, source_target_pairs={{0,4},{4,8},{8,12},{12,0},{1,5},{5,9},{9,13},{13,1},{2,6},{6,10},{... | collective-permute-start | bytes 589832 | tf_op jit(solution)/shard_map/ppermute | solution.py:491
  73.5 11.4 %collective-permute-start.22 = (bf16[96,1024]{1,0:T(8,128)(2,1)S(1)}, bf16[96,1024]{1,0:T(8,128)(2,1)S(1)}, u32[]{:S(2)}, u32[]{:S(2)}) collective-permute-start(bf16[96,1024]{1,0:T(8,128)(2,1)S(1)} %get-tuple-element.92.refs_3_), channel_id=1, source_target_pairs={{0,12},{4,0},{8,4},{12,8},{1,13},{5,1},{9,5},{13,9},{2,14},{6,2},{... | collective-permute-start | bytes 589832 | tf_op jit(solution)/shard_map/ppermute | solution.py:491
  78.9 20.1 %collective-permute-start.17 = (bf16[192,1024]{1,0:T(8,128)(2,1)S(1)}, bf16[192,1024]{1,0:T(8,128)(2,1)S(1)}, u32[]{:S(2)}, u32[]{:S(2)}) collective-permute-start(bf16[192,1024]{1,0:T(8,128)(2,1)S(1)} %copy-done.11), channel_id=1, source_target_pairs={{0,2},{1,3},{2,0},{3,1},{4,6},{5,7},{6,4},{7,5},{8,10},{9,11},{10,... | collective-permute-start | bytes 1179656 | tf_op jit(solution)/shard_map/ppermute | solution.py:472
  80.1 18.9 %collective-permute-start.18 = (bf16[192,1024]{1,0:T(8,128)(2,1)S(1)}, bf16[192,1024]{1,0:T(8,128)(2,1)S(1)}, u32[]{:S(2)}, u32[]{:S(2)}) collective-permute-start(bf16[192,1024]{1,0:T(8,128)(2,1)S(1)} %copy-done.10), channel_id=1, source_target_pairs={{0,3},{1,2},{2,1},{3,0},{4,7},{5,6},{6,5},{7,4},{8,11},{9,10},{10,... | collective-permute-start | bytes 1179656 | tf_op jit(solution)/shard_map/ppermute | solution.py:472
  83.1 9.6 %collective-permute-start.20 = (bf16[96,1024]{1,0:T(8,128)(2,1)S(1)}, bf16[96,1024]{1,0:T(8,128)(2,1)S(1)}, u32[]{:S(2)}, u32[]{:S(2)}) collective-permute-start(bf16[96,1024]{1,0:T(8,128)(2,1)S(1)} %collective-permute-done.19.refs_1_), channel_id=1, source_target_pairs={{0,4},{4,8},{8,12},{12,0},{1,5},{5,9},{9,13},{13,1},{2,6},{6,10},{... | collective-permute-start | bytes 589832 | tf_op jit(solution)/shard_map/ppermute | solution.py:491
  84.9 11.7 %collective-permute-start.23 = (bf16[96,1024]{1,0:T(8,128)(2,1)S(1)}, bf16[96,1024]{1,0:T(8,128)(2,1)S(1)}, u32[]{:S(2)}, u32[]{:S(2)}) collective-permute-start(bf16[96,1024]{1,0:T(8,128)(2,1)S(1)} %collective-permute-done.22.refs_4_), channel_id=1, source_target_pairs={{0,12},{4,0},{8,4},{12,8},{1,13},{5,1},{9,5},{13,9},{2,14},{6,2},{... | collective-permute-start | bytes 589832 | tf_op jit(solution)/shard_map/ppermute | solution.py:491
  87.2 11.8 %collective-permute-start.16 = (bf16[192,512]{1,0:T(8,128)(2,1)S(1)}, bf16[192,512]{1,0:T(8,128)(2,1)S(1)}, u32[]{:S(2)}, u32[]{:S(2)}) collective-permute-start(bf16[192,512]{1,0:T(8,128)(2,1)S(1)} %collective-permute-done.14.refs_2_), channel_id=1, source_target_pairs={{0,1},{1,0},{2,3},{3,2},{4,5},{5,4},{6,7},{7,6},{8,9},{9,8},{10,11... | collective-permute-start | bytes 589832 | tf_op jit(solution)/shard_map/ppermute | solution.py:472
  92.7 9.2 %collective-permute-start.21 = (bf16[96,1024]{1,0:T(8,128)(2,1)S(1)}, bf16[96,1024]{1,0:T(8,128)(2,1)S(1)}, u32[]{:S(2)}, u32[]{:S(2)}) collective-permute-start(bf16[96,1024]{1,0:T(8,128)(2,1)S(1)} %collective-permute-done.20.refs_2_), channel_id=1, source_target_pairs={{0,4},{4,8},{8,12},{12,0},{1,5},{5,9},{9,13},{13,1},{2,6},{6,10},{... | collective-permute-start | bytes 589832 | tf_op jit(solution)/shard_map/ppermute | solution.py:491
  96.6 8.3 %collective-permute-start.24 = (bf16[96,1024]{1,0:T(8,128)(2,1)S(1)}, bf16[96,1024]{1,0:T(8,128)(2,1)S(1)}, u32[]{:S(2)}, u32[]{:S(2)}) collective-permute-start(bf16[96,1024]{1,0:T(8,128)(2,1)S(1)} %collective-permute-done.23.refs_5_), channel_id=1, source_target_pairs={{0,12},{4,0},{8,4},{12,8},{1,13},{5,1},{9,5},{13,9},{2,14},{6,2},{... | collective-permute-start | bytes 589832 | tf_op jit(solution)/shard_map/ppermute | solution.py:491
  (9 other events, 8.5 us)
